TPU v7x, 256 devices: a whole 4x4x8 slice. The times are simulated.
256 devices in a mesh: dp: 64 (over z, x, core), mp: 4 (over y).
Axes of the slice: x: 4, y: 4, z: 8, core: 2. Of those that a mesh axis runs over, the one named last changes fastest.
Arguments:
- imp_x: bfloat16 [8192, 512], P('dp'), may hold values from -6 to 6
- imp_hist: int32 [8192, 1], P('dp'), may hold values from 0 to 63; in each aligned block of 128 rows (0 to 127, 128 to 255, ...) at most 8 rows name the same one
- imp_len: int32 [8192], P('dp'), may hold values from 512 to 2048, as said below
- owner_map: int32 [64], replicated, may hold values from 0 to 63, each once
- hist_x: bfloat16 [64, 2048, 512], P('dp'), may hold values from -6 to 6
- w_in: bfloat16 [4, 512, 512], P(None, None, 'mp'), may hold values from -0.25 to 0.25
- w_out: bfloat16 [512, 512], P('mp'), may hold values from -0.25 to 0.25
- grad_y: bfloat16 [8192, 512], P('dp'), may hold values from -6 to 6
Outputs:
- grad_x: bfloat16 [8192, 512], P(('dp', 'mp'))
- grad_kv: bfloat16 [64, 2048, 2, 512], P('dp', None, None, 'mp')
- grad_w_in: float32 [4, 512, 512], P(None, None, 'mp')
- grad_w_out: float32 [512, 512], P('mp')
Inputs may be any that keep to these rules, and one draw needn't show every extreme that they name: `imp_hist`: row i names the history of impression i. Among the 128 impressions of one log shard no history is named more than 8 times. `imp_len`: every device's block of impressions holds one that sees all 2048 events. A permutation: history h is held by device owner_map[h] of dp, as row owner_map[h] of hist_x.
All inputs are finite; a program needn't handle non-finite values.
Results may differ from a plain program's by a relative error of at most 0.01.
Values may be sent and summed in bfloat16 or wider, within the bound.
No kernel may reach another device: no remote copies, remote signals or barrier semaphores. Data moves between devices by JAX's collectives and lax.ppermute only.
A program may use at most 64 MiB of HBM per device.

v0:
```python
import jax
import jax.numpy as jnp
from jax import lax
from jax.sharding import PartitionSpec as P

DH = 64


EPSILON = 1e-05


def silu_slope(pre_act):
    sigmoid_v = jax.nn.sigmoid(pre_act)
    return sigmoid_v * (1.0 + pre_act * (1.0 - sigmoid_v))


def owner_pass(query_rows, gate_rows, cotangent, length_rows, events, w_key, w_value):
    row_count = query_rows.shape[0]
    col_width = query_rows.shape[1]
    head_count = col_width // DH
    event_count = events.shape[0]
    block_len = min(1024, event_count)
    block_count = event_count // block_len
    factor = DH ** (-0.5)
    key_pre = jnp.dot(events, w_key, preferred_element_type=jnp.float32)
    key_rows = jax.nn.silu(key_pre).astype(jnp.bfloat16)
    value_rows = jnp.dot(events, w_value, preferred_element_type=jnp.float32).astype(jnp.bfloat16)
    key_blocks = key_rows.reshape(block_count, block_len, head_count, DH)
    value_blocks = value_rows.reshape(block_count, block_len, head_count, DH)
    query_heads = query_rows.reshape(row_count, head_count, DH)
    positions = jnp.arange(block_count, dtype=jnp.int32)

    def scores_of(position, key_block):
        scores = (
            jnp.einsum("rhd,khd->hrk", query_heads, key_block, preferred_element_type=jnp.float32)
            * factor
        )
        event_ids = position * block_len + jnp.arange(block_len, dtype=jnp.int32)
        visible = event_ids[None, :] < length_rows[:, None]
        return (scores, visible[None])

    def forward(running, pieces):
        position, key_block, value_block = pieces
        scores, visible = scores_of(position, key_block)
        weights = jnp.where(visible, jax.nn.silu(scores), 0.0).astype(jnp.bfloat16)
        running = running + jnp.einsum(
            "hrk,khd->rhd", weights, value_block, preferred_element_type=jnp.float32
        )
        return (running, None)

    attended, unused = lax.scan(
        forward,
        jnp.zeros((row_count, head_count, DH), jnp.float32),
        (positions, key_blocks, value_blocks),
    )
    inverse = lax.rsqrt(jnp.mean(attended * attended, axis=-1, keepdims=True) + EPSILON)
    normed = attended * inverse
    gate_heads = gate_rows.reshape(row_count, head_count, DH).astype(jnp.float32)
    cot_heads = cotangent.reshape(row_count, head_count, DH).astype(jnp.float32)
    gated = (normed * gate_heads).astype(jnp.bfloat16)
    d_normed = cot_heads * gate_heads
    d_gate = (cot_heads * normed).astype(jnp.bfloat16)
    d_att = (
        inverse * (d_normed - normed * jnp.mean(d_normed * normed, axis=-1, keepdims=True))
    ).astype(jnp.bfloat16)

    def backward(partial_value, pieces):
        position, key_block, value_block = pieces
        scores, visible = scores_of(position, key_block)
        weights = jnp.where(visible, jax.nn.silu(scores), 0.0).astype(jnp.bfloat16)
        d_weights = jnp.einsum(
            "rhd,khd->hrk", d_att, value_block, preferred_element_type=jnp.float32
        )
        d_scores = jnp.where(visible, d_weights * silu_slope(scores) * factor, 0.0).astype(
            jnp.bfloat16
        )
        partial_value = partial_value + jnp.einsum(
            "hrk,khd->rhd", d_scores, key_block, preferred_element_type=jnp.float32
        )
        d_key = jnp.einsum(
            "hrk,rhd->khd", d_scores, query_heads, preferred_element_type=jnp.float32
        )
        d_value = jnp.einsum("hrk,rhd->khd", weights, d_att, preferred_element_type=jnp.float32)
        return (partial_value, (d_key, d_value))

    d_query, (d_keys, d_values) = lax.scan(
        backward,
        jnp.zeros((row_count, head_count, DH), jnp.float32),
        (positions, key_blocks, value_blocks),
    )
    d_keys = d_keys.reshape(event_count, col_width)
    d_values = d_values.reshape(event_count, col_width)
    grad_key = d_keys.astype(jnp.bfloat16)
    grad_value = d_values.astype(jnp.bfloat16)
    key_term = (d_keys * silu_slope(key_pre)).astype(jnp.bfloat16)
    grad_wk = jnp.dot(events.T, key_term, preferred_element_type=jnp.float32)
    grad_wv = jnp.dot(events.T, grad_value, preferred_element_type=jnp.float32)
    return (
        d_query.reshape(row_count, col_width).astype(jnp.bfloat16),
        d_gate.reshape(row_count, col_width),
        gated.reshape(row_count, col_width),
        grad_key,
        grad_value,
        grad_wk,
        grad_wv,
    )


def on_device(imp_x, imp_hist, imp_len, owner_map, hist_x, w_in, w_out, grad_y):
    owners = lax.axis_size("dp")
    local_rows = imp_x.shape[0]
    capacity = max(8, 2 * local_rows // owners)
    slots_all = owners * capacity
    histories = imp_hist[:, 0]
    owner_ids = jnp.arange(owners, dtype=jnp.int32)
    target_dev = jnp.sum(
        jnp.where(histories[:, None] == owner_ids[None, :], owner_map[None, :], 0), axis=1
    )
    hit_table = (target_dev[:, None] == owner_ids[None, :]).astype(jnp.int32)
    before = jnp.cumsum(hit_table, axis=0) - hit_table
    places = target_dev * capacity + jnp.sum(before * hit_table, axis=1)
    query_pre = jnp.dot(imp_x, w_in[0], preferred_element_type=jnp.float32)
    gate_pre = jnp.dot(imp_x, w_in[1], preferred_element_type=jnp.float32)
    queries = jax.nn.silu(query_pre).astype(jnp.bfloat16)
    gate_rows = jax.nn.silu(gate_pre).astype(jnp.bfloat16)

    def pack(row_block):
        spread = (
            jnp.zeros((slots_all,) + row_block.shape[1:], row_block.dtype).at[places].set(row_block)
        )
        return spread.reshape((owners, capacity) + row_block.shape[1:])

    def unfold(array_in):
        return array_in.reshape((slots_all,) + array_in.shape[2:])

    def refold(array_in):
        return array_in.reshape((owners, capacity) + array_in.shape[1:])

    got_query, got_gate, got_payload, got_length = (
        lax.all_to_all(pack(queries), "dp", split_axis=0, concat_axis=0, tiled=True),
        lax.all_to_all(pack(gate_rows), "dp", split_axis=0, concat_axis=0, tiled=True),
        lax.all_to_all(pack(grad_y), "dp", split_axis=0, concat_axis=0, tiled=True),
        lax.all_to_all(pack(imp_len), "dp", split_axis=0, concat_axis=0, tiled=True),
    )
    recv_query = unfold(got_query)
    recv_gate = unfold(got_gate)
    recv_payload = unfold(got_payload)
    recv_length = unfold(got_length)
    recv_cot = jnp.dot(recv_payload, w_out.T, preferred_element_type=jnp.float32).astype(
        jnp.bfloat16
    )
    d_query, d_gate, gated, grad_key, grad_value, grad_wk, grad_wv = owner_pass(
        recv_query, recv_gate, recv_cot, recv_length, hist_x[0], w_in[2], w_in[3]
    )
    back_query, back_gate = (
        lax.all_to_all(refold(d_query), "dp", split_axis=0, concat_axis=0, tiled=True),
        lax.all_to_all(refold(d_gate), "dp", split_axis=0, concat_axis=0, tiled=True),
    )
    grad_wo = jnp.dot(gated.T, recv_payload, preferred_element_type=jnp.float32)
    query_back = unfold(back_query)[places]
    gate_back = unfold(back_gate)[places]
    query_term = (query_back.astype(jnp.float32) * silu_slope(query_pre)).astype(jnp.bfloat16)
    gate_term = (gate_back.astype(jnp.float32) * silu_slope(gate_pre)).astype(jnp.bfloat16)
    grad_wq = jnp.dot(imp_x.T, query_term, preferred_element_type=jnp.float32)
    grad_wu = jnp.dot(imp_x.T, gate_term, preferred_element_type=jnp.float32)
    grad_x = lax.psum_scatter(
        jnp.dot(query_term, w_in[0].T, preferred_element_type=jnp.float32)
        + jnp.dot(gate_term, w_in[1].T, preferred_element_type=jnp.float32),
        "mp",
        scatter_dimension=0,
        tiled=True,
    ).astype(jnp.bfloat16)
    factor = (local_rows * owners) ** (-0.5)
    summed = lax.psum((jnp.stack([grad_wq, grad_wu, grad_wk, grad_wv]), grad_wo), "dp")
    grad_w_in = summed[0] * factor
    grad_w_out = summed[1] * factor
    grad_kv = jnp.stack([grad_key, grad_value], axis=1)[None]
    return (grad_x, grad_kv, grad_w_in, grad_w_out)


def solution(mesh):
    placed = (
        P("dp", None),
        P("dp", None),
        P("dp"),
        P(),
        P("dp", None, None),
        P(None, None, "mp"),
        P("mp", None),
        P("dp", None),
    )
    return jax.shard_map(
        on_device,
        mesh=mesh,
        in_specs=placed,
        out_specs=(
            P(("dp", "mp"), None),
            P("dp", None, None, "mp"),
            P(None, None, "mp"),
            P("mp", None),
        ),
        check_vma=False,
    )
```

profile of v0, /device:TPU:1, one launch (start us, length us, event | category | flops | bytes accessed | tf_op | source)
XLA Modules:
  0.0 365.3 jit_solution(11872152857420391893)
XLA Ops:
  8.0 1.0 select_reduce_fusion.1
  9.5 1.1 scatter_custom_fusion
  11.3 13.0 %all-to-all-start = ((s32[64,1,8]{2,1,0:T(1,128)}), s32[64,1,8]{2,1,0:T(1,128)S(1)}, u32[]{:S(2)}, u32[]{:S(2)}) async-start(s32[64,1,8]{2,1,0:T(1,128)} %bitcast.5), calls=%async_computation | async-start | bytes 65536 | tf_op jit(solution)/shard_map/all_to_all | solution.py:143
  24.3 1.1 fusion.74
  25.4 1.2 fusion.78
  26.6 1.5 scatter_custom_fusion.3
  28.2 1.5 scatter_custom_fusion.1
  29.7 3.9 %all-to-all-done = s32[64,1,8]{2,1,0:T(1,128)S(1)} async-done(((s32[64,1,8]{2,1,0:T(1,128)}), s32[64,1,8]{2,1,0:T(1,128)S(1)}, u32[]{:S(2)}, u32[]{:S(2)}) %all-to-all-start) | async-done | bytes 2080 | tf_op jit(solution)/shard_map/all_to_all | solution.py:143
  34.2 6.4 %all-to-all-start.1 = ((bf16[64,8,128]{2,1,0:T(8,128)(2,1)}), bf16[64,8,128]{2,1,0:T(8,128)(2,1)S(1)}, u32[]{:S(2)}, u32[]{:S(2)}) async-start(bf16[64,8,128]{2,1,0:T(8,128)(2,1)} %bitcast.9), calls=%async_computation.1 | async-start | bytes 262144 | tf_op jit(solution)/shard_map/all_to_all | solution.py:140
  40.6 2.8 multiply_convert_fusion.1
  43.4 8.3 %all-to-all-done.1 = bf16[64,8,128]{2,1,0:T(8,128)(2,1)S(1)} async-done(((bf16[64,8,128]{2,1,0:T(8,128)(2,1)}), bf16[64,8,128]{2,1,0:T(8,128)(2,1)S(1)}, u32[]{:S(2)}, u32[]{:S(2)}) %all-to-all-start.1) | async-done | bytes 131104 | tf_op jit(solution)/shard_map/all_to_all | solution.py:140
  51.7 4.4 %all-to-all-start.3 = ((bf16[64,8,128]{2,1,0:T(8,128)(2,1)}), bf16[64,8,128]{2,1,0:T(8,128)(2,1)S(1)}, u32[]{:S(2)}, u32[]{:S(2)}) async-start(bf16[64,8,128]{2,1,0:T(8,128)(2,1)} %bitcast.14), calls=%async_computation.3 | async-start | bytes 262144 | tf_op jit(solution)/shard_map/all_to_all | solution.py:141
  56.1 2.4 convolution_convert_fusion
  58.6 2.3 scatter_custom_fusion.2
  60.9 2.4 reshape.247
  63.3 1.9 copy.146
  65.2 3.2 reshape.246
  68.4 2.4 copy.145
  70.8 0.8 lt.79
  71.6 0.8 lt.85
  72.5 1.0 reshape_reshape.7
  73.7 10.6 %all-to-all-start.2 = ((bf16[64,8,512]{2,1,0:T(8,128)(2,1)}), bf16[64,8,512]{2,1,0:T(8,128)(2,1)}, u32[]{:S(2)}, u32[]{:S(2)}) async-start(bf16[64,8,512]{2,1,0:T(8,128)(2,1)} %bitcast.265), calls=%async_computation.2 | async-start | bytes 1048576 | tf_op jit(solution)/shard_map/all_to_all | solution.py:142
  84.3 10.6 %while.28 = (s32[]{:T(128)}, f32[512,2,64]{0,2,1:T(8,128)}, bf16[2,1024,2,64]{1,3,2,0:T(8,128)(2,1)}, s32[2]{0:T(128)S(1)}, s32[64,8]{1,0:T(8,128)}, /*index=5*/...) while((s32[]{:T(128)}, f32[512,2,64]{0,2,1:T(8,128)}, ...), condition=%wide.wide.region_6.7_spmd.clone, body=%wide.wide.region_5.6_spmd.clone.sunk | while | flops 276431872 | bytes 2240154 | solution.py:51
  86.0 3.6 fusion.154
  91.3 3.7 %fusion.154 = f32[512,2,64]{0,2,1:T(8,128)} fusion(bf16[512,2,64]{0,2,1:T(8,128)(2,1)S(1)} %get-tuple-element.537, pred[512,1024]{0,1:T(8,128)(4,1)S(1)} %broadcast_compare_fusion.6, f32[512,2,64]{0,2,1:T(8,128)} %get-tuple-element.521, bf16[2,1024,2,64]{1,3,2,0:T(8,128)(2,1)S(1)} %get-tuple-element.536, s32[]{:T(128)S(6)} %copy.174, ...), kind=kOutput, calls=%fused_computation.15.clone.clone.1 | convolution fusion | flops 275906560 | bytes 1705472 | tf_op jit(solution)/shard_map/while/body/eval_jaxpr/hrk,khd->rhd/dot_general | solution.py:46
  95.0 2.0 reshape.196
  97.0 1.2 copy.142
  98.2 1.0 multiply_reduce_fusion.1
  99.2 2.7 all-to-all-done.2
  101.9 1.5 multiply_reduce_fusion
  103.5 1.8 multiply_convert_fusion.3
  105.2 17.6 %while.29 = (s32[]{:T(128)}, f32[512,2,64]{0,2,1:T(8,128)S(1)}, f32[2,1024,2,64]{1,3,2,0:T(8,128)}, bf16[2,1024,2,64]{1,3,2,0:T(8,128)(2,1)}, bf16[2,1024,2,64]{...) while((s32[]{:T(128)}, f32[512,2,64]{0,2,1:T(8,128)S(1)}, ...), condition=%wide.wide.region_12.13_spmd.clone, body=%wide.wide.region_11.12_spmd.clone.sunk | while | flops 691667968 | bytes 38545772 | solution.py:86
  107.7 1.6 fusion.169
  109.3 2.5 fusion.166
  113.1 1.0 copy-done.2
  116.5 1.6 fusion.169
  118.1 2.5 fusion.166
  121.9 1.0 copy-done.2
  123.1 0.8 convert_element_type.114
  123.9 7.6 %all-to-all-start.4 = ((bf16[64,8,128]{2,1,0:T(8,128)(2,1)}), bf16[64,8,128]{2,1,0:T(8,128)(2,1)S(1)}, u32[]{:S(2)}, u32[]{:S(2)}) async-start(bf16[64,8,128]{2,1,0:T(8,128)(2,1)} %convert_element_type.114), calls=%async_computation.4 | async-start | bytes 262144 | tf_op jit(solution)/shard_map/all_to_all | solution.py:156
  131.5 1.1 copy.149
  133.3 3.9 %copy.162 = f32[2,1024,2,64]{3,2,1,0:T(2,128)} copy(f32[2,1024,2,64]{1,3,2,0:T(8,128)} %get-tuple-element.97) | data formatting | bytes 2097152 | tf_op jit(solution)/shard_map/reshape | solution.py:91
  137.3 2.6 reshape.245
  139.9 2.7 fusion.60
  142.6 10.4 %all-to-all-start.5 = ((bf16[64,8,128]{2,1,0:T(8,128)(2,1)}), bf16[64,8,128]{2,1,0:T(8,128)(2,1)S(1)}, u32[]{:S(2)}, u32[]{:S(2)}) async-start(bf16[64,8,128]{2,1,0:T(8,128)(2,1)} %reshape_reshape.8), calls=%async_computation.5 | async-start | bytes 262144 | tf_op jit(solution)/shard_map/all_to_all | solution.py:157
  153.3 2.1 fusion.66
  155.3 1.6 copy.151
  157.0 1.3 gather_fusion
  158.3 1.9 fusion.76
  160.2 3.9 %all-to-all-done.5 = bf16[64,8,128]{2,1,0:T(8,128)(2,1)S(1)} async-done(((bf16[64,8,128]{2,1,0:T(8,128)(2,1)}), bf16[64,8,128]{2,1,0:T(8,128)(2,1)S(1)}, u32[]{:S(2)}, u32[]{:S(2)}) %all-to-all-start.5) | async-done | bytes 131104 | tf_op jit(solution)/shard_map/all_to_all | solution.py:157
  164.1 1.3 gather_fusion.1
  165.4 2.0 convolution_add_fusion
  167.9 1.0 convolution_bitcast_fusion.3
  169.2 2.0 pad_maximum_fusion
  171.2 1.2 convert_element_type.124
  172.4 1.3 convert_element_type.121
  174.3 1.2 convert_element_type.122
  175.4 1.3 maximum_bitcast_fusion
  176.8 2.0 copy.156
  178.8 7.0 %reduce-scatter.2.cloned.1.call-done = f32[32,512]{1,0:T(8,128)} async-done(((f32[128,512]{1,0:T(8,128)}), f32[32,512]{1,0:T(8,128)}) %reduce-scatter.2.cloned.1.call-update) | async-done | bytes 65552 | tf_op jit(solution)/shard_map/reduce_scatter | solution.py:166
  185.8 1.5 convert_element_type.120
  187.2 167.2 %all-reduce.3.cloned.1.call-done = (f32[4,512,128]{1,2,0:T(8,128)}, f32[128,512]{1,0:T(8,128)}) async-done(((f32[4,512,128]{1,2,0:T(8,128)}, f32[128,512]{1,0:T(8,128)}), (f32[4,512,128]{1,2,0:T(8,128)}, f32[128,512]{1,0:T(8,128)})) %all-reduce.3.cloned.1.call-update) | async-done | bytes 1310736 | tf_op jit(solution)/shard_map/psum | solution.py:174
  354.4 1.4 broadcast_multiply_fusion
  355.8 1.3 copy.157
  (91 shorter events, 13.4 us)
Async XLA Ops:
  8.0 32.6 %copy-start = (bf16[1,2048,512]{2,1,0:T(8,128)(2,1)S(1)}, bf16[1,2048,512]{2,1,0:T(8,128)(2,1)}, u32[]{:S(2)}) copy-start(bf16[1,2048,512]{2,1,0:T(8,128)(2,1)} %param.16) | copy-start | bytes 6291460
  11.3 22.3 %all-to-all-start = ((s32[64,1,8]{2,1,0:T(1,128)}), s32[64,1,8]{2,1,0:T(1,128)S(1)}, u32[]{:S(2)}, u32[]{:S(2)}) async-start(s32[64,1,8]{2,1,0:T(1,128)} %bitcast.5), calls=%async_computation | async-start | bytes 65536 | tf_op jit(solution)/shard_map/all_to_all | solution.py:143
  25.4 33.1 %copy-start.4 = (f32[128,128]{1,0:T(8,128)}, f32[128,128]{1,0:T(8,128)S(1)}, u32[]{:S(2)}) copy-start(f32[128,128]{1,0:T(8,128)S(1)} %fusion.74) | copy-start | bytes 196612
  26.6 31.9 %copy-start.6 = (f32[128,128]{1,0:T(8,128)}, f32[128,128]{1,0:T(8,128)S(1)}, u32[]{:S(2)}) copy-start(f32[128,128]{1,0:T(8,128)S(1)} %fusion.78) | copy-start | bytes 196612
  33.6 0.6 copy-start.13
  34.2 17.5 %all-to-all-start.1 = ((bf16[64,8,128]{2,1,0:T(8,128)(2,1)}), bf16[64,8,128]{2,1,0:T(8,128)(2,1)S(1)}, u32[]{:S(2)}, u32[]{:S(2)}) async-start(bf16[64,8,128]{2,1,0:T(8,128)(2,1)} %bitcast.9), calls=%async_computation.1 | async-start | bytes 262144 | tf_op jit(solution)/shard_map/all_to_all | solution.py:140
  51.7 6.8 %copy-start.10 = (bf16[64,8,128]{2,1,0:T(8,128)(2,1)}, bf16[64,8,128]{2,1,0:T(8,128)(2,1)S(1)}, u32[]{:S(2)}) copy-start(bf16[64,8,128]{2,1,0:T(8,128)(2,1)S(1)} %all-to-all-done.1) | copy-start | bytes 393220
  51.7 21.9 %all-to-all-start.3 = ((bf16[64,8,128]{2,1,0:T(8,128)(2,1)}), bf16[64,8,128]{2,1,0:T(8,128)(2,1)S(1)}, u32[]{:S(2)}, u32[]{:S(2)}) async-start(bf16[64,8,128]{2,1,0:T(8,128)(2,1)} %bitcast.14), calls=%async_computation.3 | async-start | bytes 262144 | tf_op jit(solution)/shard_map/all_to_all | solution.py:141
  73.7 10.7 %copy-start.9 = (bf16[64,8,128]{2,1,0:T(8,128)(2,1)}, bf16[64,8,128]{2,1,0:T(8,128)(2,1)S(1)}, u32[]{:S(2)}) copy-start(bf16[64,8,128]{2,1,0:T(8,128)(2,1)S(1)} %all-to-all-done.3) | copy-start | bytes 393220
  73.7 28.3 %all-to-all-start.2 = ((bf16[64,8,512]{2,1,0:T(8,128)(2,1)}), bf16[64,8,512]{2,1,0:T(8,128)(2,1)}, u32[]{:S(2)}, u32[]{:S(2)}) async-start(bf16[64,8,512]{2,1,0:T(8,128)(2,1)} %bitcast.265), calls=%async_computation.2 | async-start | bytes 1048576 | tf_op jit(solution)/shard_map/all_to_all | solution.py:142
  105.2 2.4 copy-start.11
  105.2 2.4 copy-start.16
  107.6 1.6 copy-start.8
  109.2 2.6 copy-start.12
  109.2 3.1 copy-start.1
  113.1 1.0 copy-start.2
  114.1 2.4 copy-start.11
  114.1 2.4 copy-start.16
  116.5 1.6 copy-start.8
  118.1 2.6 copy-start.12
  118.1 3.1 copy-start.1
  121.9 1.0 copy-start.2
  123.9 18.7 %all-to-all-start.4 = ((bf16[64,8,128]{2,1,0:T(8,128)(2,1)}), bf16[64,8,128]{2,1,0:T(8,128)(2,1)S(1)}, u32[]{:S(2)}, u32[]{:S(2)}) async-start(bf16[64,8,128]{2,1,0:T(8,128)(2,1)} %convert_element_type.114), calls=%async_computation.4 | async-start | bytes 262144 | tf_op jit(solution)/shard_map/all_to_all | solution.py:156
  142.5 25.4 %copy-start.3 = (bf16[128,512]{1,0:T(8,128)(2,1)S(1)}, bf16[128,512]{1,0:T(8,128)(2,1)}, u32[]{:S(2)}) copy-start(bf16[128,512]{1,0:T(8,128)(2,1)} %param.12) | copy-start | bytes 393220
  142.6 21.5 %all-to-all-start.5 = ((bf16[64,8,128]{2,1,0:T(8,128)(2,1)}), bf16[64,8,128]{2,1,0:T(8,128)(2,1)S(1)}, u32[]{:S(2)}, u32[]{:S(2)}) async-start(bf16[64,8,128]{2,1,0:T(8,128)(2,1)} %reshape_reshape.8), calls=%async_computation.5 | async-start | bytes 262144 | tf_op jit(solution)/shard_map/all_to_all | solution.py:157
  153.0 32.8 %reduce-scatter.2.cloned.1.call-start = ((), (), s32[]{:S(2)}) async-start(), calls=%async_computation.7 | async-start | bytes 327680 | tf_op jit(solution)/shard_map/reduce_scatter | solution.py:166
  158.3 9.6 %copy-start.7 = (f32[128,128]{1,0:T(8,128)S(1)}, f32[128,128]{1,0:T(8,128)}, u32[]{:S(2)}) copy-start(f32[128,128]{1,0:T(8,128)} %copy-done.6) | copy-start | bytes 196612
  158.3 10.6 %copy-start.5 = (f32[128,128]{1,0:T(8,128)S(1)}, f32[128,128]{1,0:T(8,128)}, u32[]{:S(2)}) copy-start(f32[128,128]{1,0:T(8,128)} %copy-done.4) | copy-start | bytes 196612
  165.4 3.5 copy-start.14
  167.4 187.0 %all-reduce.3.cloned.1.call-start = ((), (), s32[]{:S(2)}) async-start(), calls=%async_computation.8 | async-start | bytes 2621440 | tf_op jit(solution)/shard_map/psum | solution.py:174
  354.4 2.7 copy-start.15
Sparse Core Ops, SparseCore 0:
  167.5 18.1 reduce-scatter.1
Sparse Core Ops, SparseCore 1:
  171.8 182.5 all-reduce.2
where the time goes:
time: 368 us; the launch traced here: 365 us
  waiting for transfers between devices  193 us (52%)
  starting transfers between devices  52.7 us (14%)
  local copies, waits for them, and re-layouts  45.1 us (12%)
  matrix products  38.7 us (11%)
  other arithmetic  17 us (5%)
  between operations  15.9 us (4%)
    psum x1, waiting for transfers between devices, on_device(): lax.psum((jnp.stack([grad_wq, grad_wu, grad_wk, grad_wv]), grad_wo), 'dp')  167 us
    all_to_all x1, starting transfers between devices, on_device(): lax.all_to_all(pack(imp_len), 'dp', split_axis=0, concat_axis=0, tiled=True)  13 us
    all_to_all x1, starting transfers between devices, on_device(): lax.all_to_all(pack(grad_y), 'dp', split_axis=0, concat_axis=0, tiled=True)  10.6 us
    all_to_all x1, starting transfers between devices, on_device(): lax.all_to_all(refold(d_gate), 'dp', split_axis=0, concat_axis=0, tiled=T...  10.4 us
    unnamed x28, local copies, waits for them, and re-layouts  8.49 us
    all_to_all x1, waiting for transfers between devices, on_device(): lax.all_to_all(pack(queries), 'dp', split_axis=0, concat_axis=0, tiled=True)  8.35 us
    all_to_all x1, starting transfers between devices, on_device(): lax.all_to_all(refold(d_query), 'dp', split_axis=0, concat_axis=0, tiled=...  7.57 us
  transfers between devices with their start and end apart: 8, of which 6 were waited for; matrix products, arithmetic and copies ran while one was open for 19% of the time, Pallas kernels for 0%

commit v1 on v0

v1 whole, which is shorter than its diff:
```python
import jax
import jax.numpy as jnp
from jax import lax
from jax.experimental import pallas as pl
from jax.experimental.pallas import tpu as pltpu
from jax.sharding import PartitionSpec as P

DH = 64
EPSILON = 1e-05
CAP = 8
BLOCK = 256
F32 = jnp.float32
BF16 = jnp.bfloat16
VMEM = pl.BlockSpec(memory_space=pltpu.VMEM)
SMEM = pl.BlockSpec(memory_space=pltpu.SMEM)
PARAMS = pltpu.CompilerParams(vmem_limit_bytes=48 * 1024 * 1024)


def nn(a, b):
    return lax.dot_general(a, b, (((1,), (0,)), ((), ())), preferred_element_type=F32)


def nt(a, b):
    return lax.dot_general(a, b, (((1,), (1,)), ((), ())), preferred_element_type=F32)


def tn(a, b):
    return lax.dot_general(a, b, (((0,), (0,)), ((), ())), preferred_element_type=F32)


def sigmoid(v):
    return 0.5 * jnp.tanh(0.5 * v) + 0.5


def silu_and_slope(v):
    s = sigmoid(v)
    return v * s, s * (1.0 + v * (1.0 - s))


def iota(shape, dim):
    return lax.broadcasted_iota(jnp.int32, shape, dim)


def spread(parts):
    count = parts[0].shape[0] // 8
    cut = [p.reshape(count, 8, p.shape[1]) for p in parts]
    joined = jnp.concatenate(cut, axis=1)
    return joined.reshape(count * 8 * len(parts), parts[0].shape[1])


def pre_kernel(x_ref, hist_ref, len_ref, owner_ref, w_ref, wo_ref, gy_ref, send_ref, aux_ref, place_ref):
    rows = x_ref.shape[0]
    owners = owner_ref.shape[1]
    x = x_ref[...]
    queries, slope_q = silu_and_slope(nn(x, w_ref[0]))
    gates, slope_g = silu_and_slope(nn(x, w_ref[1]))
    cot = nt(gy_ref[...], wo_ref[...]).astype(BF16).astype(F32)
    gates = gates.astype(BF16).astype(F32)
    aux_ref[0] = slope_q
    aux_ref[1] = slope_g
    aux_ref[2] = gates
    aux_ref[3] = cot
    named = hist_ref[...] == iota((rows, owners), 1)
    target = jnp.sum(jnp.where(named, owner_ref[...].astype(F32), 0.0), axis=1, keepdims=True)
    target = jnp.transpose(jnp.broadcast_to(target, (rows, rows)))
    hit = target[:owners] == iota((owners, rows), 0).astype(F32)
    hit = jnp.where(hit, 1.0, 0.0)
    earlier = jnp.where(iota((rows, rows), 0) < iota((rows, rows), 1), 1.0, 0.0)
    before = nn(hit.astype(BF16), earlier.astype(BF16))
    rank = jnp.sum(before * hit, axis=0, keepdims=True)
    slot = target[:1] * float(CAP) + rank
    slots = owners * CAP
    place = jnp.where(iota((slots, rows), 0).astype(F32) == slot, 1.0, 0.0).astype(BF16)
    place_ref[...] = place
    length = len_ref[...].astype(F32)
    high = jnp.floor(length * (1.0 / 256.0))
    low = length - 256.0 * high
    digits = jnp.where(iota((rows, rows), 0) == 0, high, low)
    digits = jnp.transpose(digits)
    payload = jnp.concatenate(
        [queries.astype(BF16), (cot * gates).astype(BF16), digits.astype(BF16)], axis=1
    )
    packed = nn(place, payload)
    width = queries.shape[1]
    send_ref[...] = spread(
        [packed[:, :width], packed[:, width : 2 * width], packed[:, 2 * width :]]
    ).astype(BF16)


def project_kernel(ev_ref, w_ref, k_ref, v_ref, kt_ref, vt_ref, slope_ref):
    def step(b, carry):
        at = pl.ds(pl.multiple_of(b * 512, 512), 512)
        ev = ev_ref[at, :]
        keys, slope = silu_and_slope(nn(ev, w_ref[2]))
        values = nn(ev, w_ref[3])
        k_ref[at, :] = keys.astype(BF16)
        v_ref[at, :] = values.astype(BF16)
        slope_ref[at, :] = slope
        kt_ref[:, at] = jnp.transpose(keys.astype(BF16))
        vt_ref[:, at] = jnp.transpose(values.astype(BF16))
        return carry

    lax.fori_loop(0, ev_ref.shape[0] // 512, step, 0)


def attend_kernel(
    recv_ref, k_ref, v_ref, kt_ref, vt_ref, slope_ref,
    back_ref, gkv_ref, term_ref,
    w_scr, s_scr, att_scr, dq_scr,
):
    slots = recv_ref.shape[0] // 3
    events, width = k_ref.shape
    heads = width // DH
    got = recv_ref[...].astype(F32).reshape(slots // CAP, 3 * CAP, width)
    q = got[:, :CAP].reshape(slots, width)
    dn = got[:, CAP : 2 * CAP].reshape(slots, width)
    digits = got[:, 2 * CAP :].reshape(slots, width)
    digits = jnp.transpose(digits)
    length = digits[0:1] * 256.0 + digits[1:2]
    qt = jnp.transpose(q)
    head_row = iota((width, slots), 0) // DH
    head_col = iota((slots, width), 1) // DH
    qt_half = (qt * (0.5 * DH ** (-0.5))).astype(BF16)
    zero = jnp.zeros((), BF16)
    qt_of = [jnp.where(head_row == h, qt_half, zero) for h in range(heads)]
    att_scr[...] = jnp.zeros_like(att_scr)

    def forward(b, carry):
        start = pl.multiple_of(b * BLOCK, BLOCK)
        at = pl.ds(start, BLOCK)
        visible = (iota((BLOCK, slots), 0) + start).astype(F32) < length
        for h in range(heads):
            half = nn(k_ref[at, :], qt_of[h])
            twice = jnp.where(visible, jnp.tanh(half) + 1.0, 0.0)
            weights = half * twice
            s_scr[h, at, :] = (twice + weights * (2.0 - twice)).astype(BF16)
            weights = weights.astype(BF16)
            w_scr[h, at, :] = weights
            mine = pl.ds(h * DH, DH)
            att_scr[mine, :] += nn(vt_ref[mine, at], weights)
        return carry

    lax.fori_loop(0, events // BLOCK, forward, 0)
    att = att_scr[...].reshape(heads, DH, slots)
    inverse = lax.rsqrt(jnp.mean(att * att, axis=1, keepdims=True) + EPSILON)
    normed = att * inverse
    dnt = jnp.transpose(dn).reshape(heads, DH, slots)
    d_att = inverse * (dnt - normed * jnp.mean(dnt * normed, axis=1, keepdims=True))
    d_att = d_att.reshape(width, slots)
    d_att_t = d_att.astype(BF16)
    d_att = jnp.transpose(d_att).astype(BF16)
    normed = jnp.transpose(normed.reshape(width, slots))
    q_bf = q.astype(BF16)
    dt_of = [jnp.where(head_row == h, d_att_t, zero) for h in range(heads)]
    d_of = [jnp.where(head_col == h, d_att, zero) for h in range(heads)]
    q_of = [jnp.where(head_col == h, q_bf, zero) for h in range(heads)]
    dq_scr[...] = jnp.zeros_like(dq_scr)

    def backward(b, carry):
        at = pl.ds(pl.multiple_of(b * BLOCK, BLOCK), BLOCK)
        d_keys = jnp.zeros((BLOCK, width), F32)
        d_values = jnp.zeros((BLOCK, width), F32)
        for h in range(heads):
            ds = (nn(v_ref[at, :], dt_of[h]) * s_scr[h, at, :].astype(F32)).astype(BF16)
            mine = pl.ds(h * DH, DH)
            dq_scr[mine, :] += nn(kt_ref[mine, at], ds)
            d_keys += nn(ds, q_of[h])
            d_values += nn(w_scr[h, at, :], d_of[h])
        d_keys = d_keys * (0.5 * DH ** (-0.5))
        gkv_ref[at, :width] = d_keys.astype(BF16)
        gkv_ref[at, width:] = d_values.astype(BF16)
        term_ref[at, :] = (d_keys * slope_ref[at, :]).astype(BF16)
        return carry

    lax.fori_loop(0, events // BLOCK, backward, 0)
    d_query = jnp.transpose(dq_scr[...] * (0.5 * DH ** (-0.5)))
    back_ref[...] = spread([d_query, normed]).astype(BF16)


def history_grads_kernel(core_ref, ev_ref, term_ref, gkv_ref, mine_ref, other_ref, scr):
    width = term_ref.shape[1]
    gk = tn(ev_ref[...], term_ref[...])
    gv = tn(ev_ref[...], gkv_ref[:, width:])
    rows = spread([gk, gv]).astype(BF16)
    half = rows.shape[0] // 2
    scr[0] = rows[:half]
    scr[1] = rows[half:]
    core = core_ref[0]
    mine_ref[...] = scr[core]
    other_ref[...] = scr[1 - core]


def post_kernel(core_ref, back_ref, place_ref, aux_ref, x_ref, w_ref, gy_ref, mine_ref, other_ref, gx_ref, scr):
    slots, rows = place_ref.shape
    width = back_ref.shape[1]
    got = back_ref[...].astype(F32).reshape(slots // CAP, 2 * CAP, width)
    d_query = got[:, :CAP].reshape(slots, width).astype(BF16)
    normed = got[:, CAP:].reshape(slots, width).astype(BF16)
    both = tn(place_ref[...], jnp.concatenate([d_query, normed], axis=1))
    d_query = both[:, :width]
    normed = both[:, width:]
    gates = aux_ref[2]
    gated = (normed * gates).astype(BF16)
    d_gate = (aux_ref[3] * normed).astype(BF16).astype(F32)
    q_term = (d_query * aux_ref[0]).astype(BF16)
    g_term = (d_gate * aux_ref[1]).astype(BF16)
    gx_ref[...] = (nt(q_term, w_ref[0]) + nt(g_term, w_ref[1])).astype(BF16)
    x = x_ref[...]
    gq = tn(x, q_term)
    gg = tn(x, g_term)
    go = tn(gated, gy_ref[...])
    go = jnp.concatenate([go[:, i * width : (i + 1) * width] for i in range(go.shape[1] // width)], axis=0)
    out = spread([gq, gg, go]).astype(BF16)
    half = out.shape[0] // 2
    scr[0] = out[:half]
    scr[1] = out[half:]
    core = core_ref[0]
    mine_ref[...] = scr[core]
    other_ref[...] = scr[1 - core]


def pair_kernel(a_ref, b_ref, c_ref, d_ref, out_ref):
    width = a_ref.shape[1]
    first = a_ref[...].astype(F32) + b_ref[...].astype(F32)
    second = c_ref[...].astype(F32) + d_ref[...].astype(F32)
    chunks = first.shape[0] // 16
    joined = jnp.concatenate(
        [first.reshape(chunks, 16, width), second.reshape(chunks, 24, width)], axis=1
    )
    out_ref[...] = joined.reshape(chunks * 40, width).astype(BF16)


def sum_kernel(factor, in_ref, out_ref):
    chunks = in_ref.shape[0] // 40
    total = jnp.sum(in_ref[...].astype(F32).reshape(chunks, 40, in_ref.shape[1]), axis=0)
    total = total * factor
    out_ref[...] = jnp.broadcast_to(total[None], (chunks, 40, total.shape[1])).reshape(out_ref.shape).astype(BF16)


def unfold_kernel(core_ref, mine_ref, other_ref, win_ref, wout_ref, scr):
    width = mine_ref.shape[1]
    core = core_ref[0]
    for ref, which in ((mine_ref, core), (other_ref, 1 - core)):
        got = ref[...].astype(F32)
        chunks = got.shape[0] // 40
        got = got.reshape(chunks, 5, 8, width)
        size = chunks * 8
        at = pl.ds(pl.multiple_of(which * size, size), size)
        for place, index in enumerate((2, 3, 0, 1)):
            win_ref[index, at, :] = got[:, place].reshape(size, width)
        scr[at, :] = got[:, 4].reshape(size, width)
    rows = wout_ref.shape[0]
    for i in range(wout_ref.shape[1] // width):
        wout_ref[:, i * width : (i + 1) * width] = scr[i * rows : (i + 1) * rows, :]


def call(kernel, outs, ins, specs=None, scratch=(), flops=0, moved=0):
    return pl.pallas_call(
        kernel,
        out_shape=[jax.ShapeDtypeStruct(s, d) for s, d in outs],
        in_specs=specs or [VMEM] * len(ins),
        out_specs=[VMEM] * len(outs),
        scratch_shapes=list(scratch),
        compiler_params=PARAMS,
        cost_estimate=pl.CostEstimate(flops=flops, bytes_accessed=moved, transcendentals=0),
    )(*ins)


def on_device(imp_x, imp_hist, imp_len, owner_map, hist_x, w_in, w_out, grad_y):
    owners = lax.axis_size("dp")
    planes = lax.axis_size("mp")
    rows, depth = imp_x.shape
    width = w_in.shape[2]
    slots = owners * CAP
    events = hist_x.shape[1]
    chips = owners // 2
    place_of = lax.axis_index("dp")
    core = (place_of % 2).reshape(1)
    hist = hist_x[0]
    pairs = [(i, i ^ 1) for i in range(owners)]
    same_core = [[2 * i + c for i in range(chips)] for c in range(2)]

    def swap(a):
        return lax.ppermute(a, "dp", pairs)

    def exchange(a):
        a = a.reshape(owners, a.shape[0] // owners, width)
        a = lax.all_to_all(a, "dp", 0, 0, tiled=True)
        return a.reshape(a.shape[0] * a.shape[1], width)

    def exchange_core(a):
        a = a.reshape(chips, a.shape[0] // chips, width)
        a = lax.all_to_all(a, "dp", 0, 0, axis_index_groups=same_core, tiled=True)
        return a.reshape(a.shape[0] * a.shape[1], width)

    send, aux, place = call(
        pre_kernel,
        [((3 * slots, width), BF16), ((4, rows, width), F32), ((slots, rows), BF16)],
        (imp_x, imp_hist, imp_len.reshape(1, rows), owner_map.reshape(1, owners), w_in, w_out, grad_y),
        flops=2 * rows * depth * width * 3,
        moved=1 << 20,
    )
    recv = exchange(send)
    keys, values, keys_t, values_t, key_slope = call(
        project_kernel,
        [((events, width), BF16)] * 2 + [((width, events), BF16)] * 2 + [((events, width), F32)],
        (hist, w_in),
        flops=4 * events * depth * width,
        moved=5 << 20,
    )
    back, gkv, term = call(
        attend_kernel,
        [((2 * slots, width), BF16), ((events, 2 * width), BF16), ((events, width), BF16)],
        (recv, keys, values, keys_t, values_t, key_slope),
        scratch=[
            pltpu.VMEM((width // DH, events, slots), BF16),
            pltpu.VMEM((width // DH, events, slots), BF16),
            pltpu.VMEM((width, slots), F32),
            pltpu.VMEM((width, slots), F32),
        ],
        flops=12 * events * slots * width,
        moved=4 << 20,
    )
    back = exchange(back)
    half = depth * width * 2 // 2 // width
    kv_mine, kv_other = call(
        history_grads_kernel,
        [((half, width), BF16)] * 2,
        (core, hist, term, gkv),
        specs=[SMEM, VMEM, VMEM, VMEM],
        scratch=[pltpu.VMEM((2, half, width), BF16)],
        flops=4 * events * depth * width,
        moved=4 << 20,
    )
    kv_other = swap(kv_other)
    half = depth * 3 // 2
    mine, other, gx = call(
        post_kernel,
        [((half, width), BF16)] * 2 + [((rows, depth), BF16)],
        (core, back, place, aux, imp_x, w_in, grad_y),
        specs=[SMEM] + [VMEM] * 6,
        scratch=[pltpu.VMEM((2, half, width), BF16)],
        flops=2 * rows * depth * width * 5,
        moved=2 << 20,
    )
    other = swap(other)
    (summed,) = call(
        pair_kernel, [((chips * 40, width), BF16)], (kv_mine, kv_other, mine, other), moved=1 << 20
    )
    plane = lax.axis_index("mp")
    share = rows // planes
    own = lax.dynamic_slice_in_dim(gx, plane * share, share, 0)
    total = own.astype(F32)
    for step in range(1, planes):
        target = (plane + step) % planes
        part = lax.dynamic_slice_in_dim(gx, target * share, share, 0)
        part = lax.ppermute(part, "mp", [(i, (i + step) % planes) for i in range(planes)])
        total = total + part.astype(F32)
    grad_x = total.astype(BF16)
    factor = (rows * owners) ** (-0.5)
    (piece,) = call(
        lambda i, o: sum_kernel(factor, i, o),
        [((chips * 40, width), BF16)],
        (exchange_core(summed),),
        moved=1 << 20,
    )
    mine = exchange_core(piece)
    other = swap(mine)
    grad_w_in, grad_w_out = call(
        unfold_kernel,
        [((4, depth, width), F32), ((width, depth), F32)],
        (core, mine, other),
        specs=[SMEM, VMEM, VMEM],
        scratch=[pltpu.VMEM((depth, width), F32)],
        moved=3 << 20,
    )
    grad_kv = gkv.reshape(1, events, 2, width)
    return (grad_x, grad_kv, grad_w_in, grad_w_out)


def solution(mesh):
    placed = (
        P("dp", None),
        P("dp", None),
        P("dp"),
        P(),
        P("dp", None, None),
        P(None, None, "mp"),
        P("mp", None),
        P("dp", None),
    )
    return jax.shard_map(
        on_device,
        mesh=mesh,
        in_specs=placed,
        out_specs=(
            P(("dp", "mp"), None),
            P("dp", None, None, "mp"),
            P(None, None, "mp"),
            P("mp", None),
        ),
        check_vma=False,
    )
```

time: 368 us -> 132 us (0.36)
  waiting for transfers between devices: 193 us -> 33.2 us
  matrix products: 38.7 us -> 0 us
  Pallas kernels: 0 us -> 21 us
  starting transfers between devices: 52.7 us -> 32.6 us
  local copies, waits for them, and re-layouts: 45.1 us -> 25.7 us
  blocking collectives: 0 us -> 16.9 us
  other arithmetic: 17 us -> 0.63 us
  between operations: 15.9 us -> 0.86 us
    psum x1 -> x0, waiting for transfers between devices: 167 us -> none  [on_device(): lax.psum((jnp.stack([grad_wq, grad_wu, grad_wk, grad_wv]), grad_wo), 'dp')]
    dot_general x24 -> x0, matrix products: 38.7 us -> none  [the longest x2 7.32 us: forward(): jnp.einsum('hrk,khd->rhd', weights, value_block, preferred_element_type=j...]
    all_to_all x6 -> x3, starting transfers between devices: 52.4 us -> 23.1 us  [the longest x2 18.6 us: exchange(): a = lax.all_to_all(a, 'dp', 0, 0, tiled=True)]
    pallas_call x0 -> x8, Pallas kernels: none -> 21 us  [call(): pl.pallas_call(kernel, out_shape=[jax.ShapeDtypeStruct(s, d) for s, d in...]
    all_to_all x0 -> x1, blocking collectives: none -> 16.9 us  [exchange_core(): a = lax.all_to_all(a, 'dp', 0, 0, axis_index_groups=same_core, tiled=True)]
    unnamed x28 -> x67, local copies, waits for them, and re-layouts: 8.49 us -> 24.6 us
    all_to_all x6 -> x3, waiting for transfers between devices: 18.9 us -> 31.5 us  [the longest x2 20.3 us: exchange(): a = lax.all_to_all(a, 'dp', 0, 0, tiled=True)]
    reshape x4 -> x1, local copies, waits for them, and re-layouts: 12.1 us -> 1.09 us  [on_device(): grad_kv = gkv.reshape(1, events, 2, width)]
  transfers between devices with their start and end apart: 8 -> 9, of which waited for: 6 -> 5; matrix products, arithmetic and copies ran while one was open for 19% -> 1% of each run, Pallas kernels for 0% -> 3%
where the time goes in v1:
time: 132 us; the launch traced here: 131 us
  waiting for transfers between devices  33.2 us (25%)
  starting transfers between devices  32.6 us (25%)
  local copies, waits for them, and re-layouts  25.7 us (19%)
  Pallas kernels  21 us (16%)
  blocking collectives  16.9 us (13%)
    unnamed x67, local copies, waits for them, and re-layouts  24.6 us
    pallas_call x8, Pallas kernels, call(): pl.pallas_call(kernel, out_shape=[jax.ShapeDtypeStruct(s, d) for s, d in...  21 us
    all_to_all x2, waiting for transfers between devices, exchange(): a = lax.all_to_all(a, 'dp', 0, 0, tiled=True)  20.3 us
    all_to_all x2, starting transfers between devices, exchange(): a = lax.all_to_all(a, 'dp', 0, 0, tiled=True)  18.6 us
    all_to_all x1, blocking collectives, exchange_core(): a = lax.all_to_all(a, 'dp', 0, 0, axis_index_groups=same_core, tiled=True)  16.9 us
    all_to_all x1, waiting for transfers between devices, exchange_core(): a = lax.all_to_all(a, 'dp', 0, 0, axis_index_groups=same_core, tiled=True)  11.2 us
    ppermute x3, starting transfers between devices, on_device(): lax.ppermute(part, 'mp', [(i, (i + step) % planes) for i in range(planes)])  5.06 us
    all_to_all x1, starting transfers between devices, exchange_core(): a = lax.all_to_all(a, 'dp', 0, 0, axis_index_groups=same_core, tiled=True)  4.56 us
  transfers between devices with their start and end apart: 9, of which 5 were waited for; matrix products, arithmetic and copies ran while one was open for 1% of the time, Pallas kernels for 3%

profile of v1, /device:TPU:1, one launch (start us, length us, event | category | flops | bytes accessed | tf_op | source)
XLA Modules:
  0.0 130.9 jit_solution(3960115460200505897)
XLA Ops:
  0.6 0.8 copy.12.hist_ref
  1.4 1.0 copy-done.2
  2.4 0.9 copy-done.7
  3.3 0.9 copy-done.9
  4.2 0.9 copy-done.16
  5.2 0.7 copy-done.21
  5.8 0.7 copy-done.22
  6.5 1.4 %shard_map.111 = (bf16[1536,128]{1,0:T(8,128)(2,1)}, f32[4,128,128]{2,1,0:T(8,128)S(1)}, bf16[512,128]{1,0:T(8,128)(2,1)S(1)}) custom-call(bf16[128,512]{1,0:T(8,128)(2,1)S(1)} %copy-done.7, s32[128,1]{1,0:T(8,128)S(1)} %copy.12.hist_ref, s32[1,128]{1,0:T(1,128)S(1)} %bitcast.21, s32[1,64]{1,0:T(1,128)S(1)} %bitcast.22, bf16[4,512,128]{2,1,0:T(8,128)(2,1)S(1)} %copy-done.2, ...), custom_call_target="tpu_custom_call" | custom-call | flops 50331648 | bytes 1048576 | tf_op jit(solution)/shard_map/pallas_call | solution.py:258
  7.9 0.7 copy-done.14
  8.6 0.7 copy-done.19
  9.2 13.0 %all-to-all-start = ((bf16[64,24,128]{2,1,0:T(8,128)(2,1)}), bf16[64,24,128]{2,1,0:T(8,128)(2,1)S(1)}, u32[]{:S(2)}, u32[]{:S(2)}) async-start(bf16[64,24,128]{2,1,0:T(8,128)(2,1)} %bitcast.3), calls=%async_computation | async-start | bytes 786432 | tf_op jit(solution)/shard_map/all_to_all | solution.py:288
  22.2 0.0 copy-done.3
  22.2 0.0 copy-start
  22.2 1.6 %copy-done = bf16[1,2048,512]{2,1,0:T(8,128)(2,1)S(1)} copy-done((bf16[1,2048,512]{2,1,0:T(8,128)(2,1)S(1)}, bf16[1,2048,512]{2,1,0:T(8,128)(2,1)}, u32[]{:S(2)}) %copy-start) | copy-done | bytes 2097176
  23.8 2.1 %shard_map.112 = (bf16[2048,128]{1,0:T(8,128)(2,1)S(1)}, bf16[2048,128]{1,0:T(8,128)(2,1)S(1)}, bf16[128,2048]{1,0:T(8,128)(2,1)S(1)}, bf16[128,2048]{1,0:T(8,128)(2,1)S(1)}, f32[2048,128]{1,0:T(8,128)S(1)}) custom-call(bf16[2048,512]{1,0:T(8,128)(2,1)S(1)} %bitcast.12, bf16[4,512,128]{2,1,0:T(8,128)(2,1)S(1)} %copy-done.3), custom_call_target="tpu_custom_call" | custom-call | flops 536870912 | bytes 5242880 | tf_op jit(solution)/shard_map/pallas_call | solution.py:258
  25.9 0.0 copy-start.23
  25.9 1.0 copy-done.23
  26.9 0.8 copy-done.25
  27.7 0.8 copy-done.27
  28.5 0.8 copy-done.29
  29.3 0.8 copy-done.31
  30.1 7.2 %all-to-all-done = bf16[64,24,128]{2,1,0:T(8,128)(2,1)S(1)} async-done(((bf16[64,24,128]{2,1,0:T(8,128)(2,1)}), bf16[64,24,128]{2,1,0:T(8,128)(2,1)S(1)}, u32[]{:S(2)}, u32[]{:S(2)}) %all-to-all-start) | async-done | bytes 393248 | tf_op jit(solution)/shard_map/all_to_all | solution.py:288
  37.3 0.7 copy-done.11
  38.0 1.0 copy-done.12
  39.0 1.2 copy-done.24
  40.2 1.0 copy-done.26
  41.3 1.0 copy-done.28
  42.3 1.0 copy-done.30
  43.4 1.0 copy-done.32
  44.4 13.7 %shard_map.113 = (bf16[1024,128]{1,0:T(8,128)(2,1)S(1)}, bf16[2048,256]{1,0:T(8,128)(2,1)S(1)}, bf16[2048,128]{1,0:T(8,128)(2,1)S(1)}) custom-call(bf16[1536,128]{1,0:T(8,128)(2,1)S(1)} %bitcast.19, bf16[2048,128]{1,0:T(8,128)(2,1)S(1)} %copy-done.26, bf16[2048,128]{1,0:T(8,128)(2,1)S(1)} %copy-done.28, bf16[128,2048]{1,0:T(8,128)(2,1)S(1)} %copy-done.30, ...), custom_call_target="tpu_custom_call" | custom-call | flops 1610612736 | bytes 4194304 | tf_op jit(solution)/shard_map/pallas_call | solution.py:258
  58.1 0.0 copy-start.4
  58.1 1.0 copy-done.4
  59.1 0.7 copy-done.13
  59.8 5.6 %all-to-all-start.1 = ((bf16[64,16,128]{2,1,0:T(8,128)(2,1)}), bf16[64,16,128]{2,1,0:T(8,128)(2,1)S(1)}, u32[]{:S(2)}, u32[]{:S(2)}) async-start(bf16[64,16,128]{2,1,0:T(8,128)(2,1)} %bitcast.20), calls=%async_computation.1 | async-start | bytes 524288 | tf_op jit(solution)/shard_map/all_to_all | solution.py:288
  65.4 13.2 %all-to-all-done.1 = bf16[64,16,128]{2,1,0:T(8,128)(2,1)S(1)} async-done(((bf16[64,16,128]{2,1,0:T(8,128)(2,1)}), bf16[64,16,128]{2,1,0:T(8,128)(2,1)S(1)}, u32[]{:S(2)}, u32[]{:S(2)}) %all-to-all-start.1) | async-done | bytes 262176 | tf_op jit(solution)/shard_map/all_to_all | solution.py:288
  78.6 1.0 copy-done.10
  79.6 0.9 copy-done.15
  80.5 0.9 copy-done.20
  81.4 0.6 shard_map.114
  82.0 0.0 copy-start.17
  82.0 0.3 collective-permute-start.4
  82.3 1.3 shard_map.115
  83.6 0.0 copy-start.6
  83.7 0.3 collective-permute-start.3
  84.0 1.1 collective-permute-done.3.b_ref
  85.1 0.0 collective-permute-done.4.d_ref
  85.1 0.1 shard_map.116
  85.2 0.0 copy-start.18
  85.2 16.9 %all_to_all.20 = bf16[32,40,128]{2,1,0:T(8,128)(2,1)S(1)} all-to-all(bf16[32,40,128]{2,1,0:T(8,128)(2,1)S(1)} %bitcast.17), channel_id=1, replica_groups={{0,8,16,24,32,40,48,56,64,72,80,88,96,104,112,120,128,136,144,152,160,1..., dimensions={0} | all-to-all | bytes 655360 | tf_op jit(solution)/shard_map/all_to_all | solution.py:293
  102.1 0.8 shard_map.117
  102.9 4.6 %all-to-all-start.3 = ((bf16[32,40,128]{2,1,0:T(8,128)(2,1)}), bf16[32,40,128]{2,1,0:T(8,128)(2,1)S(1)}, u32[]{:S(2)}, u32[]{:S(2)}) async-start(bf16[32,40,128]{2,1,0:T(8,128)(2,1)} %bitcast.10), calls=%async_computation.3 | async-start | bytes 655360 | tf_op jit(solution)/shard_map/all_to_all | solution.py:293
  107.5 11.2 %all-to-all-done.3 = bf16[32,40,128]{2,1,0:T(8,128)(2,1)S(1)} async-done(((bf16[32,40,128]{2,1,0:T(8,128)(2,1)}), bf16[32,40,128]{2,1,0:T(8,128)(2,1)S(1)}, u32[]{:S(2)}, u32[]{:S(2)}) %all-to-all-start.3) | async-done | bytes 327712 | tf_op jit(solution)/shard_map/all_to_all | solution.py:293
  118.7 3.7 %collective-permute-start.5 = (bf16[1280,128]{1,0:T(8,128)(2,1)S(1)}, bf16[1280,128]{1,0:T(8,128)(2,1)S(1)}, u32[]{:S(2)}, u32[]{:S(2)}) collective-permute-start(bf16[1280,128]{1,0:T(8,128)(2,1)S(1)} %bitcast.14), channel_id=1, source_target_pairs={{0,4},{4,0},{8,12},{12,8},{16,20},{20,16},{24,28},{28,24},{32,36},... | collective-permute-start | bytes 983048 | tf_op jit(solution)/shard_map/ppermute | solution.py:284
  122.4 1.4 %collective-permute-start = (bf16[32,512]{1,0:T(8,128)(2,1)S(1)}, bf16[32,512]{1,0:T(8,128)(2,1)S(1)}, u32[]{:S(2)}, u32[]{:S(2)}) collective-permute-start(bf16[32,512]{1,0:T(8,128)(2,1)S(1)} %get-tuple-element.40), channel_id=1, source_target_pairs={{0,1},{1,2},{2,3},{3,0},{4,5},{5,6},{6,7},{7,4},{8,9},{9,10},{10,1... | collective-permute-start | bytes 98312 | tf_op jit(solution)/shard_map/ppermute | solution.py:357
  123.8 2.6 %collective-permute-start.1 = (bf16[32,512]{1,0:T(8,128)(2,1)S(1)}, bf16[32,512]{1,0:T(8,128)(2,1)S(1)}, u32[]{:S(2)}, u32[]{:S(2)}) collective-permute-start(bf16[32,512]{1,0:T(8,128)(2,1)S(1)} %get-tuple-element.42), channel_id=1, source_target_pairs={{0,2},{1,3},{2,0},{3,1},{4,6},{5,7},{6,4},{7,5},{8,10},{9,11},{10,... | collective-permute-start | bytes 98312 | tf_op jit(solution)/shard_map/ppermute | solution.py:357
  126.4 1.1 collective-permute-start.2
  127.5 0.0 copy-done.6
  127.5 1.1 reshape.51
  128.6 0.0 collective-permute-done
  128.6 0.0 collective-permute-done.1
  128.6 0.6 collective-permute-done.2
  129.2 0.6 add_convert_fusion
  129.8 0.0 collective-permute-done.5.other_ref
  129.8 1.1 shard_map.118
  (33 shorter events, 0.1 us)
Async XLA Ops:
  1.4 1.0 copy-start.2
  2.4 0.9 copy-start.7
  3.3 0.9 copy-start.9
  4.2 0.9 copy-start.16
  5.1 0.7 copy-start.21
  5.8 0.7 copy-start.22
  6.5 15.7 %copy-start.3 = (bf16[4,512,128]{2,1,0:T(8,128)(2,1)S(1)}, bf16[4,512,128]{2,1,0:T(8,128)(2,1)}, u32[]{:S(2)}) copy-start(bf16[4,512,128]{2,1,0:T(8,128)(2,1)} %w_ref.5) | copy-start | bytes 1572868
  7.9 0.7 copy-start.14
  8.6 0.7 copy-start.19
  9.2 28.0 %all-to-all-start = ((bf16[64,24,128]{2,1,0:T(8,128)(2,1)}), bf16[64,24,128]{2,1,0:T(8,128)(2,1)S(1)}, u32[]{:S(2)}, u32[]{:S(2)}) async-start(bf16[64,24,128]{2,1,0:T(8,128)(2,1)} %bitcast.3), calls=%async_computation | async-start | bytes 786432 | tf_op jit(solution)/shard_map/all_to_all | solution.py:288
  22.2 1.6 %copy-start = (bf16[1,2048,512]{2,1,0:T(8,128)(2,1)S(1)}, bf16[1,2048,512]{2,1,0:T(8,128)(2,1)}, u32[]{:S(2)}) copy-start(bf16[1,2048,512]{2,1,0:T(8,128)(2,1)} %param.12) | copy-start | bytes 6291460
  25.9 1.0 copy-start.23
  26.9 0.8 copy-start.25
  27.7 0.8 copy-start.27
  28.5 0.8 copy-start.29
  29.3 0.8 copy-start.31
  37.3 0.7 copy-start.11
  38.0 1.0 copy-start.12
  39.0 1.2 copy-start.24
  40.2 1.0 copy-start.26
  41.3 1.0 copy-start.28
  42.3 1.0 copy-start.30
  43.4 1.0 copy-start.32
  44.4 34.2 %copy-start.8 = (bf16[128,512]{1,0:T(8,128)(2,1)S(1)}, bf16[128,512]{1,0:T(8,128)(2,1)}, u32[]{:S(2)}) copy-start(bf16[128,512]{1,0:T(8,128)(2,1)} %x_ref.3) | copy-start | bytes 393220
  44.4 37.9 %copy-start.1 = (bf16[1,2048,512]{2,1,0:T(8,128)(2,1)S(1)}, bf16[1,2048,512]{2,1,0:T(8,128)(2,1)}, u32[]{:S(2)}) copy-start(bf16[1,2048,512]{2,1,0:T(8,128)(2,1)} %param.12) | copy-start | bytes 6291460
  58.1 1.0 copy-start.4
  59.1 0.7 copy-start.13
  59.8 18.8 %all-to-all-start.1 = ((bf16[64,16,128]{2,1,0:T(8,128)(2,1)}), bf16[64,16,128]{2,1,0:T(8,128)(2,1)S(1)}, u32[]{:S(2)}, u32[]{:S(2)}) async-start(bf16[64,16,128]{2,1,0:T(8,128)(2,1)} %bitcast.20), calls=%async_computation.1 | async-start | bytes 524288 | tf_op jit(solution)/shard_map/all_to_all | solution.py:288
  78.6 3.8 %copy-start.5 = (bf16[2048,256]{1,0:T(8,128)(2,1)S(1)}, bf16[2048,256]{1,0:T(8,128)(2,1)}, u32[]{:S(2)}) copy-start(bf16[2048,256]{1,0:T(8,128)(2,1)} %copy-done.4) | copy-start | bytes 3145732
  78.6 1.0 copy-start.10
  79.6 0.9 copy-start.15
  80.5 0.9 copy-start.20
  82.0 3.2 %copy-start.17 = (bf16[128,512]{1,0:T(8,128)(2,1)}, bf16[128,512]{1,0:T(8,128)(2,1)S(1)}, u32[]{:S(2)}) copy-start(bf16[128,512]{1,0:T(8,128)(2,1)S(1)} %get-tuple-element.31) | copy-start | bytes 393220
  82.0 3.1 %collective-permute-start.4 = (bf16[768,128]{1,0:T(8,128)(2,1)S(1)}, bf16[768,128]{1,0:T(8,128)(2,1)S(1)}, u32[]{:S(2)}, u32[]{:S(2)}) collective-permute-start(bf16[768,128]{1,0:T(8,128)(2,1)S(1)} %get-tuple-element.37), channel_id=1, source_target_pairs={{0,4},{4,0},{8,12},{12,8},{16,20},{20,16},{24,28},{28,24},{32,36},... | collective-permute-start | bytes 589832 | tf_op jit(solution)/shard_map/ppermute | solution.py:284
  83.6 43.8 %copy-start.6 = (bf16[2048,256]{1,0:T(8,128)(2,1)S(1)}, bf16[2048,256]{1,0:T(8,128)(2,1)}, u32[]{:S(2)}) copy-start(bf16[2048,256]{1,0:T(8,128)(2,1)} %copy-done.4) | copy-start | bytes 3145732
  83.7 1.4 %collective-permute-start.3 = (bf16[512,128]{1,0:T(8,128)(2,1)S(1)}, bf16[512,128]{1,0:T(8,128)(2,1)S(1)}, u32[]{:S(2)}, u32[]{:S(2)}) collective-permute-start(bf16[512,128]{1,0:T(8,128)(2,1)S(1)} %get-tuple-element.35), channel_id=1, source_target_pairs={{0,4},{4,0},{8,12},{12,8},{16,20},{20,16},{24,28},{28,24},{32,36},... | collective-permute-start | bytes 393224 | tf_op jit(solution)/shard_map/ppermute | solution.py:284
  85.2 37.2 %copy-start.18 = (bf16[128,512]{1,0:T(8,128)(2,1)S(1)}, bf16[128,512]{1,0:T(8,128)(2,1)}, u32[]{:S(2)}) copy-start(bf16[128,512]{1,0:T(8,128)(2,1)} %copy-done.17) | copy-start | bytes 393220
  102.9 15.8 %all-to-all-start.3 = ((bf16[32,40,128]{2,1,0:T(8,128)(2,1)}), bf16[32,40,128]{2,1,0:T(8,128)(2,1)S(1)}, u32[]{:S(2)}, u32[]{:S(2)}) async-start(bf16[32,40,128]{2,1,0:T(8,128)(2,1)} %bitcast.10), calls=%async_computation.3 | async-start | bytes 655360 | tf_op jit(solution)/shard_map/all_to_all | solution.py:293
  118.7 11.1 %collective-permute-start.5 = (bf16[1280,128]{1,0:T(8,128)(2,1)S(1)}, bf16[1280,128]{1,0:T(8,128)(2,1)S(1)}, u32[]{:S(2)}, u32[]{:S(2)}) collective-permute-start(bf16[1280,128]{1,0:T(8,128)(2,1)S(1)} %bitcast.14), channel_id=1, source_target_pairs={{0,4},{4,0},{8,12},{12,8},{16,20},{20,16},{24,28},{28,24},{32,36},... | collective-permute-start | bytes 983048 | tf_op jit(solution)/shard_map/ppermute | solution.py:284
  122.4 6.2 %collective-permute-start = (bf16[32,512]{1,0:T(8,128)(2,1)S(1)}, bf16[32,512]{1,0:T(8,128)(2,1)S(1)}, u32[]{:S(2)}, u32[]{:S(2)}) collective-permute-start(bf16[32,512]{1,0:T(8,128)(2,1)S(1)} %get-tuple-element.40), channel_id=1, source_target_pairs={{0,1},{1,2},{2,3},{3,0},{4,5},{5,6},{6,7},{7,4},{8,9},{9,10},{10,1... | collective-permute-start | bytes 98312 | tf_op jit(solution)/shard_map/ppermute | solution.py:357
  123.8 4.8 %collective-permute-start.1 = (bf16[32,512]{1,0:T(8,128)(2,1)S(1)}, bf16[32,512]{1,0:T(8,128)(2,1)S(1)}, u32[]{:S(2)}, u32[]{:S(2)}) collective-permute-start(bf16[32,512]{1,0:T(8,128)(2,1)S(1)} %get-tuple-element.42), channel_id=1, source_target_pairs={{0,2},{1,3},{2,0},{3,1},{4,6},{5,7},{6,4},{7,5},{8,10},{9,11},{10,... | collective-permute-start | bytes 98312 | tf_op jit(solution)/shard_map/ppermute | solution.py:357
  126.4 2.8 %collective-permute-start.2 = (bf16[32,512]{1,0:T(8,128)(2,1)S(1)}, bf16[32,512]{1,0:T(8,128)(2,1)S(1)}, u32[]{:S(2)}, u32[]{:S(2)}) collective-permute-start(bf16[32,512]{1,0:T(8,128)(2,1)S(1)} %get-tuple-element.41), channel_id=1, source_target_pairs={{0,3},{1,0},{2,1},{3,2},{4,7},{5,4},{6,5},{7,6},{8,11},{9,8},{10,9... | collective-permute-start | bytes 98312 | tf_op jit(solution)/shard_map/ppermute | solution.py:357

commit v2 on v1

--- a/solution.py
+++ b/solution.py
@@ -8,12 +8,12 @@
 DH = 64
 EPSILON = 1e-05
 CAP = 8
-BLOCK = 256
+BLOCK = 1024
 F32 = jnp.float32
 BF16 = jnp.bfloat16
-VMEM = pl.BlockSpec(memory_space=pltpu.VMEM)
+ANY = pl.BlockSpec(memory_space=pl.ANY)
 SMEM = pl.BlockSpec(memory_space=pltpu.SMEM)
-PARAMS = pltpu.CompilerParams(vmem_limit_bytes=48 * 1024 * 1024)
+PARAMS = pltpu.CompilerParams(vmem_limit_bytes=62 * 1024 * 1024)
 
 
 def nn(a, b):
@@ -48,68 +48,72 @@
     return joined.reshape(count * 8 * len(parts), parts[0].shape[1])
 
 
-def pre_kernel(x_ref, hist_ref, len_ref, owner_ref, w_ref, wo_ref, gy_ref, send_ref, aux_ref, place_ref):
-    rows = x_ref.shape[0]
-    owners = owner_ref.shape[1]
-    x = x_ref[...]
-    queries, slope_q = silu_and_slope(nn(x, w_ref[0]))
-    gates, slope_g = silu_and_slope(nn(x, w_ref[1]))
-    cot = nt(gy_ref[...], wo_ref[...]).astype(BF16).astype(F32)
-    gates = gates.astype(BF16).astype(F32)
-    aux_ref[0] = slope_q
-    aux_ref[1] = slope_g
-    aux_ref[2] = gates
-    aux_ref[3] = cot
-    named = hist_ref[...] == iota((rows, owners), 1)
-    target = jnp.sum(jnp.where(named, owner_ref[...].astype(F32), 0.0), axis=1, keepdims=True)
-    target = jnp.transpose(jnp.broadcast_to(target, (rows, rows)))
-    hit = target[:owners] == iota((owners, rows), 0).astype(F32)
-    hit = jnp.where(hit, 1.0, 0.0)
+def pre_kernel(x_in, hist_in, len_in, owner_in, w_in, wo_in, gy_in, send_out, aux_out, place_out):
+    hist = hist_in.get()[...]
+    owner = owner_in.get()[...]
+    rows, owners = hist.shape[1], owner.shape[1]
+    named = jnp.where(iota((owners, rows), 0) == hist, 1.0, 0.0).astype(BF16)
+    owner = jnp.broadcast_to(owner.astype(F32), (8, owners)).astype(BF16)
+    target = nn(owner, named)[:1]
+    hit = jnp.where(iota((owners, rows), 0).astype(F32) == target, 1.0, 0.0)
     earlier = jnp.where(iota((rows, rows), 0) < iota((rows, rows), 1), 1.0, 0.0)
     before = nn(hit.astype(BF16), earlier.astype(BF16))
     rank = jnp.sum(before * hit, axis=0, keepdims=True)
-    slot = target[:1] * float(CAP) + rank
+    slot = target * float(CAP) + rank
     slots = owners * CAP
     place = jnp.where(iota((slots, rows), 0).astype(F32) == slot, 1.0, 0.0).astype(BF16)
-    place_ref[...] = place
-    length = len_ref[...].astype(F32)
+    place_out.buffer[...] = place
+    place_out.send()
+    length = len_in.get()[...].astype(F32)
     high = jnp.floor(length * (1.0 / 256.0))
     low = length - 256.0 * high
-    digits = jnp.where(iota((rows, rows), 0) == 0, high, low)
-    digits = jnp.transpose(digits)
+    digits = jnp.transpose(jnp.where(iota((rows, rows), 0) == 0, high, low))
+    x, w_ref = x_in.get()[...], w_in.get()
+    queries, slope_q = silu_and_slope(nn(x, w_ref[0]))
+    gates, slope_g = silu_and_slope(nn(x, w_ref[1]))
+    cot = nt(gy_in.get()[...], wo_in.get()[...]).astype(BF16).astype(F32)
+    gates = gates.astype(BF16).astype(F32)
     payload = jnp.concatenate(
         [queries.astype(BF16), (cot * gates).astype(BF16), digits.astype(BF16)], axis=1
     )
     packed = nn(place, payload)
     width = queries.shape[1]
-    send_ref[...] = spread(
+    send_out.buffer[...] = spread(
         [packed[:, :width], packed[:, width : 2 * width], packed[:, 2 * width :]]
     ).astype(BF16)
-
-
-def project_kernel(ev_ref, w_ref, k_ref, v_ref, kt_ref, vt_ref, slope_ref):
+    send_out.send()
+    aux_out.buffer[0] = slope_q
+    aux_out.buffer[1] = slope_g
+    aux_out.buffer[2] = gates
+    aux_out.buffer[3] = cot
+
+
+def project_kernel(ev_in, w_in, k_out, v_out, kt_out, vt_out, slope_out):
+    ev_ref, w_ref = ev_in.get(), w_in.get()
+
     def step(b, carry):
         at = pl.ds(pl.multiple_of(b * 512, 512), 512)
         ev = ev_ref[at, :]
         keys, slope = silu_and_slope(nn(ev, w_ref[2]))
         values = nn(ev, w_ref[3])
-        k_ref[at, :] = keys.astype(BF16)
-        v_ref[at, :] = values.astype(BF16)
-        slope_ref[at, :] = slope
-        kt_ref[:, at] = jnp.transpose(keys.astype(BF16))
-        vt_ref[:, at] = jnp.transpose(values.astype(BF16))
+        k_out.buffer[at, :] = keys.astype(BF16)
+        v_out.buffer[at, :] = values.astype(BF16)
+        slope_out.buffer[at, :] = slope
+        kt_out.buffer[:, at] = jnp.transpose(keys.astype(BF16))
+        vt_out.buffer[:, at] = jnp.transpose(values.astype(BF16))
         return carry
 
     lax.fori_loop(0, ev_ref.shape[0] // 512, step, 0)
 
 
 def attend_kernel(
-    recv_ref, k_ref, v_ref, kt_ref, vt_ref, slope_ref,
-    back_ref, gkv_ref, term_ref,
+    recv_in, k_in, vt_in, v_in, kt_in, slope_in,
+    back_out, gkv_out, term_out,
     w_scr, s_scr, att_scr, dq_scr,
 ):
-    slots = recv_ref.shape[0] // 3
-    events, width = k_ref.shape
+    gkv_ref, term_ref = gkv_out.buffer, term_out.buffer
+    recv_ref = recv_in.get()
+    slots, width = recv_ref.shape[0] // 3, recv_ref.shape[1]
     heads = width // DH
     got = recv_ref[...].astype(F32).reshape(slots // CAP, 3 * CAP, width)
     q = got[:, :CAP].reshape(slots, width)
@@ -124,6 +128,8 @@
     zero = jnp.zeros((), BF16)
     qt_of = [jnp.where(head_row == h, qt_half, zero) for h in range(heads)]
     att_scr[...] = jnp.zeros_like(att_scr)
+    k_ref, vt_ref = k_in.get(), vt_in.get()
+    events = k_ref.shape[0]
 
     def forward(b, carry):
         start = pl.multiple_of(b * BLOCK, BLOCK)
@@ -155,6 +161,7 @@
     d_of = [jnp.where(head_col == h, d_att, zero) for h in range(heads)]
     q_of = [jnp.where(head_col == h, q_bf, zero) for h in range(heads)]
     dq_scr[...] = jnp.zeros_like(dq_scr)
+    v_ref, kt_ref, slope_ref = v_in.get(), kt_in.get(), slope_in.get()
 
     def backward(b, carry):
         at = pl.ds(pl.multiple_of(b * BLOCK, BLOCK), BLOCK)
@@ -174,29 +181,35 @@
 
     lax.fori_loop(0, events // BLOCK, backward, 0)
     d_query = jnp.transpose(dq_scr[...] * (0.5 * DH ** (-0.5)))
-    back_ref[...] = spread([d_query, normed]).astype(BF16)
-
-
-def history_grads_kernel(core_ref, ev_ref, term_ref, gkv_ref, mine_ref, other_ref, scr):
-    width = term_ref.shape[1]
-    gk = tn(ev_ref[...], term_ref[...])
-    gv = tn(ev_ref[...], gkv_ref[:, width:])
-    rows = spread([gk, gv]).astype(BF16)
+    back_out.buffer[...] = spread([d_query, normed]).astype(BF16)
+
+
+def split_halves(core, rows, scr, mine_out, other_out):
     half = rows.shape[0] // 2
     scr[0] = rows[:half]
     scr[1] = rows[half:]
-    core = core_ref[0]
-    mine_ref[...] = scr[core]
-    other_ref[...] = scr[1 - core]
-
-
-def post_kernel(core_ref, back_ref, place_ref, aux_ref, x_ref, w_ref, gy_ref, mine_ref, other_ref, gx_ref, scr):
-    slots, rows = place_ref.shape
+    other_out.buffer[...] = scr[1 - core]
+    other_out.send()
+    mine_out.buffer[...] = scr[core]
+
+
+def history_grads_kernel(core_ref, ev_in, term_in, gkv_in, mine_out, other_out, scr):
+    term_ref = term_in.get()
+    width = term_ref.shape[1]
+    gv = tn(ev_in.get()[...], gkv_in.get()[:, width:])
+    gk = tn(ev_in.get()[...], term_ref[...])
+    split_halves(core_ref[0], spread([gk, gv]).astype(BF16), scr, mine_out, other_out)
+
+
+def post_kernel(core_ref, back_in, place_in, aux_in, x_in, w_in, gy_in, mine_out, other_out, gx_out, scr):
+    place = place_in.get()[...]
+    back_ref, aux_ref, w_ref = back_in.get(), aux_in.get(), w_in.get()
+    slots = place.shape[0]
     width = back_ref.shape[1]
     got = back_ref[...].astype(F32).reshape(slots // CAP, 2 * CAP, width)
     d_query = got[:, :CAP].reshape(slots, width).astype(BF16)
     normed = got[:, CAP:].reshape(slots, width).astype(BF16)
-    both = tn(place_ref[...], jnp.concatenate([d_query, normed], axis=1))
+    both = tn(place, jnp.concatenate([d_query, normed], axis=1))
     d_query = both[:, :width]
     normed = both[:, width:]
     gates = aux_ref[2]
@@ -204,44 +217,42 @@
     d_gate = (aux_ref[3] * normed).astype(BF16).astype(F32)
     q_term = (d_query * aux_ref[0]).astype(BF16)
     g_term = (d_gate * aux_ref[1]).astype(BF16)
-    gx_ref[...] = (nt(q_term, w_ref[0]) + nt(g_term, w_ref[1])).astype(BF16)
-    x = x_ref[...]
+    gx_out.buffer[...] = (nt(q_term, w_ref[0]) + nt(g_term, w_ref[1])).astype(BF16)
+    gx_out.send()
+    x = x_in.get()[...]
     gq = tn(x, q_term)
     gg = tn(x, g_term)
-    go = tn(gated, gy_ref[...])
+    go = tn(gated, gy_in.get()[...])
     go = jnp.concatenate([go[:, i * width : (i + 1) * width] for i in range(go.shape[1] // width)], axis=0)
-    out = spread([gq, gg, go]).astype(BF16)
-    half = out.shape[0] // 2
-    scr[0] = out[:half]
-    scr[1] = out[half:]
-    core = core_ref[0]
-    mine_ref[...] = scr[core]
-    other_ref[...] = scr[1 - core]
-
-
-def pair_kernel(a_ref, b_ref, c_ref, d_ref, out_ref):
-    width = a_ref.shape[1]
-    first = a_ref[...].astype(F32) + b_ref[...].astype(F32)
-    second = c_ref[...].astype(F32) + d_ref[...].astype(F32)
+    split_halves(core_ref[0], spread([gq, gg, go]).astype(BF16), scr, mine_out, other_out)
+
+
+def pair_kernel(a_in, b_in, c_in, d_in, out):
+    width = a_in.buffer.shape[1]
+    first = a_in.get()[...].astype(F32) + b_in.get()[...].astype(F32)
+    second = c_in.get()[...].astype(F32) + d_in.get()[...].astype(F32)
     chunks = first.shape[0] // 16
     joined = jnp.concatenate(
         [first.reshape(chunks, 16, width), second.reshape(chunks, 24, width)], axis=1
     )
-    out_ref[...] = joined.reshape(chunks * 40, width).astype(BF16)
-
-
-def sum_kernel(factor, in_ref, out_ref):
-    chunks = in_ref.shape[0] // 40
-    total = jnp.sum(in_ref[...].astype(F32).reshape(chunks, 40, in_ref.shape[1]), axis=0)
+    out.buffer[...] = joined.reshape(chunks * 40, width).astype(BF16)
+
+
+def sum_kernel(factor, rows_in, out):
+    got = rows_in.get()[...]
+    chunks = got.shape[0] // 40
+    total = jnp.sum(got.astype(F32).reshape(chunks, 40, got.shape[1]), axis=0)
     total = total * factor
-    out_ref[...] = jnp.broadcast_to(total[None], (chunks, 40, total.shape[1])).reshape(out_ref.shape).astype(BF16)
-
-
-def unfold_kernel(core_ref, mine_ref, other_ref, win_ref, wout_ref, scr):
-    width = mine_ref.shape[1]
+    shape = out.buffer.shape
+    out.buffer[...] = jnp.broadcast_to(total[None], (chunks, 40, shape[1])).reshape(shape).astype(BF16)
+
+
+def unfold_kernel(core_ref, mine_in, other_in, win_out, wout_out, scr):
+    win_ref, wout_ref = win_out.buffer, wout_out.buffer
+    width = mine_in.buffer.shape[1]
     core = core_ref[0]
-    for ref, which in ((mine_ref, core), (other_ref, 1 - core)):
-        got = ref[...].astype(F32)
+    for source, which in ((mine_in, core), (other_in, 1 - core)):
+        got = source.get()[...].astype(F32)
         chunks = got.shape[0] // 40
         got = got.reshape(chunks, 5, 8, width)
         size = chunks * 8
@@ -254,16 +265,64 @@
         wout_ref[:, i * width : (i + 1) * width] = scr[i * rows : (i + 1) * rows, :]
 
 
-def call(kernel, outs, ins, specs=None, scratch=(), flops=0, moved=0):
+class Load:
+    def __init__(self, source, buffer, sem):
+        self.buffer = buffer
+        self.copy = pltpu.make_async_copy(source, buffer, sem)
+        self.copy.start()
+        self.done = False
+
+    def get(self):
+        if not self.done:
+            self.copy.wait()
+            self.done = True
+        return self.buffer
+
+
+class Store:
+    def __init__(self, target, buffer, sem):
+        self.buffer = buffer
+        self.copy = pltpu.make_async_copy(buffer, target, sem)
+        self.started = False
+
+    def send(self):
+        if not self.started:
+            self.copy.start()
+            self.started = True
+
+
+def call(kernel, outs, ins, scalars=(), scratch=(), flops=0, moved=0):
+    ns, ni, no = len(scalars), len(ins), len(outs)
+
+    def body(*refs):
+        given, refs = refs[:ns], refs[ns:]
+        sources, refs = refs[:ni], refs[ni:]
+        targets, refs = refs[:no], refs[no:]
+        in_bufs, refs = refs[:ni], refs[ni:]
+        out_bufs, refs = refs[:no], refs[no:]
+        in_sems, out_sems, extra = refs[0], refs[1], refs[2:]
+        loads = [Load(r, b, in_sems.at[i]) for i, (r, b) in enumerate(zip(sources, in_bufs))]
+        stores = [Store(r, b, out_sems.at[i]) for i, (r, b) in enumerate(zip(targets, out_bufs))]
+        kernel(*given, *loads, *stores, *extra)
+        for load in loads:
+            load.get()
+        for store in stores:
+            store.send()
+        for store in stores:
+            store.copy.wait()
+
     return pl.pallas_call(
-        kernel,
+        body,
         out_shape=[jax.ShapeDtypeStruct(s, d) for s, d in outs],
-        in_specs=specs or [VMEM] * len(ins),
-        out_specs=[VMEM] * len(outs),
-        scratch_shapes=list(scratch),
+        in_specs=[SMEM] * ns + [ANY] * ni,
+        out_specs=[ANY] * no,
+        scratch_shapes=[pltpu.VMEM(a.shape, a.dtype) for a in ins]
+        + [pltpu.VMEM(s, d) for s, d in outs]
+        + [pltpu.SemaphoreType.DMA((ni,)), pltpu.SemaphoreType.DMA((no,))]
+        + list(scratch),
         compiler_params=PARAMS,
         cost_estimate=pl.CostEstimate(flops=flops, bytes_accessed=moved, transcendentals=0),
-    )(*ins)
+    )(*scalars, *ins)
 
 
 def on_device(imp_x, imp_hist, imp_len, owner_map, hist_x, w_in, w_out, grad_y):
@@ -296,7 +355,7 @@
     send, aux, place = call(
         pre_kernel,
         [((3 * slots, width), BF16), ((4, rows, width), F32), ((slots, rows), BF16)],
-        (imp_x, imp_hist, imp_len.reshape(1, rows), owner_map.reshape(1, owners), w_in, w_out, grad_y),
+        (imp_x, imp_hist.reshape(1, rows), imp_len.reshape(1, rows), owner_map.reshape(1, owners), w_in, w_out, grad_y),
         flops=2 * rows * depth * width * 3,
         moved=1 << 20,
     )
@@ -311,7 +370,7 @@
     back, gkv, term = call(
         attend_kernel,
         [((2 * slots, width), BF16), ((events, 2 * width), BF16), ((events, width), BF16)],
-        (recv, keys, values, keys_t, values_t, key_slope),
+        (recv, keys, values_t, values, keys_t, key_slope),
         scratch=[
             pltpu.VMEM((width // DH, events, slots), BF16),
             pltpu.VMEM((width // DH, events, slots), BF16),
@@ -326,19 +385,20 @@
     kv_mine, kv_other = call(
         history_grads_kernel,
         [((half, width), BF16)] * 2,
-        (core, hist, term, gkv),
-        specs=[SMEM, VMEM, VMEM, VMEM],
+        (hist, term, gkv),
+        (core,),
         scratch=[pltpu.VMEM((2, half, width), BF16)],
         flops=4 * events * depth * width,
         moved=4 << 20,
     )
     kv_other = swap(kv_other)
+    back, kv_mine, kv_other = lax.optimization_barrier((back, kv_mine, kv_other))
     half = depth * 3 // 2
     mine, other, gx = call(
         post_kernel,
         [((half, width), BF16)] * 2 + [((rows, depth), BF16)],
-        (core, back, place, aux, imp_x, w_in, grad_y),
-        specs=[SMEM] + [VMEM] * 6,
+        (back, place, aux, imp_x, w_in, grad_y),
+        (core,),
         scratch=[pltpu.VMEM((2, half, width), BF16)],
         flops=2 * rows * depth * width * 5,
         moved=2 << 20,
@@ -349,19 +409,20 @@
     )
     plane = lax.axis_index("mp")
     share = rows // planes
-    own = lax.dynamic_slice_in_dim(gx, plane * share, share, 0)
-    total = own.astype(F32)
+    parts = []
     for step in range(1, planes):
-        target = (plane + step) % planes
-        part = lax.dynamic_slice_in_dim(gx, target * share, share, 0)
-        part = lax.ppermute(part, "mp", [(i, (i + step) % planes) for i in range(planes)])
+        part = lax.dynamic_slice_in_dim(gx, (plane + step) % planes * share, share, 0)
+        parts.append(lax.ppermute(part, "mp", [(i, (i + step) % planes) for i in range(planes)]))
+    factor = (rows * owners) ** (-0.5)
+    summed, *parts = lax.optimization_barrier((exchange_core(summed), *parts))
+    total = lax.dynamic_slice_in_dim(gx, plane * share, share, 0).astype(F32)
+    for part in parts:
         total = total + part.astype(F32)
     grad_x = total.astype(BF16)
-    factor = (rows * owners) ** (-0.5)
     (piece,) = call(
         lambda i, o: sum_kernel(factor, i, o),
         [((chips * 40, width), BF16)],
-        (exchange_core(summed),),
+        (summed,),
         moved=1 << 20,
     )
     mine = exchange_core(piece)
@@ -369,8 +430,8 @@
     grad_w_in, grad_w_out = call(
         unfold_kernel,
         [((4, depth, width), F32), ((width, depth), F32)],
-        (core, mine, other),
-        specs=[SMEM, VMEM, VMEM],
+        (mine, other),
+        (core,),
         scratch=[pltpu.VMEM((depth, width), F32)],
         moved=3 << 20,
     )

time: 132 us -> 116 us (0.88)
  local copies, waits for them, and re-layouts: 25.7 us -> 5.49 us
  Pallas kernels: 21 us -> 32.4 us
  waiting for transfers between devices: 33.2 us -> 26.4 us
  blocking collectives: 16.9 us -> 15.5 us
    unnamed x67 -> x16, local copies, waits for them, and re-layouts: 24.6 us -> 3.59 us
    pallas_call x8, Pallas kernels: 21 us -> 32.4 us  [call(): pl.pallas_call(body, out_shape=[jax.ShapeDtypeStruct(s, d) for s, d in ou...]
    all_to_all x1, waiting for transfers between devices: 11.2 us -> 4.86 us  [exchange_core(): a = lax.all_to_all(a, 'dp', 0, 0, axis_index_groups=same_core, tiled=True)]
    all_to_all x2, waiting for transfers between devices: 20.3 us -> 17 us  [exchange(): a = lax.all_to_all(a, 'dp', 0, 0, tiled=True)]
    ppermute x3, waiting for transfers between devices: 1.1 us -> 2.59 us  [swap(): return lax.ppermute(a, 'dp', pairs)]
    ppermute x3, waiting for transfers between devices: 0.6 us -> 1.99 us  [on_device(): lax.ppermute(part, 'mp', [(i, (i + step) % planes) for i in range(planes)])]
    all_to_all x1, blocking collectives: 16.9 us -> 15.5 us  [exchange_core(): a = lax.all_to_all(a, 'dp', 0, 0, axis_index_groups=same_core, tiled=True)]
  transfers between devices with their start and end apart: 9 -> 9, of which waited for: 5 -> 7; matrix products, arithmetic and copies ran while one was open for 1% -> 3% of each run, Pallas kernels for 3% -> 8%
where the time goes in v2:
time: 116 us; the launch traced here: 115 us
  starting transfers between devices  33.1 us (29%)
  Pallas kernels  32.4 us (28%)
  waiting for transfers between devices  26.4 us (23%)
  blocking collectives  15.5 us (13%)
  local copies, waits for them, and re-layouts  5.49 us (5%)
  other arithmetic  1.39 us (1%)
    pallas_call x8, Pallas kernels, call(): pl.pallas_call(body, out_shape=[jax.ShapeDtypeStruct(s, d) for s, d in ou...  32.4 us
    all_to_all x2, starting transfers between devices, exchange(): a = lax.all_to_all(a, 'dp', 0, 0, tiled=True)  18.6 us
    all_to_all x2, waiting for transfers between devices, exchange(): a = lax.all_to_all(a, 'dp', 0, 0, tiled=True)  17 us
    all_to_all x1, blocking collectives, exchange_core(): a = lax.all_to_all(a, 'dp', 0, 0, axis_index_groups=same_core, tiled=True)  15.5 us
    ppermute x3, starting transfers between devices, swap(): return lax.ppermute(a, 'dp', pairs)  5.57 us
    ppermute x3, starting transfers between devices, on_device(): lax.ppermute(part, 'mp', [(i, (i + step) % planes) for i in range(planes)])  5.04 us
    all_to_all x1, waiting for transfers between devices, exchange_core(): a = lax.all_to_all(a, 'dp', 0, 0, axis_index_groups=same_core, tiled=True)  4.86 us
    all_to_all x1, starting transfers between devices, exchange_core(): a = lax.all_to_all(a, 'dp', 0, 0, axis_index_groups=same_core, tiled=True)  3.91 us
  transfers between devices with their start and end apart: 9, of which 7 were waited for; matrix products, arithmetic and copies ran while one was open for 3% of the time, Pallas kernels for 8%

profile of v2, /device:TPU:1, one launch (start us, length us, event | category | flops | bytes accessed | tf_op | source)
XLA Modules:
  0.0 115.2 jit_solution(3156895177531144307)
XLA Ops:
  0.6 2.8 %shard_map.111 = (bf16[1536,128]{1,0:T(8,128)(2,1)}, f32[4,128,128]{2,1,0:T(8,128)}, bf16[512,128]{1,0:T(8,128)(2,1)}) custom-call(bf16[128,512]{1,0:T(8,128)(2,1)} %refs_4_.3, s32[1,128]{1,0:T(1,128)} %bitcast.24, s32[1,128]{1,0:T(1,128)} %bitcast.25, s32[1,64]{1,0:T(1,128)} %bitcast.26, bf16[4,512,128]{2,1,0:T(8,128)(2,1)} %refs_5_.3, ...), custom_call_target="tpu_custom_call" | custom-call | flops 50331648 | bytes 1048576 | tf_op jit(solution)/shard_map/pallas_call | solution.py:314
  3.4 13.0 %all-to-all-start = ((bf16[64,24,128]{2,1,0:T(8,128)(2,1)}), bf16[64,24,128]{2,1,0:T(8,128)(2,1)S(1)}, u32[]{:S(2)}, u32[]{:S(2)}) async-start(bf16[64,24,128]{2,1,0:T(8,128)(2,1)} %bitcast.22), calls=%async_computation | async-start | bytes 786432 | tf_op jit(solution)/shard_map/all_to_all | solution.py:347
  16.4 5.4 %shard_map.112 = (bf16[2048,128]{1,0:T(8,128)(2,1)}, bf16[2048,128]{1,0:T(8,128)(2,1)}, bf16[128,2048]{1,0:T(8,128)(2,1)}, bf16[128,2048]{1,0:T(8,128)(2,1)}, f32[2048,128]{1,0:T(8,128)}) custom-call(bf16[2048,512]{1,0:T(8,128)(2,1)} %bitcast.13, bf16[4,512,128]{2,1,0:T(8,128)(2,1)} %refs_5_.3), custom_call_target="tpu_custom_call" | custom-call | flops 536870912 | bytes 5242880 | tf_op jit(solution)/shard_map/pallas_call | solution.py:314
  21.9 9.6 %all-to-all-done = bf16[64,24,128]{2,1,0:T(8,128)(2,1)S(1)} async-done(((bf16[64,24,128]{2,1,0:T(8,128)(2,1)}), bf16[64,24,128]{2,1,0:T(8,128)(2,1)S(1)}, u32[]{:S(2)}, u32[]{:S(2)}) %all-to-all-start) | async-done | bytes 393248 | tf_op jit(solution)/shard_map/all_to_all | solution.py:347
  31.5 0.0 copy-start.4
  31.5 0.8 copy-done.4
  32.3 11.0 %shard_map.113 = (bf16[1024,128]{1,0:T(8,128)(2,1)}, bf16[2048,256]{1,0:T(8,128)(2,1)}, bf16[2048,128]{1,0:T(8,128)(2,1)}) custom-call(bf16[1536,128]{1,0:T(8,128)(2,1)} %bitcast.21, bf16[2048,128]{1,0:T(8,128)(2,1)} %get-tuple-element.30.refs_1_, bf16[128,2048]{1,0:T(8,128)(2,1)} %get-tuple-element.31.refs_2_, bf16[2048,128]{1,0:T(8,128)(2,1)} %get-tuple-element.32.refs_3_, ...), custom_call_target="tpu_custom_call" | custom-call | flops 1610612736 | bytes 4194304 | tf_op jit(solution)/shard_map/pallas_call | solution.py:314
  43.3 5.6 %all-to-all-start.1 = ((bf16[64,16,128]{2,1,0:T(8,128)(2,1)}), bf16[64,16,128]{2,1,0:T(8,128)(2,1)S(1)}, u32[]{:S(2)}, u32[]{:S(2)}) async-start(bf16[64,16,128]{2,1,0:T(8,128)(2,1)} %bitcast.23), calls=%async_computation.1 | async-start | bytes 524288 | tf_op jit(solution)/shard_map/all_to_all | solution.py:347
  48.9 4.1 %shard_map.114 = (bf16[512,128]{1,0:T(8,128)(2,1)}, bf16[512,128]{1,0:T(8,128)(2,1)}) custom-call(s32[1]{0:T(128)} %bitcast.refs_0_, bf16[2048,512]{1,0:T(8,128)(2,1)} %bitcast.14, bf16[2048,128]{1,0:T(8,128)(2,1)} %get-tuple-element.36.refs_2_, bf16[2048,256]{1,0:T(8,128)(2,1)} %get-tuple-element.37.refs_3_), custom_call_target="tpu_custom_call" | custom-call | flops 536870912 | bytes 4194304 | tf_op jit(solution)/shard_map/pallas_call | solution.py:314
  53.0 0.5 collective-permute-start
  53.5 1.2 %collective-permute-done.refs_1_ = bf16[512,128]{1,0:T(8,128)(2,1)S(1)} collective-permute-done((bf16[512,128]{1,0:T(8,128)(2,1)}, bf16[512,128]{1,0:T(8,128)(2,1)S(1)}, u32[]{:S(2)}, u32[]{:S(2)}) %collective-permute-start) | collective-permute-done | bytes 131104 | tf_op jit(solution)/shard_map/ppermute | solution.py:343
  54.7 0.0 copy-start.7
  54.7 7.3 %all-to-all-done.1 = bf16[64,16,128]{2,1,0:T(8,128)(2,1)S(1)} async-done(((bf16[64,16,128]{2,1,0:T(8,128)(2,1)}), bf16[64,16,128]{2,1,0:T(8,128)(2,1)S(1)}, u32[]{:S(2)}, u32[]{:S(2)}) %all-to-all-start.1) | async-done | bytes 262176 | tf_op jit(solution)/shard_map/all_to_all | solution.py:347
  62.1 0.0 copy-start.3
  62.1 0.7 copy-done.3
  62.8 0.0 copy-start
  62.8 3.2 %shard_map.115 = (bf16[768,128]{1,0:T(8,128)(2,1)}, bf16[768,128]{1,0:T(8,128)(2,1)}, bf16[128,512]{1,0:T(8,128)(2,1)}) custom-call(s32[1]{0:T(128)} %bitcast.refs_0_, bf16[1024,128]{1,0:T(8,128)(2,1)} %bitcast.20, bf16[512,128]{1,0:T(8,128)(2,1)} %get-tuple-element.41.refs_2_, f32[4,128,128]{2,1,0:T(8,128)} %get-tuple-element.42.refs_3_, ...), custom_call_target="tpu_custom_call" | custom-call | flops 83886080 | bytes 2097152 | tf_op jit(solution)/shard_map/pallas_call | solution.py:314
  66.0 0.3 collective-permute-start.1
  66.3 1.4 %collective-permute-done.1.refs_3_ = bf16[768,128]{1,0:T(8,128)(2,1)S(1)} collective-permute-done((bf16[768,128]{1,0:T(8,128)(2,1)}, bf16[768,128]{1,0:T(8,128)(2,1)S(1)}, u32[]{:S(2)}, u32[]{:S(2)}) %collective-permute-start.1) | collective-permute-done | bytes 196640 | tf_op jit(solution)/shard_map/ppermute | solution.py:343
  67.7 0.0 copy-start.6
  67.7 0.0 copy-done.7
  67.7 0.7 copy-done.6
  68.4 1.9 %shard_map.116 = bf16[1280,128]{1,0:T(8,128)(2,1)} custom-call(bf16[512,128]{1,0:T(8,128)(2,1)} %get-tuple-element.44.refs_0_, bf16[512,128]{1,0:T(8,128)(2,1)} %copy-done.7, bf16[768,128]{1,0:T(8,128)(2,1)} %get-tuple-element.46.refs_2_, bf16[768,128]{1,0:T(8,128)(2,1)} %copy-done.6), custom_call_target="tpu_custom_call" | custom-call | bytes 1048576 | tf_op jit(solution)/shard_map/pallas_call | solution.py:314
  70.4 3.9 %all-to-all-start.2 = ((bf16[32,40,128]{2,1,0:T(8,128)(2,1)}), bf16[32,40,128]{2,1,0:T(8,128)(2,1)S(1)}, u32[]{:S(2)}, u32[]{:S(2)}) async-start(bf16[32,40,128]{2,1,0:T(8,128)(2,1)} %bitcast.19), calls=%async_computation.2 | async-start | bytes 655360 | tf_op jit(solution)/shard_map/all_to_all | solution.py:352
  74.3 0.8 constant_dynamic-slice_fusion
  75.1 1.4 %collective-permute-start.2 = (bf16[32,512]{1,0:T(8,128)(2,1)S(1)}, bf16[32,512]{1,0:T(8,128)(2,1)S(1)}, u32[]{:S(2)}, u32[]{:S(2)}) collective-permute-start(bf16[32,512]{1,0:T(8,128)(2,1)S(1)} %get-tuple-element.56), channel_id=1, source_target_pairs={{0,1},{1,2},{2,3},{3,0},{4,5},{5,6},{6,7},{7,4},{8,9},{9,10},{10,1... | collective-permute-start | bytes 98312 | tf_op jit(solution)/shard_map/ppermute | solution.py:415
  76.5 2.6 %collective-permute-start.3 = (bf16[32,512]{1,0:T(8,128)(2,1)S(1)}, bf16[32,512]{1,0:T(8,128)(2,1)S(1)}, u32[]{:S(2)}, u32[]{:S(2)}) collective-permute-start(bf16[32,512]{1,0:T(8,128)(2,1)S(1)} %get-tuple-element.55), channel_id=1, source_target_pairs={{0,2},{1,3},{2,0},{3,1},{4,6},{5,7},{6,4},{7,5},{8,10},{9,11},{10,... | collective-permute-start | bytes 98312 | tf_op jit(solution)/shard_map/ppermute | solution.py:415
  79.1 1.1 collective-permute-start.4
  80.2 0.0 collective-permute-done.2
  80.2 0.9 collective-permute-done.3
  81.1 1.1 collective-permute-done.4
  82.2 4.9 %all-to-all-done.2 = bf16[32,40,128]{2,1,0:T(8,128)(2,1)S(1)} async-done(((bf16[32,40,128]{2,1,0:T(8,128)(2,1)}), bf16[32,40,128]{2,1,0:T(8,128)(2,1)S(1)}, u32[]{:S(2)}, u32[]{:S(2)}) %all-to-all-start.2) | async-done | bytes 327712 | tf_op jit(solution)/shard_map/all_to_all | solution.py:352
  87.0 0.0 copy-start.1
  87.0 0.7 copy-done.1
  87.8 1.8 %shard_map.117 = bf16[1280,128]{1,0:T(8,128)(2,1)} custom-call(bf16[1280,128]{1,0:T(8,128)(2,1)} %bitcast.15), custom_call_target="tpu_custom_call" | custom-call | bytes 1048576 | tf_op jit(solution)/shard_map/pallas_call | solution.py:314
  89.6 15.5 %all_to_all.20 = bf16[32,40,128]{2,1,0:T(8,128)(2,1)S(1)} all-to-all(bf16[32,40,128]{2,1,0:T(8,128)(2,1)} %bitcast.18), channel_id=1, replica_groups={{0,8,16,24,32,40,48,56,64,72,80,88,96,104,112,120,128,136,144,152,160,1..., dimensions={0} | all-to-all | bytes 655360 | tf_op jit(solution)/shard_map/all_to_all | solution.py:352
  105.1 0.0 copy-start.2
  105.1 4.7 %collective-permute-start.5 = (bf16[1280,128]{1,0:T(8,128)(2,1)S(1)}, bf16[1280,128]{1,0:T(8,128)(2,1)S(1)}, u32[]{:S(2)}, u32[]{:S(2)}) collective-permute-start(bf16[1280,128]{1,0:T(8,128)(2,1)S(1)} %bitcast.16), channel_id=1, source_target_pairs={{0,4},{4,0},{8,12},{12,8},{16,20},{20,16},{24,28},{28,24},{32,36},... | collective-permute-start | bytes 983048 | tf_op jit(solution)/shard_map/ppermute | solution.py:343
  109.8 0.0 copy-done
  109.8 1.1 reshape.57
  110.9 1.4 %add_convert_fusion = bf16[32,512]{1,0:T(8,128)(2,1)} fusion(bf16[32,512]{1,0:T(8,128)(2,1)S(1)} %collective-permute-done.4, bf16[32,512]{1,0:T(8,128)(2,1)S(1)} %collective-permute-done.3, bf16[32,512]{1,0:T(8,128)(2,1)S(1)} %collective-permute-done.2, bf16[128,512]{1,0:T(8,128)(2,1)} %get-tuple-element.43, s32[]{:T(128)S(6)} %select_n.32), kind=kLoop, calls=%fused_computation | loop fusion | flops 131072 | bytes 163844 | tf_op jit(solution)/shard_map/convert_element_type | solution.py:421
  112.3 0.0 collective-permute-done.5.refs_2_
  112.3 0.0 copy-done.2
  112.3 0.0 copy-start.5
  112.3 0.7 copy-done.5
  113.0 2.2 %shard_map.118 = (f32[4,512,128]{2,1,0:T(8,128)}, f32[128,512]{1,0:T(8,128)}) custom-call(s32[1]{0:T(128)} %bitcast.refs_0_, bf16[1280,128]{1,0:T(8,128)(2,1)} %bitcast.17, bf16[1280,128]{1,0:T(8,128)(2,1)} %copy-done.5), custom_call_target="tpu_custom_call" | custom-call | bytes 3145728 | tf_op jit(solution)/shard_map/pallas_call | solution.py:314
Async XLA Ops:
  3.4 28.1 %all-to-all-start = ((bf16[64,24,128]{2,1,0:T(8,128)(2,1)}), bf16[64,24,128]{2,1,0:T(8,128)(2,1)S(1)}, u32[]{:S(2)}, u32[]{:S(2)}) async-start(bf16[64,24,128]{2,1,0:T(8,128)(2,1)} %bitcast.22), calls=%async_computation | async-start | bytes 786432 | tf_op jit(solution)/shard_map/all_to_all | solution.py:347
  31.5 0.8 copy-start.4
  43.3 18.8 %all-to-all-start.1 = ((bf16[64,16,128]{2,1,0:T(8,128)(2,1)}), bf16[64,16,128]{2,1,0:T(8,128)(2,1)S(1)}, u32[]{:S(2)}, u32[]{:S(2)}) async-start(bf16[64,16,128]{2,1,0:T(8,128)(2,1)} %bitcast.23), calls=%async_computation.1 | async-start | bytes 524288 | tf_op jit(solution)/shard_map/all_to_all | solution.py:347
  53.0 1.7 %collective-permute-start = (bf16[512,128]{1,0:T(8,128)(2,1)}, bf16[512,128]{1,0:T(8,128)(2,1)S(1)}, u32[]{:S(2)}, u32[]{:S(2)}) collective-permute-start(bf16[512,128]{1,0:T(8,128)(2,1)} %get-tuple-element.39), channel_id=1, source_target_pairs={{0,4},{4,0},{8,12},{12,8},{16,20},{20,16},{24,28},{28,24},{32,36},... | collective-permute-start | bytes 393224 | tf_op jit(solution)/shard_map/ppermute | solution.py:343
  54.7 13.0 %copy-start.7 = (bf16[512,128]{1,0:T(8,128)(2,1)}, bf16[512,128]{1,0:T(8,128)(2,1)S(1)}, u32[]{:S(2)}) copy-start(bf16[512,128]{1,0:T(8,128)(2,1)S(1)} %collective-permute-done.refs_1_) | copy-start | bytes 393220
  62.1 0.7 copy-start.3
  62.8 47.0 %copy-start = (bf16[2048,256]{1,0:T(8,128)(2,1)S(1)}, bf16[2048,256]{1,0:T(8,128)(2,1)}, u32[]{:S(2)}) copy-start(bf16[2048,256]{1,0:T(8,128)(2,1)} %get-tuple-element.37.refs_3_) | copy-start | bytes 3145732
  66.0 1.7 %collective-permute-start.1 = (bf16[768,128]{1,0:T(8,128)(2,1)}, bf16[768,128]{1,0:T(8,128)(2,1)S(1)}, u32[]{:S(2)}, u32[]{:S(2)}) collective-permute-start(bf16[768,128]{1,0:T(8,128)(2,1)} %get-tuple-element.47), channel_id=1, source_target_pairs={{0,4},{4,0},{8,12},{12,8},{16,20},{20,16},{24,28},{28,24},{32,36},... | collective-permute-start | bytes 589832 | tf_op jit(solution)/shard_map/ppermute | solution.py:343
  67.7 0.7 copy-start.6
  70.4 16.7 %all-to-all-start.2 = ((bf16[32,40,128]{2,1,0:T(8,128)(2,1)}), bf16[32,40,128]{2,1,0:T(8,128)(2,1)S(1)}, u32[]{:S(2)}, u32[]{:S(2)}) async-start(bf16[32,40,128]{2,1,0:T(8,128)(2,1)} %bitcast.19), calls=%async_computation.2 | async-start | bytes 655360 | tf_op jit(solution)/shard_map/all_to_all | solution.py:352
  75.1 5.0 %collective-permute-start.2 = (bf16[32,512]{1,0:T(8,128)(2,1)S(1)}, bf16[32,512]{1,0:T(8,128)(2,1)S(1)}, u32[]{:S(2)}, u32[]{:S(2)}) collective-permute-start(bf16[32,512]{1,0:T(8,128)(2,1)S(1)} %get-tuple-element.56), channel_id=1, source_target_pairs={{0,1},{1,2},{2,3},{3,0},{4,5},{5,6},{6,7},{7,4},{8,9},{9,10},{10,1... | collective-permute-start | bytes 98312 | tf_op jit(solution)/shard_map/ppermute | solution.py:415
  76.5 4.6 %collective-permute-start.3 = (bf16[32,512]{1,0:T(8,128)(2,1)S(1)}, bf16[32,512]{1,0:T(8,128)(2,1)S(1)}, u32[]{:S(2)}, u32[]{:S(2)}) collective-permute-start(bf16[32,512]{1,0:T(8,128)(2,1)S(1)} %get-tuple-element.55), channel_id=1, source_target_pairs={{0,2},{1,3},{2,0},{3,1},{4,6},{5,7},{6,4},{7,5},{8,10},{9,11},{10,... | collective-permute-start | bytes 98312 | tf_op jit(solution)/shard_map/ppermute | solution.py:415
  79.1 3.1 %collective-permute-start.4 = (bf16[32,512]{1,0:T(8,128)(2,1)S(1)}, bf16[32,512]{1,0:T(8,128)(2,1)S(1)}, u32[]{:S(2)}, u32[]{:S(2)}) collective-permute-start(bf16[32,512]{1,0:T(8,128)(2,1)S(1)} %get-tuple-element.54), channel_id=1, source_target_pairs={{0,3},{1,0},{2,1},{3,2},{4,7},{5,4},{6,5},{7,6},{8,11},{9,8},{10,9... | collective-permute-start | bytes 98312 | tf_op jit(solution)/shard_map/ppermute | solution.py:415
  87.0 0.7 copy-start.1
  105.1 7.2 %copy-start.2 = (bf16[32,40,128]{2,1,0:T(8,128)(2,1)}, bf16[32,40,128]{2,1,0:T(8,128)(2,1)S(1)}, u32[]{:S(2)}) copy-start(bf16[32,40,128]{2,1,0:T(8,128)(2,1)S(1)} %all_to_all.20) | copy-start | bytes 983044
  105.1 7.2 %collective-permute-start.5 = (bf16[1280,128]{1,0:T(8,128)(2,1)S(1)}, bf16[1280,128]{1,0:T(8,128)(2,1)S(1)}, u32[]{:S(2)}, u32[]{:S(2)}) collective-permute-start(bf16[1280,128]{1,0:T(8,128)(2,1)S(1)} %bitcast.16), channel_id=1, source_target_pairs={{0,4},{4,0},{8,12},{12,8},{16,20},{20,16},{24,28},{28,24},{32,36},... | collective-permute-start | bytes 983048 | tf_op jit(solution)/shard_map/ppermute | solution.py:343
  112.3 0.7 copy-start.5

commit v3 on v2

--- a/solution.py
+++ b/solution.py
@@ -12,8 +12,9 @@
 F32 = jnp.float32
 BF16 = jnp.bfloat16
 ANY = pl.BlockSpec(memory_space=pl.ANY)
+VMEM = pl.BlockSpec(memory_space=pltpu.VMEM)
 SMEM = pl.BlockSpec(memory_space=pltpu.SMEM)
-PARAMS = pltpu.CompilerParams(vmem_limit_bytes=62 * 1024 * 1024)
+PARAMS = pltpu.CompilerParams(vmem_limit_bytes=40 * 1024 * 1024)
 
 
 def nn(a, b):
@@ -266,59 +267,78 @@
 
 
 class Load:
-    def __init__(self, source, buffer, sem):
-        self.buffer = buffer
-        self.copy = pltpu.make_async_copy(source, buffer, sem)
-        self.copy.start()
-        self.done = False
+    def __init__(self, source, buffer=None, sem=None):
+        self.buffer, self.copy = source, None
+        if buffer is not None:
+            self.buffer = buffer
+            self.copy = pltpu.make_async_copy(source, buffer, sem)
+            self.copy.start()
 
     def get(self):
-        if not self.done:
+        if self.copy is not None:
             self.copy.wait()
-            self.done = True
+            self.copy = None
         return self.buffer
 
 
 class Store:
-    def __init__(self, target, buffer, sem):
-        self.buffer = buffer
-        self.copy = pltpu.make_async_copy(buffer, target, sem)
-        self.started = False
+    def __init__(self, target, buffer=None, sem=None):
+        self.buffer, self.copy, self.started = target, None, False
+        if buffer is not None:
+            self.buffer = buffer
+            self.copy = pltpu.make_async_copy(buffer, target, sem)
 
     def send(self):
-        if not self.started:
+        if self.copy is not None and not self.started:
             self.copy.start()
             self.started = True
 
-
-def call(kernel, outs, ins, scalars=(), scratch=(), flops=0, moved=0):
+    def wait(self):
+        if self.copy is not None:
+            self.copy.wait()
+
+
+def call(kernel, outs, ins, scalars=(), scratch=(), near_in=(), near_out=(), flops=0, moved=0):
     ns, ni, no = len(scalars), len(ins), len(outs)
+    far_in = [i for i in range(ni) if i not in near_in]
+    far_out = [i for i in range(no) if i not in near_out]
+
+    ins = [
+        a if i in near_in else pltpu.with_memory_space_constraint(a, pltpu.HBM) for i, a in enumerate(ins)
+    ]
 
     def body(*refs):
         given, refs = refs[:ns], refs[ns:]
         sources, refs = refs[:ni], refs[ni:]
         targets, refs = refs[:no], refs[no:]
-        in_bufs, refs = refs[:ni], refs[ni:]
-        out_bufs, refs = refs[:no], refs[no:]
-        in_sems, out_sems, extra = refs[0], refs[1], refs[2:]
-        loads = [Load(r, b, in_sems.at[i]) for i, (r, b) in enumerate(zip(sources, in_bufs))]
-        stores = [Store(r, b, out_sems.at[i]) for i, (r, b) in enumerate(zip(targets, out_bufs))]
+        in_bufs, refs = dict(zip(far_in, refs)), refs[len(far_in) :]
+        out_bufs, refs = dict(zip(far_out, refs)), refs[len(far_out) :]
+        sems, extra = refs[0], refs[1:]
+        loads = [
+            Load(r, in_bufs[i], sems.at[i]) if i in in_bufs else Load(r) for i, r in enumerate(sources)
+        ]
+        stores = [
+            Store(r, out_bufs[i], sems.at[ni + i]) if i in out_bufs else Store(r)
+            for i, r in enumerate(targets)
+        ]
         kernel(*given, *loads, *stores, *extra)
         for load in loads:
             load.get()
         for store in stores:
             store.send()
         for store in stores:
-            store.copy.wait()
+            store.wait()
 
     return pl.pallas_call(
         body,
-        out_shape=[jax.ShapeDtypeStruct(s, d) for s, d in outs],
-        in_specs=[SMEM] * ns + [ANY] * ni,
-        out_specs=[ANY] * no,
-        scratch_shapes=[pltpu.VMEM(a.shape, a.dtype) for a in ins]
-        + [pltpu.VMEM(s, d) for s, d in outs]
-        + [pltpu.SemaphoreType.DMA((ni,)), pltpu.SemaphoreType.DMA((no,))]
+        out_shape=[
+            jax.ShapeDtypeStruct(s, d) if i in near_out else pltpu.HBM(s, d) for i, (s, d) in enumerate(outs)
+        ],
+        in_specs=[SMEM] * ns + [VMEM if i in near_in else ANY for i in range(ni)],
+        out_specs=[VMEM if i in near_out else ANY for i in range(no)],
+        scratch_shapes=[pltpu.VMEM(ins[i].shape, ins[i].dtype) for i in far_in]
+        + [pltpu.VMEM(*outs[i]) for i in far_out]
+        + [pltpu.SemaphoreType.DMA((ni + no,))]
         + list(scratch),
         compiler_params=PARAMS,
         cost_estimate=pl.CostEstimate(flops=flops, bytes_accessed=moved, transcendentals=0),
@@ -356,6 +376,7 @@
         pre_kernel,
         [((3 * slots, width), BF16), ((4, rows, width), F32), ((slots, rows), BF16)],
         (imp_x, imp_hist.reshape(1, rows), imp_len.reshape(1, rows), owner_map.reshape(1, owners), w_in, w_out, grad_y),
+        near_out=(0,),
         flops=2 * rows * depth * width * 3,
         moved=1 << 20,
     )
@@ -377,6 +398,8 @@
             pltpu.VMEM((width, slots), F32),
             pltpu.VMEM((width, slots), F32),
         ],
+        near_in=(0,),
+        near_out=(0,),
         flops=12 * events * slots * width,
         moved=4 << 20,
     )
@@ -388,6 +411,7 @@
         (hist, term, gkv),
         (core,),
         scratch=[pltpu.VMEM((2, half, width), BF16)],
+        near_out=(0, 1),
         flops=4 * events * depth * width,
         moved=4 << 20,
     )
@@ -400,12 +424,19 @@
         (back, place, aux, imp_x, w_in, grad_y),
         (core,),
         scratch=[pltpu.VMEM((2, half, width), BF16)],
+        near_in=(0,),
+        near_out=(0, 1, 2),
         flops=2 * rows * depth * width * 5,
         moved=2 << 20,
     )
     other = swap(other)
     (summed,) = call(
-        pair_kernel, [((chips * 40, width), BF16)], (kv_mine, kv_other, mine, other), moved=1 << 20
+        pair_kernel,
+        [((chips * 40, width), BF16)],
+        (kv_mine, kv_other, mine, other),
+        near_in=(0, 1, 2, 3),
+        near_out=(0,),
+        moved=1 << 20,
     )
     plane = lax.axis_index("mp")
     share = rows // planes
@@ -423,6 +454,8 @@
         lambda i, o: sum_kernel(factor, i, o),
         [((chips * 40, width), BF16)],
         (summed,),
+        near_in=(0,),
+        near_out=(0,),
         moved=1 << 20,
     )
     mine = exchange_core(piece)
@@ -433,6 +466,7 @@
         (mine, other),
         (core,),
         scratch=[pltpu.VMEM((depth, width), F32)],
+        near_in=(0, 1),
         moved=3 << 20,
     )
     grad_kv = gkv.reshape(1, events, 2, width)

time: 116 us -> 107 us (0.922)
  Pallas kernels: 32.4 us -> 27.9 us
  local copies, waits for them, and re-layouts: 5.49 us -> 1.11 us
  waiting for transfers between devices: 26.4 us -> 27.7 us
    pallas_call x8, Pallas kernels: 32.4 us -> 27.9 us  [call(): pl.pallas_call(body, out_shape=[jax.ShapeDtypeStruct(s, d) if i in near_o...]
    unnamed x16 -> x2, local copies, waits for them, and re-layouts: 3.59 us -> 0.01 us
  transfers between devices with their start and end apart: 9 -> 9, of which waited for: 7 -> 7; matrix products, arithmetic and copies ran while one was open for 3% -> 2% of each run, Pallas kernels for 8% -> 8%
where the time goes in v3:
time: 107 us; the launch traced here: 106 us
  starting transfers between devices  32.1 us (30%)
  Pallas kernels  27.9 us (26%)
  waiting for transfers between devices  27.7 us (26%)
  blocking collectives  15.8 us (15%)
  local copies, waits for them, and re-layouts  1.11 us (1%)
    pallas_call x8, Pallas kernels, call(): pl.pallas_call(body, out_shape=[jax.ShapeDtypeStruct(s, d) if i in near_o...  27.9 us
    all_to_all x2, starting transfers between devices, exchange(): a = lax.all_to_all(a, 'dp', 0, 0, tiled=True)  18.6 us
    all_to_all x2, waiting for transfers between devices, exchange(): a = lax.all_to_all(a, 'dp', 0, 0, tiled=True)  17.9 us
    all_to_all x1, blocking collectives, exchange_core(): a = lax.all_to_all(a, 'dp', 0, 0, axis_index_groups=same_core, tiled=True)  15.8 us
    all_to_all x1, waiting for transfers between devices, exchange_core(): a = lax.all_to_all(a, 'dp', 0, 0, axis_index_groups=same_core, tiled=True)  5.63 us
    ppermute x3, starting transfers between devices, on_device(): lax.ppermute(part, 'mp', [(i, (i + step) % planes) for i in range(planes)])  5.06 us
    ppermute x3, starting transfers between devices, swap(): return lax.ppermute(a, 'dp', pairs)  4.56 us
    all_to_all x1, starting transfers between devices, exchange_core(): a = lax.all_to_all(a, 'dp', 0, 0, axis_index_groups=same_core, tiled=True)  3.91 us
  transfers between devices with their start and end apart: 9, of which 7 were waited for; matrix products, arithmetic and copies ran while one was open for 2% of the time, Pallas kernels for 8%

profile of v3, /device:TPU:1, one launch (start us, length us, event | category | flops | bytes accessed | tf_op | source)
XLA Modules:
  0.0 106.1 jit_solution(6638612430856935590)
XLA Ops:
  0.6 3.2 %shard_map.111 = (bf16[1536,128]{1,0:T(8,128)(2,1)}, f32[4,128,128]{2,1,0:T(8,128)}, bf16[512,128]{1,0:T(8,128)(2,1)}) custom-call(bf16[128,512]{1,0:T(8,128)(2,1)} %refs_4_.3, s32[1,128]{1,0:T(1,128)} %bitcast.21, s32[1,128]{1,0:T(1,128)} %bitcast.22, s32[1,64]{1,0:T(1,128)} %bitcast.23, bf16[4,512,128]{2,1,0:T(8,128)(2,1)} %refs_5_.3, ...), custom_call_target="tpu_custom_call" | custom-call | flops 50331648 | bytes 1048576 | tf_op jit(solution)/shard_map/pallas_call | solution.py:332
  3.8 13.0 %all-to-all-start = ((bf16[64,24,128]{2,1,0:T(8,128)(2,1)}), bf16[64,24,128]{2,1,0:T(8,128)(2,1)S(1)}, u32[]{:S(2)}, u32[]{:S(2)}) async-start(bf16[64,24,128]{2,1,0:T(8,128)(2,1)} %bitcast.4), calls=%async_computation | async-start | bytes 786432 | tf_op jit(solution)/shard_map/all_to_all | solution.py:367
  16.8 5.4 %shard_map.112 = (bf16[2048,128]{1,0:T(8,128)(2,1)}, bf16[2048,128]{1,0:T(8,128)(2,1)}, bf16[128,2048]{1,0:T(8,128)(2,1)}, bf16[128,2048]{1,0:T(8,128)(2,1)}, f32[2048,128]{1,0:T(8,128)}) custom-call(bf16[2048,512]{1,0:T(8,128)(2,1)} %bitcast.19, bf16[4,512,128]{2,1,0:T(8,128)(2,1)} %refs_5_.3), custom_call_target="tpu_custom_call" | custom-call | flops 536870912 | bytes 5242880 | tf_op jit(solution)/shard_map/pallas_call | solution.py:332
  22.2 9.6 %all-to-all-done = bf16[64,24,128]{2,1,0:T(8,128)(2,1)S(1)} async-done(((bf16[64,24,128]{2,1,0:T(8,128)(2,1)}), bf16[64,24,128]{2,1,0:T(8,128)(2,1)S(1)}, u32[]{:S(2)}, u32[]{:S(2)}) %all-to-all-start) | async-done | bytes 393248 | tf_op jit(solution)/shard_map/all_to_all | solution.py:367
  31.9 11.5 %shard_map.113 = (bf16[1024,128]{1,0:T(8,128)(2,1)}, bf16[2048,256]{1,0:T(8,128)(2,1)}, bf16[2048,128]{1,0:T(8,128)(2,1)}) custom-call(bf16[1536,128]{1,0:T(8,128)(2,1)S(1)} %bitcast.18, bf16[2048,128]{1,0:T(8,128)(2,1)} %get-tuple-element.30.refs_1_, bf16[128,2048]{1,0:T(8,128)(2,1)} %get-tuple-element.31.refs_2_, ...), custom_call_target="tpu_custom_call" | custom-call | flops 1610612736 | bytes 4194304 | tf_op jit(solution)/shard_map/pallas_call | solution.py:332
  43.3 5.6 %all-to-all-start.1 = ((bf16[64,16,128]{2,1,0:T(8,128)(2,1)}), bf16[64,16,128]{2,1,0:T(8,128)(2,1)S(1)}, u32[]{:S(2)}, u32[]{:S(2)}) async-start(bf16[64,16,128]{2,1,0:T(8,128)(2,1)} %bitcast.7), calls=%async_computation.1 | async-start | bytes 524288 | tf_op jit(solution)/shard_map/all_to_all | solution.py:367
  49.0 3.4 %shard_map.114 = (bf16[512,128]{1,0:T(8,128)(2,1)S(1)}, bf16[512,128]{1,0:T(8,128)(2,1)S(1)}) custom-call(s32[1]{0:T(128)} %bitcast.refs_0_, bf16[2048,512]{1,0:T(8,128)(2,1)} %bitcast.20, bf16[2048,128]{1,0:T(8,128)(2,1)} %get-tuple-element.36.refs_2_, bf16[2048,256]{1,0:T(8,128)(2,1)} %get-tuple-element.37.refs_3_), custom_call_target="tpu_custom_call" | custom-call | flops 536870912 | bytes 4194304 | tf_op jit(solution)/shard_map/pallas_call | solution.py:332
  52.3 0.5 collective-permute-start
  52.9 1.0 collective-permute-done.refs_1_
  53.9 8.3 %all-to-all-done.1 = bf16[64,16,128]{2,1,0:T(8,128)(2,1)S(1)} async-done(((bf16[64,16,128]{2,1,0:T(8,128)(2,1)}), bf16[64,16,128]{2,1,0:T(8,128)(2,1)S(1)}, u32[]{:S(2)}, u32[]{:S(2)}) %all-to-all-start.1) | async-done | bytes 262176 | tf_op jit(solution)/shard_map/all_to_all | solution.py:367
  62.1 0.0 copy-start
  62.1 2.4 %shard_map.115 = (bf16[768,128]{1,0:T(8,128)(2,1)S(1)}, bf16[768,128]{1,0:T(8,128)(2,1)S(1)}, bf16[128,512]{1,0:T(8,128)(2,1)S(1)}) custom-call(s32[1]{0:T(128)} %bitcast.refs_0_, bf16[1024,128]{1,0:T(8,128)(2,1)S(1)} %bitcast.17, bf16[512,128]{1,0:T(8,128)(2,1)} %get-tuple-element.41.refs_2_, f32[4,128,128]{2,1,0:T(8,128)} %get-tuple-element.42.refs_3_, ...), custom_call_target="tpu_custom_call" | custom-call | flops 83886080 | bytes 2097152 | tf_op jit(solution)/shard_map/pallas_call | solution.py:332
  64.6 0.3 collective-permute-start.1
  64.9 1.2 %collective-permute-done.1.refs_3_ = bf16[768,128]{1,0:T(8,128)(2,1)S(1)} collective-permute-done((bf16[768,128]{1,0:T(8,128)(2,1)S(1)}, bf16[768,128]{1,0:T(8,128)(2,1)S(1)}, u32[]{:S(2)}, u32[]{:S(2)}) %collective-permute-start.1) | collective-permute-done | bytes 196640 | tf_op jit(solution)/shard_map/ppermute | solution.py:363
  66.1 0.8 shard_map.116
  66.9 3.9 %all-to-all-start.2 = ((bf16[32,40,128]{2,1,0:T(8,128)(2,1)}), bf16[32,40,128]{2,1,0:T(8,128)(2,1)S(1)}, u32[]{:S(2)}, u32[]{:S(2)}) async-start(bf16[32,40,128]{2,1,0:T(8,128)(2,1)} %bitcast.9), calls=%async_computation.2 | async-start | bytes 655360 | tf_op jit(solution)/shard_map/all_to_all | solution.py:372
  70.9 1.4 %collective-permute-start.2 = (bf16[32,512]{1,0:T(8,128)(2,1)S(1)}, bf16[32,512]{1,0:T(8,128)(2,1)S(1)}, u32[]{:S(2)}, u32[]{:S(2)}) collective-permute-start(bf16[32,512]{1,0:T(8,128)(2,1)S(1)} %get-tuple-element.56), channel_id=1, source_target_pairs={{0,1},{1,2},{2,3},{3,0},{4,5},{5,6},{6,7},{7,4},{8,9},{9,10},{10,1... | collective-permute-start | bytes 98312 | tf_op jit(solution)/shard_map/ppermute | solution.py:446
  72.3 2.6 %collective-permute-start.3 = (bf16[32,512]{1,0:T(8,128)(2,1)S(1)}, bf16[32,512]{1,0:T(8,128)(2,1)S(1)}, u32[]{:S(2)}, u32[]{:S(2)}) collective-permute-start(bf16[32,512]{1,0:T(8,128)(2,1)S(1)} %get-tuple-element.55), channel_id=1, source_target_pairs={{0,2},{1,3},{2,0},{3,1},{4,6},{5,7},{6,4},{7,5},{8,10},{9,11},{10,... | collective-permute-start | bytes 98312 | tf_op jit(solution)/shard_map/ppermute | solution.py:446
  74.9 1.1 %collective-permute-start.4 = (bf16[32,512]{1,0:T(8,128)(2,1)S(1)}, bf16[32,512]{1,0:T(8,128)(2,1)S(1)}, u32[]{:S(2)}, u32[]{:S(2)}) collective-permute-start(bf16[32,512]{1,0:T(8,128)(2,1)S(1)} %get-tuple-element.54), channel_id=1, source_target_pairs={{0,3},{1,0},{2,1},{3,2},{4,7},{5,4},{6,5},{7,6},{8,11},{9,8},{10,9... | collective-permute-start | bytes 98312 | tf_op jit(solution)/shard_map/ppermute | solution.py:446
  76.0 0.0 collective-permute-done.2
  76.0 0.6 collective-permute-done.3
  76.6 1.4 %collective-permute-done.4 = bf16[32,512]{1,0:T(8,128)(2,1)S(1)} collective-permute-done((bf16[32,512]{1,0:T(8,128)(2,1)S(1)}, bf16[32,512]{1,0:T(8,128)(2,1)S(1)}, u32[]{:S(2)}, u32[]{:S(2)}) %collective-permute-start.4) | collective-permute-done | bytes 32800 | tf_op jit(solution)/shard_map/ppermute | solution.py:446
  78.0 5.6 %all-to-all-done.2 = bf16[32,40,128]{2,1,0:T(8,128)(2,1)S(1)} async-done(((bf16[32,40,128]{2,1,0:T(8,128)(2,1)}), bf16[32,40,128]{2,1,0:T(8,128)(2,1)S(1)}, u32[]{:S(2)}, u32[]{:S(2)}) %all-to-all-start.2) | async-done | bytes 327712 | tf_op jit(solution)/shard_map/all_to_all | solution.py:372
  83.6 0.1 shard_map.117
  83.7 15.8 %all_to_all.20 = bf16[32,40,128]{2,1,0:T(8,128)(2,1)S(1)} all-to-all(bf16[32,40,128]{2,1,0:T(8,128)(2,1)S(1)} %bitcast.16), channel_id=1, replica_groups={{0,8,16,24,32,40,48,56,64,72,80,88,96,104,112,120,128,136,144,152,160,1..., dimensions={0} | all-to-all | bytes 655360 | tf_op jit(solution)/shard_map/all_to_all | solution.py:372
  99.5 3.7 %collective-permute-start.5 = (bf16[1280,128]{1,0:T(8,128)(2,1)S(1)}, bf16[1280,128]{1,0:T(8,128)(2,1)S(1)}, u32[]{:S(2)}, u32[]{:S(2)}) collective-permute-start(bf16[1280,128]{1,0:T(8,128)(2,1)S(1)} %bitcast.14), channel_id=1, source_target_pairs={{0,4},{4,0},{8,12},{12,8},{16,20},{20,16},{24,28},{28,24},{32,36},... | collective-permute-start | bytes 983048 | tf_op jit(solution)/shard_map/ppermute | solution.py:363
  103.2 0.0 copy-done
  103.2 1.1 %reshape.57 = bf16[1,2048,2,128]{3,2,1,0:T(2,128)(2,1)} reshape(bf16[2048,256]{1,0:T(8,128)(2,1)S(1)} %copy-done) | data formatting | bytes 2097152 | tf_op jit(solution)/shard_map/reshape | solution.py:472
  104.3 0.6 add_convert_fusion
  104.9 0.0 collective-permute-done.5.refs_2_
  104.9 1.2 %shard_map.118 = (f32[4,512,128]{2,1,0:T(8,128)}, f32[128,512]{1,0:T(8,128)}) custom-call(s32[1]{0:T(128)} %bitcast.refs_0_, bf16[1280,128]{1,0:T(8,128)(2,1)S(1)} %bitcast.15, bf16[1280,128]{1,0:T(8,128)(2,1)S(1)} %collective-permute-done.5.refs_2_), custom_call_target="tpu_custom_call" | custom-call | bytes 3145728 | tf_op jit(solution)/shard_map/pallas_call | solution.py:332
  (1 shorter events, 0.0 us)
Async XLA Ops:
  3.8 28.1 %all-to-all-start = ((bf16[64,24,128]{2,1,0:T(8,128)(2,1)}), bf16[64,24,128]{2,1,0:T(8,128)(2,1)S(1)}, u32[]{:S(2)}, u32[]{:S(2)}) async-start(bf16[64,24,128]{2,1,0:T(8,128)(2,1)} %bitcast.4), calls=%async_computation | async-start | bytes 786432 | tf_op jit(solution)/shard_map/all_to_all | solution.py:367
  43.3 18.8 %all-to-all-start.1 = ((bf16[64,16,128]{2,1,0:T(8,128)(2,1)}), bf16[64,16,128]{2,1,0:T(8,128)(2,1)S(1)}, u32[]{:S(2)}, u32[]{:S(2)}) async-start(bf16[64,16,128]{2,1,0:T(8,128)(2,1)} %bitcast.7), calls=%async_computation.1 | async-start | bytes 524288 | tf_op jit(solution)/shard_map/all_to_all | solution.py:367
  52.3 1.5 %collective-permute-start = (bf16[512,128]{1,0:T(8,128)(2,1)S(1)}, bf16[512,128]{1,0:T(8,128)(2,1)S(1)}, u32[]{:S(2)}, u32[]{:S(2)}) collective-permute-start(bf16[512,128]{1,0:T(8,128)(2,1)S(1)} %get-tuple-element.39), channel_id=1, source_target_pairs={{0,4},{4,0},{8,12},{12,8},{16,20},{20,16},{24,28},{28,24},{32,36},... | collective-permute-start | bytes 393224 | tf_op jit(solution)/shard_map/ppermute | solution.py:363
  62.1 41.1 %copy-start = (bf16[2048,256]{1,0:T(8,128)(2,1)S(1)}, bf16[2048,256]{1,0:T(8,128)(2,1)}, u32[]{:S(2)}) copy-start(bf16[2048,256]{1,0:T(8,128)(2,1)} %get-tuple-element.37.refs_3_) | copy-start | bytes 3145732
  64.6 1.5 %collective-permute-start.1 = (bf16[768,128]{1,0:T(8,128)(2,1)S(1)}, bf16[768,128]{1,0:T(8,128)(2,1)S(1)}, u32[]{:S(2)}, u32[]{:S(2)}) collective-permute-start(bf16[768,128]{1,0:T(8,128)(2,1)S(1)} %get-tuple-element.47), channel_id=1, source_target_pairs={{0,4},{4,0},{8,12},{12,8},{16,20},{20,16},{24,28},{28,24},{32,36},... | collective-permute-start | bytes 589832 | tf_op jit(solution)/shard_map/ppermute | solution.py:363
  66.9 16.7 %all-to-all-start.2 = ((bf16[32,40,128]{2,1,0:T(8,128)(2,1)}), bf16[32,40,128]{2,1,0:T(8,128)(2,1)S(1)}, u32[]{:S(2)}, u32[]{:S(2)}) async-start(bf16[32,40,128]{2,1,0:T(8,128)(2,1)} %bitcast.9), calls=%async_computation.2 | async-start | bytes 655360 | tf_op jit(solution)/shard_map/all_to_all | solution.py:372
  70.9 5.1 %collective-permute-start.2 = (bf16[32,512]{1,0:T(8,128)(2,1)S(1)}, bf16[32,512]{1,0:T(8,128)(2,1)S(1)}, u32[]{:S(2)}, u32[]{:S(2)}) collective-permute-start(bf16[32,512]{1,0:T(8,128)(2,1)S(1)} %get-tuple-element.56), channel_id=1, source_target_pairs={{0,1},{1,2},{2,3},{3,0},{4,5},{5,6},{6,7},{7,4},{8,9},{9,10},{10,1... | collective-permute-start | bytes 98312 | tf_op jit(solution)/shard_map/ppermute | solution.py:446
  72.3 4.3 %collective-permute-start.3 = (bf16[32,512]{1,0:T(8,128)(2,1)S(1)}, bf16[32,512]{1,0:T(8,128)(2,1)S(1)}, u32[]{:S(2)}, u32[]{:S(2)}) collective-permute-start(bf16[32,512]{1,0:T(8,128)(2,1)S(1)} %get-tuple-element.55), channel_id=1, source_target_pairs={{0,2},{1,3},{2,0},{3,1},{4,6},{5,7},{6,4},{7,5},{8,10},{9,11},{10,... | collective-permute-start | bytes 98312 | tf_op jit(solution)/shard_map/ppermute | solution.py:446
  74.9 3.1 %collective-permute-start.4 = (bf16[32,512]{1,0:T(8,128)(2,1)S(1)}, bf16[32,512]{1,0:T(8,128)(2,1)S(1)}, u32[]{:S(2)}, u32[]{:S(2)}) collective-permute-start(bf16[32,512]{1,0:T(8,128)(2,1)S(1)} %get-tuple-element.54), channel_id=1, source_target_pairs={{0,3},{1,0},{2,1},{3,2},{4,7},{5,4},{6,5},{7,6},{8,11},{9,8},{10,9... | collective-permute-start | bytes 98312 | tf_op jit(solution)/shard_map/ppermute | solution.py:446
  99.5 5.4 %collective-permute-start.5 = (bf16[1280,128]{1,0:T(8,128)(2,1)S(1)}, bf16[1280,128]{1,0:T(8,128)(2,1)S(1)}, u32[]{:S(2)}, u32[]{:S(2)}) collective-permute-start(bf16[1280,128]{1,0:T(8,128)(2,1)S(1)} %bitcast.14), channel_id=1, source_target_pairs={{0,4},{4,0},{8,12},{12,8},{16,20},{20,16},{24,28},{28,24},{32,36},... | collective-permute-start | bytes 983048 | tf_op jit(solution)/shard_map/ppermute | solution.py:363

commit v4 on v3

--- a/solution.py
+++ b/solution.py
@@ -9,6 +9,8 @@
 EPSILON = 1e-05
 CAP = 8
 BLOCK = 1024
+HISTORY_PARTS = 4
+LATE = 5
 F32 = jnp.float32
 BF16 = jnp.bfloat16
 ANY = pl.BlockSpec(memory_space=pl.ANY)
@@ -49,9 +51,7 @@
     return joined.reshape(count * 8 * len(parts), parts[0].shape[1])
 
 
-def pre_kernel(x_in, hist_in, len_in, owner_in, w_in, wo_in, gy_in, send_out, aux_out, place_out):
-    hist = hist_in.get()[...]
-    owner = owner_in.get()[...]
+def slot_table(hist, owner):
     rows, owners = hist.shape[1], owner.shape[1]
     named = jnp.where(iota((owners, rows), 0) == hist, 1.0, 0.0).astype(BF16)
     owner = jnp.broadcast_to(owner.astype(F32), (8, owners)).astype(BF16)
@@ -61,17 +61,19 @@
     before = nn(hit.astype(BF16), earlier.astype(BF16))
     rank = jnp.sum(before * hit, axis=0, keepdims=True)
     slot = target * float(CAP) + rank
-    slots = owners * CAP
-    place = jnp.where(iota((slots, rows), 0).astype(F32) == slot, 1.0, 0.0).astype(BF16)
-    place_out.buffer[...] = place
-    place_out.send()
+    return jnp.where(iota((owners * CAP, rows), 0).astype(F32) == slot, 1.0, 0.0).astype(BF16)
+
+
+def pre_kernel(hist_in, len_in, owner_in, x_in, w_in, wo_in, gy_in, send_out):
+    place = slot_table(hist_in.get()[...], owner_in.get()[...])
     length = len_in.get()[...].astype(F32)
+    rows = length.shape[1]
     high = jnp.floor(length * (1.0 / 256.0))
     low = length - 256.0 * high
     digits = jnp.transpose(jnp.where(iota((rows, rows), 0) == 0, high, low))
     x, w_ref = x_in.get()[...], w_in.get()
-    queries, slope_q = silu_and_slope(nn(x, w_ref[0]))
-    gates, slope_g = silu_and_slope(nn(x, w_ref[1]))
+    queries, _ = silu_and_slope(nn(x, w_ref[0]))
+    gates, _ = silu_and_slope(nn(x, w_ref[1]))
     cot = nt(gy_in.get()[...], wo_in.get()[...]).astype(BF16).astype(F32)
     gates = gates.astype(BF16).astype(F32)
     payload = jnp.concatenate(
@@ -82,18 +84,16 @@
     send_out.buffer[...] = spread(
         [packed[:, :width], packed[:, width : 2 * width], packed[:, 2 * width :]]
     ).astype(BF16)
-    send_out.send()
-    aux_out.buffer[0] = slope_q
-    aux_out.buffer[1] = slope_g
-    aux_out.buffer[2] = gates
-    aux_out.buffer[3] = cot
-
-
-def project_kernel(ev_in, w_in, k_out, v_out, kt_out, vt_out, slope_out):
-    ev_ref, w_ref = ev_in.get(), w_in.get()
-
-    def step(b, carry):
-        at = pl.ds(pl.multiple_of(b * 512, 512), 512)
+
+
+def project_kernel(
+    w_in, ev_in, hist_in, owner_in, x_in, wo_in, gy_in,
+    k_out, vt_out, v_out, kt_out, slope_out, aux_out, place_out,
+):
+    w_ref, ev_ref = w_in.get(), ev_in.get()
+    count = ev_ref.shape[0] // 512
+    for b in range(count):
+        at = pl.ds(b * 512, 512)
         ev = ev_ref[at, :]
         keys, slope = silu_and_slope(nn(ev, w_ref[2]))
         values = nn(ev, w_ref[3])
@@ -102,87 +102,123 @@
         slope_out.buffer[at, :] = slope
         kt_out.buffer[:, at] = jnp.transpose(keys.astype(BF16))
         vt_out.buffer[:, at] = jnp.transpose(values.astype(BF16))
-        return carry
-
-    lax.fori_loop(0, ev_ref.shape[0] // 512, step, 0)
+    for out in (k_out, v_out, kt_out, vt_out, slope_out):
+        out.send()
+    place_out.buffer[...] = slot_table(hist_in.get()[...], owner_in.get()[...])
+    x = x_in.get()[...]
+    _, slope_q = silu_and_slope(nn(x, w_ref[0]))
+    gates, slope_g = silu_and_slope(nn(x, w_ref[1]))
+    aux_out.buffer[0] = slope_q
+    aux_out.buffer[1] = slope_g
+    aux_out.buffer[2] = gates.astype(BF16).astype(F32)
+    aux_out.buffer[3] = nt(gy_in.get()[...], wo_in.get()[...]).astype(BF16).astype(F32)
 
 
 def attend_kernel(
-    recv_in, k_in, vt_in, v_in, kt_in, slope_in,
-    back_out, gkv_out, term_out,
-    w_scr, s_scr, att_scr, dq_scr,
+    recv_in, k_in, vt_in, v_in, kt_in,
+    back_out, weights_out, d_keys_out, d_att_out,
+    s_scr,
 ):
-    gkv_ref, term_ref = gkv_out.buffer, term_out.buffer
-    recv_ref = recv_in.get()
+    recv_ref, k_ref, vt_ref = recv_in.get(), k_in.get(), vt_in.get()
     slots, width = recv_ref.shape[0] // 3, recv_ref.shape[1]
     heads = width // DH
+    events = k_ref.shape[0]
     got = recv_ref[...].astype(F32).reshape(slots // CAP, 3 * CAP, width)
     q = got[:, :CAP].reshape(slots, width)
     dn = got[:, CAP : 2 * CAP].reshape(slots, width)
     digits = got[:, 2 * CAP :].reshape(slots, width)
     digits = jnp.transpose(digits)
     length = digits[0:1] * 256.0 + digits[1:2]
-    qt = jnp.transpose(q)
     head_row = iota((width, slots), 0) // DH
     head_col = iota((slots, width), 1) // DH
-    qt_half = (qt * (0.5 * DH ** (-0.5))).astype(BF16)
+    qt_half = (jnp.transpose(q) * (0.5 * DH ** (-0.5))).astype(BF16)
     zero = jnp.zeros((), BF16)
     qt_of = [jnp.where(head_row == h, qt_half, zero) for h in range(heads)]
-    att_scr[...] = jnp.zeros_like(att_scr)
-    k_ref, vt_ref = k_in.get(), vt_in.get()
-    events = k_ref.shape[0]
-
-    def forward(b, carry):
-        start = pl.multiple_of(b * BLOCK, BLOCK)
+    att = [jnp.zeros((DH, slots), F32)] * heads
+    for start in range(0, events, BLOCK):
         at = pl.ds(start, BLOCK)
         visible = (iota((BLOCK, slots), 0) + start).astype(F32) < length
         for h in range(heads):
+            cols = slice(h * slots, (h + 1) * slots)
             half = nn(k_ref[at, :], qt_of[h])
             twice = jnp.where(visible, jnp.tanh(half) + 1.0, 0.0)
             weights = half * twice
-            s_scr[h, at, :] = (twice + weights * (2.0 - twice)).astype(BF16)
+            s_scr[at, cols] = (twice + weights * (2.0 - twice)).astype(BF16)
             weights = weights.astype(BF16)
-            w_scr[h, at, :] = weights
-            mine = pl.ds(h * DH, DH)
-            att_scr[mine, :] += nn(vt_ref[mine, at], weights)
-        return carry
-
-    lax.fori_loop(0, events // BLOCK, forward, 0)
-    att = att_scr[...].reshape(heads, DH, slots)
+            weights_out.buffer[at, cols] = weights
+            att[h] += nn(vt_ref[h * DH : (h + 1) * DH, at], weights)
+        weights_out.send_part((at,))
+    att = jnp.concatenate(att, axis=0).reshape(heads, DH, slots)
     inverse = lax.rsqrt(jnp.mean(att * att, axis=1, keepdims=True) + EPSILON)
     normed = att * inverse
     dnt = jnp.transpose(dn).reshape(heads, DH, slots)
     d_att = inverse * (dnt - normed * jnp.mean(dnt * normed, axis=1, keepdims=True))
     d_att = d_att.reshape(width, slots)
     d_att_t = d_att.astype(BF16)
-    d_att = jnp.transpose(d_att).astype(BF16)
+    d_att_out.buffer[...] = jnp.transpose(d_att).astype(BF16)
+    d_att_out.send()
     normed = jnp.transpose(normed.reshape(width, slots))
+    dt_of = [jnp.where(head_row == h, d_att_t, zero) for h in range(heads)]
     q_bf = q.astype(BF16)
-    dt_of = [jnp.where(head_row == h, d_att_t, zero) for h in range(heads)]
-    d_of = [jnp.where(head_col == h, d_att, zero) for h in range(heads)]
-    q_of = [jnp.where(head_col == h, q_bf, zero) for h in range(heads)]
-    dq_scr[...] = jnp.zeros_like(dq_scr)
-    v_ref, kt_ref, slope_ref = v_in.get(), kt_in.get(), slope_in.get()
-
-    def backward(b, carry):
-        at = pl.ds(pl.multiple_of(b * BLOCK, BLOCK), BLOCK)
-        d_keys = jnp.zeros((BLOCK, width), F32)
-        d_values = jnp.zeros((BLOCK, width), F32)
+    q_of = jnp.concatenate([jnp.where(head_col == h, q_bf, zero) for h in range(heads)], axis=0)
+    v_ref, kt_ref = v_in.get(), kt_in.get()
+    d_query = [jnp.zeros((DH, slots), F32)] * heads
+    for start in range(0, events, BLOCK):
+        at = pl.ds(start, BLOCK)
         for h in range(heads):
-            ds = (nn(v_ref[at, :], dt_of[h]) * s_scr[h, at, :].astype(F32)).astype(BF16)
-            mine = pl.ds(h * DH, DH)
-            dq_scr[mine, :] += nn(kt_ref[mine, at], ds)
-            d_keys += nn(ds, q_of[h])
-            d_values += nn(w_scr[h, at, :], d_of[h])
-        d_keys = d_keys * (0.5 * DH ** (-0.5))
-        gkv_ref[at, :width] = d_keys.astype(BF16)
-        gkv_ref[at, width:] = d_values.astype(BF16)
-        term_ref[at, :] = (d_keys * slope_ref[at, :]).astype(BF16)
-        return carry
-
-    lax.fori_loop(0, events // BLOCK, backward, 0)
-    d_query = jnp.transpose(dq_scr[...] * (0.5 * DH ** (-0.5)))
-    back_out.buffer[...] = spread([d_query, normed]).astype(BF16)
+            cols = slice(h * slots, (h + 1) * slots)
+            ds = (nn(v_ref[at, :], dt_of[h]) * s_scr[at, cols].astype(F32)).astype(BF16)
+            s_scr[at, cols] = ds
+            d_query[h] += nn(kt_ref[h * DH : (h + 1) * DH, at], ds)
+        d_keys = nn(s_scr[at, :], q_of) * (0.5 * DH ** (-0.5))
+        d_keys_out.buffer[at, :] = d_keys.astype(BF16)
+        d_keys_out.send_part((at,))
+    d_query = jnp.concatenate(d_query, axis=0) * (0.5 * DH ** (-0.5))
+    back_out.buffer[...] = spread([jnp.transpose(d_query), normed]).astype(BF16)
+
+
+def history_kernel(
+    core_ref, d_att_in, d_keys_in, slope_in, weights_in, ev_in, *rest
+):
+    late, rest = rest[:LATE], rest[LATE:]
+    gkv_out, mine_out, other_out, rest = rest[0], rest[1], rest[2], rest[3:]
+    kept, (scr, w_scr, term_scr, sems, late_sems) = rest[:LATE], rest[LATE:]
+    events = w_scr.shape[0]
+    step = events // HISTORY_PARTS
+    parts = [pl.ds(b * step, step) for b in range(HISTORY_PARTS)]
+    copies = [
+        pltpu.make_async_copy(weights_in.get().at[at], w_scr.at[at], sems.at[b])
+        for b, at in enumerate(parts)
+    ]
+    for copy in copies:
+        copy.start()
+    moves = [
+        pltpu.make_async_copy(src.get().at[: dst.buffer.shape[0]], dst.buffer, late_sems.at[i])
+        for i, (src, dst) in enumerate(zip(late, kept))
+    ]
+    for move in moves:
+        move.start()
+    d_att = d_att_in.get()[...]
+    slots, width = d_att.shape
+    heads = width // DH
+    head_col = iota((slots, width), 1) // DH
+    zero = jnp.zeros((), BF16)
+    d_of = jnp.concatenate([jnp.where(head_col == h, d_att, zero) for h in range(heads)], axis=0)
+    d_keys_ref, slope_ref, gkv_ref = d_keys_in.get(), slope_in.get(), gkv_out.buffer
+    for at, copy in zip(parts, copies):
+        d_keys = d_keys_ref[at, :]
+        gkv_ref[at, :width] = d_keys
+        term_scr[at, :width] = (d_keys.astype(F32) * slope_ref[at, :]).astype(BF16)
+        copy.wait()
+        d_values = nn(w_scr[at, :], d_of).astype(BF16)
+        gkv_ref[at, width:] = d_values
+        gkv_out.send_part((at,))
+        term_scr[at, width:] = d_values
+    both = jnp.transpose(tn(term_scr[...], ev_in.get()[...]))
+    rows = spread([both[:, :width], both[:, width:]]).astype(BF16)
+    split_halves(core_ref[0], rows, scr, mine_out, other_out)
+    for move in moves:
+        move.wait()
 
 
 def split_halves(core, rows, scr, mine_out, other_out):
@@ -192,14 +228,6 @@
     other_out.buffer[...] = scr[1 - core]
     other_out.send()
     mine_out.buffer[...] = scr[core]
-
-
-def history_grads_kernel(core_ref, ev_in, term_in, gkv_in, mine_out, other_out, scr):
-    term_ref = term_in.get()
-    width = term_ref.shape[1]
-    gv = tn(ev_in.get()[...], gkv_in.get()[:, width:])
-    gk = tn(ev_in.get()[...], term_ref[...])
-    split_halves(core_ref[0], spread([gk, gv]).astype(BF16), scr, mine_out, other_out)
 
 
 def post_kernel(core_ref, back_in, place_in, aux_in, x_in, w_in, gy_in, mine_out, other_out, gx_out, scr):
@@ -284,6 +312,7 @@
 class Store:
     def __init__(self, target, buffer=None, sem=None):
         self.buffer, self.copy, self.started = target, None, False
+        self.target, self.sem = target, sem
         if buffer is not None:
             self.buffer = buffer
             self.copy = pltpu.make_async_copy(buffer, target, sem)
@@ -293,14 +322,18 @@
             self.copy.start()
             self.started = True
 
+    def send_part(self, at):
+        pltpu.make_async_copy(self.buffer.at[at], self.target.at[at], self.sem).start()
+        self.started = True
+
     def wait(self):
         if self.copy is not None:
             self.copy.wait()
 
 
-def call(kernel, outs, ins, scalars=(), scratch=(), near_in=(), near_out=(), flops=0, moved=0):
+def call(kernel, outs, ins, scalars=(), scratch=(), near_in=(), raw_in=(), near_out=(), flops=0, moved=0):
     ns, ni, no = len(scalars), len(ins), len(outs)
-    far_in = [i for i in range(ni) if i not in near_in]
+    far_in = [i for i in range(ni) if i not in near_in and i not in raw_in]
     far_out = [i for i in range(no) if i not in near_out]
 
     ins = [
@@ -372,48 +405,70 @@
         a = lax.all_to_all(a, "dp", 0, 0, axis_index_groups=same_core, tiled=True)
         return a.reshape(a.shape[0] * a.shape[1], width)
 
-    send, aux, place = call(
+    hist_rows = imp_hist.reshape(1, rows)
+    owner_row = owner_map.reshape(1, owners)
+    (send,) = call(
         pre_kernel,
-        [((3 * slots, width), BF16), ((4, rows, width), F32), ((slots, rows), BF16)],
-        (imp_x, imp_hist.reshape(1, rows), imp_len.reshape(1, rows), owner_map.reshape(1, owners), w_in, w_out, grad_y),
+        [((3 * slots, width), BF16)],
+        (hist_rows, imp_len.reshape(1, rows), owner_row, imp_x, w_in, w_out, grad_y),
         near_out=(0,),
         flops=2 * rows * depth * width * 3,
         moved=1 << 20,
     )
     recv = exchange(send)
-    keys, values, keys_t, values_t, key_slope = call(
+    keys, values_t, values, keys_t, key_slope, aux, place = call(
         project_kernel,
-        [((events, width), BF16)] * 2 + [((width, events), BF16)] * 2 + [((events, width), F32)],
-        (hist, w_in),
+        [
+            ((events, width), BF16),
+            ((width, events), BF16),
+            ((events, width), BF16),
+            ((width, events), BF16),
+            ((events, width), F32),
+            ((4, rows, width), F32),
+            ((slots, rows), BF16),
+        ],
+        (w_in, hist, hist_rows, owner_row, imp_x, w_out, grad_y),
+        near_out=(0, 1),
         flops=4 * events * depth * width,
         moved=5 << 20,
     )
-    back, gkv, term = call(
+    heads = width // DH
+    back, weights, d_keys, d_att = call(
         attend_kernel,
-        [((2 * slots, width), BF16), ((events, 2 * width), BF16), ((events, width), BF16)],
-        (recv, keys, values_t, values, keys_t, key_slope),
+        [
+            ((2 * slots, width), BF16),
+            ((events, heads * slots), BF16),
+            ((events, width), BF16),
+            ((slots, width), BF16),
+        ],
+        (recv, keys, values_t, values, keys_t),
+        scratch=[pltpu.VMEM((events, heads * slots), BF16)],
+        near_in=(0, 1, 2),
+        near_out=(0,),
+        flops=10 * events * slots * width,
+        moved=8 << 20,
+    )
+    back = exchange(back)
+    half = depth * 2 // 2
+    gkv, kv_mine, kv_other, place, aux, x_near, w_near, gy_near = call(
+        history_kernel,
+        [((events, 2 * width), BF16)]
+        + [((half, width), BF16)] * 2
+        + [(place.shape, BF16), (aux.shape, F32), (imp_x.shape, BF16)]
+        + [((2,) + w_in.shape[1:], BF16), (grad_y.shape, BF16)],
+        (d_att, d_keys, key_slope, weights, hist, place, aux, imp_x, w_in, grad_y),
+        (core,),
         scratch=[
-            pltpu.VMEM((width // DH, events, slots), BF16),
-            pltpu.VMEM((width // DH, events, slots), BF16),
-            pltpu.VMEM((width, slots), F32),
-            pltpu.VMEM((width, slots), F32),
+            pltpu.VMEM((2, half, width), BF16),
+            pltpu.VMEM((events, heads * slots), BF16),
+            pltpu.VMEM((events, 2 * width), BF16),
+            pltpu.SemaphoreType.DMA((HISTORY_PARTS,)),
+            pltpu.SemaphoreType.DMA((LATE,)),
         ],
-        near_in=(0,),
-        near_out=(0,),
-        flops=12 * events * slots * width,
-        moved=4 << 20,
-    )
-    back = exchange(back)
-    half = depth * width * 2 // 2 // width
-    kv_mine, kv_other = call(
-        history_grads_kernel,
-        [((half, width), BF16)] * 2,
-        (hist, term, gkv),
-        (core,),
-        scratch=[pltpu.VMEM((2, half, width), BF16)],
-        near_out=(0, 1),
-        flops=4 * events * depth * width,
-        moved=4 << 20,
+        raw_in=(3, 5, 6, 7, 8, 9),
+        near_out=(1, 2, 3, 4, 5, 6, 7),
+        flops=4 * events * depth * width + 2 * events * slots * width,
+        moved=10 << 20,
     )
     kv_other = swap(kv_other)
     back, kv_mine, kv_other = lax.optimization_barrier((back, kv_mine, kv_other))
@@ -421,10 +476,10 @@
     mine, other, gx = call(
         post_kernel,
         [((half, width), BF16)] * 2 + [((rows, depth), BF16)],
-        (back, place, aux, imp_x, w_in, grad_y),
+        (back, place, aux, x_near, w_near, gy_near),
         (core,),
         scratch=[pltpu.VMEM((2, half, width), BF16)],
-        near_in=(0,),
+        near_in=(0, 1, 2, 3, 4, 5),
         near_out=(0, 1, 2),
         flops=2 * rows * depth * width * 5,
         moved=2 << 20,

time: 107 us -> 102 us (0.953)
  waiting for transfers between devices: 27.7 us -> 25.2 us
  Pallas kernels: 27.9 us -> 25.5 us
    all_to_all x2, waiting for transfers between devices: 17.9 us -> 15.4 us  [exchange(): a = lax.all_to_all(a, 'dp', 0, 0, tiled=True)]
    pallas_call x8, Pallas kernels: 27.9 us -> 25.5 us  [call(): pl.pallas_call(body, out_shape=[jax.ShapeDtypeStruct(s, d) if i in near_o...]
  transfers between devices with their start and end apart: 9 -> 9, of which waited for: 7 -> 7; matrix products, arithmetic and copies ran while one was open for 2% -> 2% of each run, Pallas kernels for 8% -> 11%
where the time goes in v4:
time: 102 us
  starting transfers between devices  32.5 us (32%)
  Pallas kernels  25.5 us (25%)
  waiting for transfers between devices  25.2 us (25%)
  blocking collectives  15.8 us (15%)
  local copies, waits for them, and re-layouts  1.11 us (1%)
    pallas_call x8, Pallas kernels, call(): pl.pallas_call(body, out_shape=[jax.ShapeDtypeStruct(s, d) if i in near_o...  25.5 us
    all_to_all x2, starting transfers between devices, exchange(): a = lax.all_to_all(a, 'dp', 0, 0, tiled=True)  18.6 us
    all_to_all x1, blocking collectives, exchange_core(): a = lax.all_to_all(a, 'dp', 0, 0, axis_index_groups=same_core, tiled=True)  15.8 us
    all_to_all x2, waiting for transfers between devices, exchange(): a = lax.all_to_all(a, 'dp', 0, 0, tiled=True)  15.4 us
    all_to_all x1, waiting for transfers between devices, exchange_core(): a = lax.all_to_all(a, 'dp', 0, 0, axis_index_groups=same_core, tiled=True)  5.64 us
    ppermute x3, starting transfers between devices, on_device(): lax.ppermute(part, 'mp', [(i, (i + step) % planes) for i in range(planes)])  5.06 us
    ppermute x3, starting transfers between devices, swap(): return lax.ppermute(a, 'dp', pairs)  4.74 us
    all_to_all x1, starting transfers between devices, exchange_core(): a = lax.all_to_all(a, 'dp', 0, 0, axis_index_groups=same_core, tiled=True)  4.1 us
  transfers between devices with their start and end apart: 9, of which 7 were waited for; matrix products, arithmetic and copies ran while one was open for 2% of the time, Pallas kernels for 11%

profile of v4, /device:TPU:1, one launch (start us, length us, event | category | flops | bytes accessed | tf_op | source)
XLA Modules:
  0.0 101.8 jit_solution(13491946559965809900)
XLA Ops:
  0.6 2.7 %shard_map.111 = bf16[1536,128]{1,0:T(8,128)(2,1)} custom-call(s32[1,128]{1,0:T(1,128)} %bitcast.21, s32[1,128]{1,0:T(1,128)} %bitcast.25, s32[1,64]{1,0:T(1,128)} %bitcast.23, bf16[128,512]{1,0:T(8,128)(2,1)} %refs_8_.1, bf16[4,512,128]{2,1,0:T(8,128)(2,1)} %refs_9_.1, bf16[128,512]{1,0:T(8,128)(2,1)} %refs_5_.3, bf16[128,512]{1,0:T(8,128)(2,1)} %refs_10_.1), custom_call_target="tpu_custom_call" | custom-call | flops 50331648 | bytes 1048576 | tf_op jit(solution)/shard_map/pallas_call | solution.py:365
  3.3 13.0 %all-to-all-start = ((bf16[64,24,128]{2,1,0:T(8,128)(2,1)}), bf16[64,24,128]{2,1,0:T(8,128)(2,1)S(1)}, u32[]{:S(2)}, u32[]{:S(2)}) async-start(bf16[64,24,128]{2,1,0:T(8,128)(2,1)} %bitcast.4), calls=%async_computation | async-start | bytes 786432 | tf_op jit(solution)/shard_map/all_to_all | solution.py:400
  16.3 4.8 %shard_map.112 = (bf16[2048,128]{1,0:T(8,128)(2,1)S(1)}, bf16[128,2048]{1,0:T(8,128)(2,1)S(1)}, bf16[2048,128]{1,0:T(8,128)(2,1)}, bf16[128,2048]{1,0:T(8,128)(2...) custom-call(bf16[4,512,128]{2,1,0:T(8,128)(2,1)} %refs_9_.1, ...), custom_call_target="tpu_custom_call" | custom-call | flops 536870912 | bytes 5242880 | tf_op jit(solution)/shard_map/pallas_call | solution.py:365
  21.1 10.3 %all-to-all-done = bf16[64,24,128]{2,1,0:T(8,128)(2,1)S(1)} async-done(((bf16[64,24,128]{2,1,0:T(8,128)(2,1)}), bf16[64,24,128]{2,1,0:T(8,128)(2,1)S(1)}, u32[]{:S(2)}, u32[]{:S(2)}) %all-to-all-start) | async-done | bytes 393248 | tf_op jit(solution)/shard_map/all_to_all | solution.py:400
  31.4 9.1 %shard_map.113 = (bf16[1024,128]{1,0:T(8,128)(2,1)}, bf16[2048,1024]{1,0:T(8,128)(2,1)}, bf16[2048,128]{1,0:T(8,128)(2,1)}, bf16[512,128]{1,0:T(8,128)(2,1)}) custom-call(bf16[1536,128]{1,0:T(8,128)(2,1)S(1)} %bitcast.18, bf16[2048,128]{1,0:T(8,128)(2,1)S(1)} %get-tuple-element.35.refs_1_, bf16[128,2048]{1,0:T(8,128)(2,1)S(1)} %get-tuple-element.36.refs_2_, ...), custom_call_target="tpu_custom_call" | custom-call | flops 1342177280 | bytes 8388608 | tf_op jit(solution)/shard_map/pallas_call | solution.py:365
  40.5 5.6 %all-to-all-start.1 = ((bf16[64,16,128]{2,1,0:T(8,128)(2,1)}), bf16[64,16,128]{2,1,0:T(8,128)(2,1)S(1)}, u32[]{:S(2)}, u32[]{:S(2)}) async-start(bf16[64,16,128]{2,1,0:T(8,128)(2,1)} %bitcast.7), calls=%async_computation.1 | async-start | bytes 524288 | tf_op jit(solution)/shard_map/all_to_all | solution.py:400
  46.1 6.3 %shard_map.114 = (bf16[2048,256]{1,0:T(8,128)(2,1)}, bf16[512,128]{1,0:T(8,128)(2,1)S(1)}, bf16[512,128]{1,0:T(8,128)(2,1)S(1)}, bf16[512,128]{1,0:T(8,128)(2,1)...) custom-call(s32[1]{0:T(128)} %bitcast.refs_0_, ...), custom_call_target="tpu_custom_call" | custom-call | flops 805306368 | bytes 10485760 | tf_op jit(solution)/shard_map/pallas_call | solution.py:365
  52.4 0.0 copy-start
  52.4 0.7 collective-permute-start
  53.1 1.0 collective-permute-done.refs_1_
  54.1 5.1 %all-to-all-done.1 = bf16[64,16,128]{2,1,0:T(8,128)(2,1)S(1)} async-done(((bf16[64,16,128]{2,1,0:T(8,128)(2,1)}), bf16[64,16,128]{2,1,0:T(8,128)(2,1)S(1)}, u32[]{:S(2)}, u32[]{:S(2)}) %all-to-all-start.1) | async-done | bytes 262176 | tf_op jit(solution)/shard_map/all_to_all | solution.py:400
  59.2 0.6 shard_map.115
  59.9 0.3 collective-permute-start.1
  60.2 1.2 %collective-permute-done.1.refs_3_ = bf16[768,128]{1,0:T(8,128)(2,1)S(1)} collective-permute-done((bf16[768,128]{1,0:T(8,128)(2,1)S(1)}, bf16[768,128]{1,0:T(8,128)(2,1)S(1)}, u32[]{:S(2)}, u32[]{:S(2)}) %collective-permute-start.1) | collective-permute-done | bytes 196640 | tf_op jit(solution)/shard_map/ppermute | solution.py:396
  61.4 0.8 shard_map.116
  62.3 4.1 %all-to-all-start.2 = ((bf16[32,40,128]{2,1,0:T(8,128)(2,1)}), bf16[32,40,128]{2,1,0:T(8,128)(2,1)S(1)}, u32[]{:S(2)}, u32[]{:S(2)}) async-start(bf16[32,40,128]{2,1,0:T(8,128)(2,1)} %bitcast.9), calls=%async_computation.2 | async-start | bytes 655360 | tf_op jit(solution)/shard_map/all_to_all | solution.py:405
  66.5 1.4 %collective-permute-start.2 = (bf16[32,512]{1,0:T(8,128)(2,1)S(1)}, bf16[32,512]{1,0:T(8,128)(2,1)S(1)}, u32[]{:S(2)}, u32[]{:S(2)}) collective-permute-start(bf16[32,512]{1,0:T(8,128)(2,1)S(1)} %get-tuple-element.68), channel_id=1, source_target_pairs={{0,1},{1,2},{2,3},{3,0},{4,5},{5,6},{6,7},{7,4},{8,9},{9,10},{10,1... | collective-permute-start | bytes 98312 | tf_op jit(solution)/shard_map/ppermute | solution.py:501
  67.8 2.6 %collective-permute-start.3 = (bf16[32,512]{1,0:T(8,128)(2,1)S(1)}, bf16[32,512]{1,0:T(8,128)(2,1)S(1)}, u32[]{:S(2)}, u32[]{:S(2)}) collective-permute-start(bf16[32,512]{1,0:T(8,128)(2,1)S(1)} %get-tuple-element.67), channel_id=1, source_target_pairs={{0,2},{1,3},{2,0},{3,1},{4,6},{5,7},{6,4},{7,5},{8,10},{9,11},{10,... | collective-permute-start | bytes 98312 | tf_op jit(solution)/shard_map/ppermute | solution.py:501
  70.4 1.1 %collective-permute-start.4 = (bf16[32,512]{1,0:T(8,128)(2,1)S(1)}, bf16[32,512]{1,0:T(8,128)(2,1)S(1)}, u32[]{:S(2)}, u32[]{:S(2)}) collective-permute-start(bf16[32,512]{1,0:T(8,128)(2,1)S(1)} %get-tuple-element.66), channel_id=1, source_target_pairs={{0,3},{1,0},{2,1},{3,2},{4,7},{5,4},{6,5},{7,6},{8,11},{9,8},{10,9... | collective-permute-start | bytes 98312 | tf_op jit(solution)/shard_map/ppermute | solution.py:501
  71.5 0.0 collective-permute-done.2
  71.5 0.6 collective-permute-done.3
  72.1 1.4 %collective-permute-done.4 = bf16[32,512]{1,0:T(8,128)(2,1)S(1)} collective-permute-done((bf16[32,512]{1,0:T(8,128)(2,1)S(1)}, bf16[32,512]{1,0:T(8,128)(2,1)S(1)}, u32[]{:S(2)}, u32[]{:S(2)}) %collective-permute-start.4) | collective-permute-done | bytes 32800 | tf_op jit(solution)/shard_map/ppermute | solution.py:501
  73.5 5.6 %all-to-all-done.2 = bf16[32,40,128]{2,1,0:T(8,128)(2,1)S(1)} async-done(((bf16[32,40,128]{2,1,0:T(8,128)(2,1)}), bf16[32,40,128]{2,1,0:T(8,128)(2,1)S(1)}, u32[]{:S(2)}, u32[]{:S(2)}) %all-to-all-start.2) | async-done | bytes 327712 | tf_op jit(solution)/shard_map/all_to_all | solution.py:405
  79.2 0.1 shard_map.117
  79.2 15.8 %all_to_all.20 = bf16[32,40,128]{2,1,0:T(8,128)(2,1)S(1)} all-to-all(bf16[32,40,128]{2,1,0:T(8,128)(2,1)S(1)} %bitcast.16), channel_id=1, replica_groups={{0,8,16,24,32,40,48,56,64,72,80,88,96,104,112,120,128,136,144,152,160,1..., dimensions={0} | all-to-all | bytes 655360 | tf_op jit(solution)/shard_map/all_to_all | solution.py:405
  95.0 3.7 %collective-permute-start.5 = (bf16[1280,128]{1,0:T(8,128)(2,1)S(1)}, bf16[1280,128]{1,0:T(8,128)(2,1)S(1)}, u32[]{:S(2)}, u32[]{:S(2)}) collective-permute-start(bf16[1280,128]{1,0:T(8,128)(2,1)S(1)} %bitcast.14), channel_id=1, source_target_pairs={{0,4},{4,0},{8,12},{12,8},{16,20},{20,16},{24,28},{28,24},{32,36},... | collective-permute-start | bytes 983048 | tf_op jit(solution)/shard_map/ppermute | solution.py:396
  98.7 0.0 copy-done
  98.7 1.1 %reshape.57 = bf16[1,2048,2,128]{3,2,1,0:T(2,128)(2,1)} reshape(bf16[2048,256]{1,0:T(8,128)(2,1)S(1)} %copy-done) | data formatting | bytes 2097152 | tf_op jit(solution)/shard_map/reshape | solution.py:527
  99.8 0.6 add_convert_fusion
  100.4 0.0 collective-permute-done.5.refs_2_
  100.4 1.2 %shard_map.118 = (f32[4,512,128]{2,1,0:T(8,128)}, f32[128,512]{1,0:T(8,128)}) custom-call(s32[1]{0:T(128)} %bitcast.refs_0_, bf16[1280,128]{1,0:T(8,128)(2,1)S(1)} %bitcast.15, bf16[1280,128]{1,0:T(8,128)(2,1)S(1)} %collective-permute-done.5.refs_2_), custom_call_target="tpu_custom_call" | custom-call | bytes 3145728 | tf_op jit(solution)/shard_map/pallas_call | solution.py:365
  (1 shorter events, 0.0 us)
Async XLA Ops:
  3.3 28.1 %all-to-all-start = ((bf16[64,24,128]{2,1,0:T(8,128)(2,1)}), bf16[64,24,128]{2,1,0:T(8,128)(2,1)S(1)}, u32[]{:S(2)}, u32[]{:S(2)}) async-start(bf16[64,24,128]{2,1,0:T(8,128)(2,1)} %bitcast.4), calls=%async_computation | async-start | bytes 786432 | tf_op jit(solution)/shard_map/all_to_all | solution.py:400
  40.5 18.8 %all-to-all-start.1 = ((bf16[64,16,128]{2,1,0:T(8,128)(2,1)}), bf16[64,16,128]{2,1,0:T(8,128)(2,1)S(1)}, u32[]{:S(2)}, u32[]{:S(2)}) async-start(bf16[64,16,128]{2,1,0:T(8,128)(2,1)} %bitcast.7), calls=%async_computation.1 | async-start | bytes 524288 | tf_op jit(solution)/shard_map/all_to_all | solution.py:400
  52.4 46.3 %copy-start = (bf16[2048,256]{1,0:T(8,128)(2,1)S(1)}, bf16[2048,256]{1,0:T(8,128)(2,1)}, u32[]{:S(2)}) copy-start(bf16[2048,256]{1,0:T(8,128)(2,1)} %get-tuple-element.62) | copy-start | bytes 3145732
  52.4 1.7 %collective-permute-start = (bf16[512,128]{1,0:T(8,128)(2,1)S(1)}, bf16[512,128]{1,0:T(8,128)(2,1)S(1)}, u32[]{:S(2)}, u32[]{:S(2)}) collective-permute-start(bf16[512,128]{1,0:T(8,128)(2,1)S(1)} %get-tuple-element.47), channel_id=1, source_target_pairs={{0,4},{4,0},{8,12},{12,8},{16,20},{20,16},{24,28},{28,24},{32,36},... | collective-permute-start | bytes 393224 | tf_op jit(solution)/shard_map/ppermute | solution.py:396
  59.9 1.5 %collective-permute-start.1 = (bf16[768,128]{1,0:T(8,128)(2,1)S(1)}, bf16[768,128]{1,0:T(8,128)(2,1)S(1)}, u32[]{:S(2)}, u32[]{:S(2)}) collective-permute-start(bf16[768,128]{1,0:T(8,128)(2,1)S(1)} %get-tuple-element.58), channel_id=1, source_target_pairs={{0,4},{4,0},{8,12},{12,8},{16,20},{20,16},{24,28},{28,24},{32,36},... | collective-permute-start | bytes 589832 | tf_op jit(solution)/shard_map/ppermute | solution.py:396
  62.3 16.9 %all-to-all-start.2 = ((bf16[32,40,128]{2,1,0:T(8,128)(2,1)}), bf16[32,40,128]{2,1,0:T(8,128)(2,1)S(1)}, u32[]{:S(2)}, u32[]{:S(2)}) async-start(bf16[32,40,128]{2,1,0:T(8,128)(2,1)} %bitcast.9), calls=%async_computation.2 | async-start | bytes 655360 | tf_op jit(solution)/shard_map/all_to_all | solution.py:405
  66.5 5.1 %collective-permute-start.2 = (bf16[32,512]{1,0:T(8,128)(2,1)S(1)}, bf16[32,512]{1,0:T(8,128)(2,1)S(1)}, u32[]{:S(2)}, u32[]{:S(2)}) collective-permute-start(bf16[32,512]{1,0:T(8,128)(2,1)S(1)} %get-tuple-element.68), channel_id=1, source_target_pairs={{0,1},{1,2},{2,3},{3,0},{4,5},{5,6},{6,7},{7,4},{8,9},{9,10},{10,1... | collective-permute-start | bytes 98312 | tf_op jit(solution)/shard_map/ppermute | solution.py:501
  67.8 4.3 %collective-permute-start.3 = (bf16[32,512]{1,0:T(8,128)(2,1)S(1)}, bf16[32,512]{1,0:T(8,128)(2,1)S(1)}, u32[]{:S(2)}, u32[]{:S(2)}) collective-permute-start(bf16[32,512]{1,0:T(8,128)(2,1)S(1)} %get-tuple-element.67), channel_id=1, source_target_pairs={{0,2},{1,3},{2,0},{3,1},{4,6},{5,7},{6,4},{7,5},{8,10},{9,11},{10,... | collective-permute-start | bytes 98312 | tf_op jit(solution)/shard_map/ppermute | solution.py:501
  70.4 3.1 %collective-permute-start.4 = (bf16[32,512]{1,0:T(8,128)(2,1)S(1)}, bf16[32,512]{1,0:T(8,128)(2,1)S(1)}, u32[]{:S(2)}, u32[]{:S(2)}) collective-permute-start(bf16[32,512]{1,0:T(8,128)(2,1)S(1)} %get-tuple-element.66), channel_id=1, source_target_pairs={{0,3},{1,0},{2,1},{3,2},{4,7},{5,4},{6,5},{7,6},{8,11},{9,8},{10,9... | collective-permute-start | bytes 98312 | tf_op jit(solution)/shard_map/ppermute | solution.py:501
  95.0 5.4 %collective-permute-start.5 = (bf16[1280,128]{1,0:T(8,128)(2,1)S(1)}, bf16[1280,128]{1,0:T(8,128)(2,1)S(1)}, u32[]{:S(2)}, u32[]{:S(2)}) collective-permute-start(bf16[1280,128]{1,0:T(8,128)(2,1)S(1)} %bitcast.14), channel_id=1, source_target_pairs={{0,4},{4,0},{8,12},{12,8},{16,20},{20,16},{24,28},{28,24},{32,36},... | collective-permute-start | bytes 983048 | tf_op jit(solution)/shard_map/ppermute | solution.py:396

commit v5 on v4

--- a/solution.py
+++ b/solution.py
@@ -8,8 +8,8 @@
 DH = 64
 EPSILON = 1e-05
 CAP = 8
-BLOCK = 1024
-HISTORY_PARTS = 4
+BLOCK = 256
+HISTORY_PARTS = 2
 LATE = 5
 F32 = jnp.float32
 BF16 = jnp.bfloat16
@@ -64,17 +64,20 @@
     return jnp.where(iota((owners * CAP, rows), 0).astype(F32) == slot, 1.0, 0.0).astype(BF16)
 
 
-def pre_kernel(hist_in, len_in, owner_in, x_in, w_in, wo_in, gy_in, send_out):
+def pre_kernel(hist_in, len_in, owner_in, x_in, w_in, wo_in, gy_in, send_out, w_scr, w_sem):
+    w_copy = pltpu.make_async_copy(w_in.get().at[:2], w_scr, w_sem)
+    w_copy.start()
     place = slot_table(hist_in.get()[...], owner_in.get()[...])
     length = len_in.get()[...].astype(F32)
     rows = length.shape[1]
     high = jnp.floor(length * (1.0 / 256.0))
     low = length - 256.0 * high
     digits = jnp.transpose(jnp.where(iota((rows, rows), 0) == 0, high, low))
-    x, w_ref = x_in.get()[...], w_in.get()
-    queries, _ = silu_and_slope(nn(x, w_ref[0]))
-    gates, _ = silu_and_slope(nn(x, w_ref[1]))
     cot = nt(gy_in.get()[...], wo_in.get()[...]).astype(BF16).astype(F32)
+    x = x_in.get()[...]
+    w_copy.wait()
+    queries, _ = silu_and_slope(nn(x, w_scr[0]))
+    gates, _ = silu_and_slope(nn(x, w_scr[1]))
     gates = gates.astype(BF16).astype(F32)
     payload = jnp.concatenate(
         [queries.astype(BF16), (cot * gates).astype(BF16), digits.astype(BF16)], axis=1
@@ -99,7 +102,7 @@
         values = nn(ev, w_ref[3])
         k_out.buffer[at, :] = keys.astype(BF16)
         v_out.buffer[at, :] = values.astype(BF16)
-        slope_out.buffer[at, :] = slope
+        slope_out.buffer[at, :] = slope.astype(BF16)
         kt_out.buffer[:, at] = jnp.transpose(keys.astype(BF16))
         vt_out.buffer[:, at] = jnp.transpose(values.astype(BF16))
     for out in (k_out, v_out, kt_out, vt_out, slope_out):
@@ -124,57 +127,52 @@
     heads = width // DH
     events = k_ref.shape[0]
     got = recv_ref[...].astype(F32).reshape(slots // CAP, 3 * CAP, width)
-    q = got[:, :CAP].reshape(slots, width)
-    dn = got[:, CAP : 2 * CAP].reshape(slots, width)
-    digits = got[:, 2 * CAP :].reshape(slots, width)
-    digits = jnp.transpose(digits)
+    q = got[:, :CAP].reshape(slots, width).astype(BF16)
+    dn = got[:, CAP : 2 * CAP].reshape(slots, width).astype(BF16)
+    digits = got[:, 2 * CAP :].reshape(slots, width).astype(BF16)
+    digits = jnp.transpose(digits).astype(F32)
     length = digits[0:1] * 256.0 + digits[1:2]
     head_row = iota((width, slots), 0) // DH
     head_col = iota((slots, width), 1) // DH
-    qt_half = (jnp.transpose(q) * (0.5 * DH ** (-0.5))).astype(BF16)
+    qt_half = (jnp.transpose(q).astype(F32) * (0.5 * DH ** (-0.5))).astype(BF16)
     zero = jnp.zeros((), BF16)
     qt_of = [jnp.where(head_row == h, qt_half, zero) for h in range(heads)]
-    att = [jnp.zeros((DH, slots), F32)] * heads
+    cols_of = [slice(h * slots, (h + 1) * slots) for h in range(heads)]
+    mine_of = [slice(h * DH, (h + 1) * DH) for h in range(heads)]
     for start in range(0, events, BLOCK):
         at = pl.ds(start, BLOCK)
         visible = (iota((BLOCK, slots), 0) + start).astype(F32) < length
         for h in range(heads):
-            cols = slice(h * slots, (h + 1) * slots)
             half = nn(k_ref[at, :], qt_of[h])
             twice = jnp.where(visible, jnp.tanh(half) + 1.0, 0.0)
             weights = half * twice
-            s_scr[at, cols] = (twice + weights * (2.0 - twice)).astype(BF16)
-            weights = weights.astype(BF16)
-            weights_out.buffer[at, cols] = weights
-            att[h] += nn(vt_ref[h * DH : (h + 1) * DH, at], weights)
+            s_scr[at, cols_of[h]] = (twice + weights * (2.0 - twice)).astype(BF16)
+            weights_out.buffer[at, cols_of[h]] = weights.astype(BF16)
         weights_out.send_part((at,))
+    att = [nn(vt_ref[mine_of[h], :], weights_out.buffer[:, cols_of[h]]) for h in range(heads)]
     att = jnp.concatenate(att, axis=0).reshape(heads, DH, slots)
     inverse = lax.rsqrt(jnp.mean(att * att, axis=1, keepdims=True) + EPSILON)
     normed = att * inverse
-    dnt = jnp.transpose(dn).reshape(heads, DH, slots)
+    dnt = jnp.transpose(dn).astype(F32).reshape(heads, DH, slots)
     d_att = inverse * (dnt - normed * jnp.mean(dnt * normed, axis=1, keepdims=True))
-    d_att = d_att.reshape(width, slots)
-    d_att_t = d_att.astype(BF16)
-    d_att_out.buffer[...] = jnp.transpose(d_att).astype(BF16)
+    d_att = d_att.reshape(width, slots).astype(BF16)
+    d_att_out.buffer[...] = jnp.transpose(d_att)
     d_att_out.send()
-    normed = jnp.transpose(normed.reshape(width, slots))
-    dt_of = [jnp.where(head_row == h, d_att_t, zero) for h in range(heads)]
-    q_bf = q.astype(BF16)
-    q_of = jnp.concatenate([jnp.where(head_col == h, q_bf, zero) for h in range(heads)], axis=0)
+    normed = jnp.transpose(normed.reshape(width, slots).astype(BF16)).astype(F32)
+    dt_of = [jnp.where(head_row == h, d_att, zero) for h in range(heads)]
+    q_of = jnp.concatenate([jnp.where(head_col == h, q, zero) for h in range(heads)], axis=0)
     v_ref, kt_ref = v_in.get(), kt_in.get()
-    d_query = [jnp.zeros((DH, slots), F32)] * heads
     for start in range(0, events, BLOCK):
         at = pl.ds(start, BLOCK)
         for h in range(heads):
-            cols = slice(h * slots, (h + 1) * slots)
-            ds = (nn(v_ref[at, :], dt_of[h]) * s_scr[at, cols].astype(F32)).astype(BF16)
-            s_scr[at, cols] = ds
-            d_query[h] += nn(kt_ref[h * DH : (h + 1) * DH, at], ds)
+            ds = nn(v_ref[at, :], dt_of[h]) * s_scr[at, cols_of[h]].astype(F32)
+            s_scr[at, cols_of[h]] = ds.astype(BF16)
         d_keys = nn(s_scr[at, :], q_of) * (0.5 * DH ** (-0.5))
         d_keys_out.buffer[at, :] = d_keys.astype(BF16)
         d_keys_out.send_part((at,))
-    d_query = jnp.concatenate(d_query, axis=0) * (0.5 * DH ** (-0.5))
-    back_out.buffer[...] = spread([jnp.transpose(d_query), normed]).astype(BF16)
+    d_query = [nn(kt_ref[mine_of[h], :], s_scr[:, cols_of[h]]) for h in range(heads)]
+    d_query = (jnp.concatenate(d_query, axis=0) * (0.5 * DH ** (-0.5))).astype(BF16)
+    back_out.buffer[...] = spread([jnp.transpose(d_query).astype(F32), normed]).astype(BF16)
 
 
 def history_kernel(
@@ -182,7 +180,7 @@
 ):
     late, rest = rest[:LATE], rest[LATE:]
     gkv_out, mine_out, other_out, rest = rest[0], rest[1], rest[2], rest[3:]
-    kept, (scr, w_scr, term_scr, sems, late_sems) = rest[:LATE], rest[LATE:]
+    kept, (scr, w_scr, term_scr, ev_scr, sems, ev_sem, late_sems) = rest[:LATE], rest[LATE:]
     events = w_scr.shape[0]
     step = events // HISTORY_PARTS
     parts = [pl.ds(b * step, step) for b in range(HISTORY_PARTS)]
@@ -192,6 +190,8 @@
     ]
     for copy in copies:
         copy.start()
+    ev_copy = pltpu.make_async_copy(ev_in.get(), ev_scr, ev_sem)
+    ev_copy.start()
     moves = [
         pltpu.make_async_copy(src.get().at[: dst.buffer.shape[0]], dst.buffer, late_sems.at[i])
         for i, (src, dst) in enumerate(zip(late, kept))
@@ -208,13 +208,14 @@
     for at, copy in zip(parts, copies):
         d_keys = d_keys_ref[at, :]
         gkv_ref[at, :width] = d_keys
-        term_scr[at, :width] = (d_keys.astype(F32) * slope_ref[at, :]).astype(BF16)
+        term_scr[at, :width] = (d_keys.astype(F32) * slope_ref[at, :].astype(F32)).astype(BF16)
         copy.wait()
         d_values = nn(w_scr[at, :], d_of).astype(BF16)
         gkv_ref[at, width:] = d_values
         gkv_out.send_part((at,))
         term_scr[at, width:] = d_values
-    both = jnp.transpose(tn(term_scr[...], ev_in.get()[...]))
+    ev_copy.wait()
+    both = jnp.transpose(tn(term_scr[...], ev_scr[...]))
     rows = spread([both[:, :width], both[:, width:]]).astype(BF16)
     split_halves(core_ref[0], rows, scr, mine_out, other_out)
     for move in moves:
@@ -230,7 +231,10 @@
     mine_out.buffer[...] = scr[core]
 
 
-def post_kernel(core_ref, back_in, place_in, aux_in, x_in, w_in, gy_in, mine_out, other_out, gx_out, scr):
+def post_kernel(
+    core_ref, back_in, kv_mine_in, kv_other_in, place_in, aux_in, x_in, w_in, gy_in,
+    mine_out, other_out, gx_out, scr,
+):
     place = place_in.get()[...]
     back_ref, aux_ref, w_ref = back_in.get(), aux_in.get(), w_in.get()
     slots = place.shape[0]
@@ -253,18 +257,28 @@
     gg = tn(x, g_term)
     go = tn(gated, gy_in.get()[...])
     go = jnp.concatenate([go[:, i * width : (i + 1) * width] for i in range(go.shape[1] // width)], axis=0)
-    split_halves(core_ref[0], spread([gq, gg, go]).astype(BF16), scr, mine_out, other_out)
-
-
-def pair_kernel(a_in, b_in, c_in, d_in, out):
-    width = a_in.buffer.shape[1]
-    first = a_in.get()[...].astype(F32) + b_in.get()[...].astype(F32)
-    second = c_in.get()[...].astype(F32) + d_in.get()[...].astype(F32)
-    chunks = first.shape[0] // 16
+    out = spread([gq, gg, go])
+    half = out.shape[0] // 2
+    scr[0] = out[:half]
+    scr[1] = out[half:]
+    core = core_ref[0]
+    other_out.buffer[...] = scr[1 - core].astype(BF16)
+    chunks = half // 24
+    pair = kv_mine_in.get()[...].astype(F32) + kv_other_in.get()[...].astype(F32)
     joined = jnp.concatenate(
-        [first.reshape(chunks, 16, width), second.reshape(chunks, 24, width)], axis=1
-    )
-    out.buffer[...] = joined.reshape(chunks * 40, width).astype(BF16)
+        [pair.reshape(chunks, 16, width), scr[core].reshape(chunks, 24, width)], axis=1
+    )
+    mine_out.buffer[...] = joined.reshape(chunks * 40, width).astype(BF16)
+
+
+def pair_kernel(mine_in, other_in, out):
+    width = other_in.buffer.shape[1]
+    other = other_in.get()[...].astype(F32)
+    chunks = other.shape[0] // 24
+    other = other.reshape(chunks, 24, width)
+    other = jnp.concatenate([jnp.zeros((chunks, 16, width), F32), other], axis=1)
+    total = mine_in.get()[...].astype(F32) + other.reshape(chunks * 40, width)
+    out.buffer[...] = total.astype(BF16)
 
 
 def sum_kernel(factor, rows_in, out):
@@ -276,22 +290,45 @@
     out.buffer[...] = jnp.broadcast_to(total[None], (chunks, 40, shape[1])).reshape(shape).astype(BF16)
 
 
-def unfold_kernel(core_ref, mine_in, other_in, win_out, wout_out, scr):
-    win_ref, wout_ref = win_out.buffer, wout_out.buffer
-    width = mine_in.buffer.shape[1]
-    core = core_ref[0]
-    for source, which in ((mine_in, core), (other_in, 1 - core)):
-        got = source.get()[...].astype(F32)
-        chunks = got.shape[0] // 40
-        got = got.reshape(chunks, 5, 8, width)
-        size = chunks * 8
-        at = pl.ds(pl.multiple_of(which * size, size), size)
-        for place, index in enumerate((2, 3, 0, 1)):
-            win_ref[index, at, :] = got[:, place].reshape(size, width)
-        scr[at, :] = got[:, 4].reshape(size, width)
-    rows = wout_ref.shape[0]
-    for i in range(wout_ref.shape[1] // width):
-        wout_ref[:, i * width : (i + 1) * width] = scr[i * rows : (i + 1) * rows, :]
+def unfold_kernel(which_ref, source_ref, *refs):
+    win_ref, wout_ref, win_scr, wout_scr, sems = refs[-5:]
+    got = source_ref[...].astype(F32)
+    width = got.shape[1]
+    chunks = got.shape[0] // 40
+    size = chunks * 8
+    got = got.reshape(chunks, 5, 8, width)
+    at = pl.ds(pl.multiple_of(which_ref[0] * size, size), size)
+    copies = []
+    for place, index in enumerate((2, 3, 0, 1)):
+        win_scr[index] = got[:, place].reshape(size, width)
+        copies.append(pltpu.make_async_copy(win_scr.at[index], win_ref.at[index, at], sems.at[place]))
+        copies[-1].start()
+    last = got[:, 4].reshape(size, width)
+    rows = wout_scr.shape[0]
+    for i in range(size // rows):
+        wout_scr[:, i * width : (i + 1) * width] = last[i * rows : (i + 1) * rows]
+    copies.append(pltpu.make_async_copy(wout_scr, wout_ref.at[:, at], sems.at[4]))
+    copies[-1].start()
+    for copy in copies:
+        copy.wait()
+
+
+def unfold(which, source, depth, filled=()):
+    width = source.shape[1]
+    return pl.pallas_call(
+        unfold_kernel,
+        out_shape=[pltpu.HBM((4, depth, width), F32), pltpu.HBM((width, depth), F32)],
+        in_specs=[SMEM, VMEM] + [ANY] * len(filled),
+        out_specs=[ANY, ANY],
+        scratch_shapes=[
+            pltpu.VMEM((4, depth // 2, width), F32),
+            pltpu.VMEM((width, depth // 2), F32),
+            pltpu.SemaphoreType.DMA((5,)),
+        ],
+        input_output_aliases={2 + i: i for i in range(len(filled))},
+        compiler_params=PARAMS,
+        cost_estimate=pl.CostEstimate(flops=0, bytes_accessed=1 << 20, transcendentals=0),
+    )(which, source, *filled)
 
 
 class Load:
@@ -411,6 +448,8 @@
         pre_kernel,
         [((3 * slots, width), BF16)],
         (hist_rows, imp_len.reshape(1, rows), owner_row, imp_x, w_in, w_out, grad_y),
+        scratch=[pltpu.VMEM((2,) + w_in.shape[1:], BF16), pltpu.SemaphoreType.DMA(())],
+        raw_in=(4,),
         near_out=(0,),
         flops=2 * rows * depth * width * 3,
         moved=1 << 20,
@@ -423,7 +462,7 @@
             ((width, events), BF16),
             ((events, width), BF16),
             ((width, events), BF16),
-            ((events, width), F32),
+            ((events, width), BF16),
             ((4, rows, width), F32),
             ((slots, rows), BF16),
         ],
@@ -462,10 +501,12 @@
             pltpu.VMEM((2, half, width), BF16),
             pltpu.VMEM((events, heads * slots), BF16),
             pltpu.VMEM((events, 2 * width), BF16),
+            pltpu.VMEM((events, depth), BF16),
             pltpu.SemaphoreType.DMA((HISTORY_PARTS,)),
+            pltpu.SemaphoreType.DMA(()),
             pltpu.SemaphoreType.DMA((LATE,)),
         ],
-        raw_in=(3, 5, 6, 7, 8, 9),
+        raw_in=(3, 4, 5, 6, 7, 8, 9),
         near_out=(1, 2, 3, 4, 5, 6, 7),
         flops=4 * events * depth * width + 2 * events * slots * width,
         moved=10 << 20,
@@ -475,11 +516,11 @@
     half = depth * 3 // 2
     mine, other, gx = call(
         post_kernel,
-        [((half, width), BF16)] * 2 + [((rows, depth), BF16)],
-        (back, place, aux, x_near, w_near, gy_near),
+        [((chips * 40, width), BF16), ((half, width), BF16), ((rows, depth), BF16)],
+        (back, kv_mine, kv_other, place, aux, x_near, w_near, gy_near),
         (core,),
-        scratch=[pltpu.VMEM((2, half, width), BF16)],
-        near_in=(0, 1, 2, 3, 4, 5),
+        scratch=[pltpu.VMEM((2, half, width), F32)],
+        near_in=(0, 1, 2, 3, 4, 5, 6, 7),
         near_out=(0, 1, 2),
         flops=2 * rows * depth * width * 5,
         moved=2 << 20,
@@ -488,8 +529,8 @@
     (summed,) = call(
         pair_kernel,
         [((chips * 40, width), BF16)],
-        (kv_mine, kv_other, mine, other),
-        near_in=(0, 1, 2, 3),
+        (mine, other),
+        near_in=(0, 1),
         near_out=(0,),
         moved=1 << 20,
     )
@@ -500,7 +541,8 @@
         part = lax.dynamic_slice_in_dim(gx, (plane + step) % planes * share, share, 0)
         parts.append(lax.ppermute(part, "mp", [(i, (i + step) % planes) for i in range(planes)]))
     factor = (rows * owners) ** (-0.5)
-    summed, *parts = lax.optimization_barrier((exchange_core(summed), *parts))
+    grad_kv = gkv.reshape(1, events, 2, width)
+    summed, grad_kv, *parts = lax.optimization_barrier((exchange_core(summed), grad_kv, *parts))
     total = lax.dynamic_slice_in_dim(gx, plane * share, share, 0).astype(F32)
     for part in parts:
         total = total + part.astype(F32)
@@ -513,18 +555,11 @@
         near_out=(0,),
         moved=1 << 20,
     )
+    piece, grad_x = lax.optimization_barrier((piece, grad_x))
     mine = exchange_core(piece)
     other = swap(mine)
-    grad_w_in, grad_w_out = call(
-        unfold_kernel,
-        [((4, depth, width), F32), ((width, depth), F32)],
-        (mine, other),
-        (core,),
-        scratch=[pltpu.VMEM((depth, width), F32)],
-        near_in=(0, 1),
-        moved=3 << 20,
-    )
-    grad_kv = gkv.reshape(1, events, 2, width)
+    filled = unfold(core, mine, depth)
+    grad_w_in, grad_w_out = unfold(1 - core, other, depth, filled)
     return (grad_x, grad_kv, grad_w_in, grad_w_out)
 
 

time: 102 us -> 100 us (0.980)
  waiting for transfers between devices: 25.2 us -> 23.8 us
  Pallas kernels: 25.5 us -> 24.3 us
  local copies, waits for them, and re-layouts: 1.11 us -> 2.15 us
    pallas_call x8 -> x7, Pallas kernels: 25.5 us -> 22.5 us  [call(): pl.pallas_call(body, out_shape=[jax.ShapeDtypeStruct(s, d) if i in near_o...]
    ppermute x3, waiting for transfers between devices: 1.99 us -> 0.01 us  [on_device(): lax.ppermute(part, 'mp', [(i, (i + step) % planes) for i in range(planes)])]
    pallas_call x0 -> x2, Pallas kernels: none -> 1.76 us  [unfold(): pl.pallas_call(unfold_kernel, out_shape=[pltpu.HBM((4, depth, width), F32...]
    reshape x1, local copies, waits for them, and re-layouts: 1.09 us -> 2.13 us  [on_device(): grad_kv = gkv.reshape(1, events, 2, width)]
  transfers between devices with their start and end apart: 9 -> 9, of which waited for: 7 -> 6; matrix products, arithmetic and copies ran while one was open for 2% -> 2% of each run, Pallas kernels for 11% -> 12%
where the time goes in v5:
time: 100 us; the launch traced here: 99.9 us
  starting transfers between devices  32.3 us (32%)
  Pallas kernels  24.3 us (24%)
  waiting for transfers between devices  23.8 us (24%)
  blocking collectives  15.8 us (16%)
  local copies, waits for them, and re-layouts  2.15 us (2%)
    pallas_call x7, Pallas kernels, call(): pl.pallas_call(body, out_shape=[jax.ShapeDtypeStruct(s, d) if i in near_o...  22.5 us
    all_to_all x2, starting transfers between devices, exchange(): a = lax.all_to_all(a, 'dp', 0, 0, tiled=True)  18.6 us
    all_to_all x2, waiting for transfers between devices, exchange(): a = lax.all_to_all(a, 'dp', 0, 0, tiled=True)  15.8 us
    all_to_all x1, blocking collectives, exchange_core(): a = lax.all_to_all(a, 'dp', 0, 0, axis_index_groups=same_core, tiled=True)  15.8 us
    all_to_all x1, waiting for transfers between devices, exchange_core(): a = lax.all_to_all(a, 'dp', 0, 0, axis_index_groups=same_core, tiled=True)  5.47 us
    ppermute x3, starting transfers between devices, on_device(): lax.ppermute(part, 'mp', [(i, (i + step) % planes) for i in range(planes)])  5.06 us
    ppermute x3, starting transfers between devices, swap(): return lax.ppermute(a, 'dp', pairs)  4.74 us
    all_to_all x1, starting transfers between devices, exchange_core(): a = lax.all_to_all(a, 'dp', 0, 0, axis_index_groups=same_core, tiled=True)  3.91 us
  transfers between devices with their start and end apart: 9, of which 6 were waited for; matrix products, arithmetic and copies ran while one was open for 2% of the time, Pallas kernels for 12%

profile of v5, /device:TPU:1, one launch (start us, length us, event | category | flops | bytes accessed | tf_op | source)
XLA Modules:
  0.0 99.9 jit_solution(497896841246649829)
XLA Ops:
  0.6 2.6 %shard_map.111 = bf16[1536,128]{1,0:T(8,128)(2,1)} custom-call(s32[1,128]{1,0:T(1,128)} %bitcast.21, s32[1,128]{1,0:T(1,128)} %bitcast.25, s32[1,64]{1,0:T(1,128)} %bitcast.23, bf16[128,512]{1,0:T(8,128)(2,1)} %refs_8_.1, bf16[4,512,128]{2,1,0:T(8,128)(2,1)} %refs_9_.1, bf16[128,512]{1,0:T(8,128)(2,1)} %refs_5_.3, bf16[128,512]{1,0:T(8,128)(2,1)} %refs_10_.1), custom_call_target="tpu_custom_call" | custom-call | flops 50331648 | bytes 1048576 | tf_op jit(solution)/shard_map/pallas_call | solution.py:402
  3.3 13.0 %all-to-all-start = ((bf16[64,24,128]{2,1,0:T(8,128)(2,1)}), bf16[64,24,128]{2,1,0:T(8,128)(2,1)S(1)}, u32[]{:S(2)}, u32[]{:S(2)}) async-start(bf16[64,24,128]{2,1,0:T(8,128)(2,1)} %bitcast.4), calls=%async_computation | async-start | bytes 786432 | tf_op jit(solution)/shard_map/all_to_all | solution.py:437
  16.3 4.8 %shard_map.112 = (bf16[2048,128]{1,0:T(8,128)(2,1)S(1)}, bf16[128,2048]{1,0:T(8,128)(2,1)S(1)}, bf16[2048,128]{1,0:T(8,128)(2,1)}, bf16[128,2048]{1,0:T(8,128)(2...) custom-call(bf16[4,512,128]{2,1,0:T(8,128)(2,1)} %refs_9_.1, ...), custom_call_target="tpu_custom_call" | custom-call | flops 536870912 | bytes 5242880 | tf_op jit(solution)/shard_map/pallas_call | solution.py:402
  21.0 10.3 %all-to-all-done = bf16[64,24,128]{2,1,0:T(8,128)(2,1)S(1)} async-done(((bf16[64,24,128]{2,1,0:T(8,128)(2,1)}), bf16[64,24,128]{2,1,0:T(8,128)(2,1)S(1)}, u32[]{:S(2)}, u32[]{:S(2)}) %all-to-all-start) | async-done | bytes 393248 | tf_op jit(solution)/shard_map/all_to_all | solution.py:437
  31.3 7.6 %shard_map.113 = (bf16[1024,128]{1,0:T(8,128)(2,1)}, bf16[2048,1024]{1,0:T(8,128)(2,1)}, bf16[2048,128]{1,0:T(8,128)(2,1)}, bf16[512,128]{1,0:T(8,128)(2,1)}) custom-call(bf16[1536,128]{1,0:T(8,128)(2,1)S(1)} %bitcast.18, bf16[2048,128]{1,0:T(8,128)(2,1)S(1)} %get-tuple-element.40.refs_1_, bf16[128,2048]{1,0:T(8,128)(2,1)S(1)} %get-tuple-element.41.refs_2_, ...), custom_call_target="tpu_custom_call" | custom-call | flops 1342177280 | bytes 8388608 | tf_op jit(solution)/shard_map/pallas_call | solution.py:402
  39.0 5.6 %all-to-all-start.1 = ((bf16[64,16,128]{2,1,0:T(8,128)(2,1)}), bf16[64,16,128]{2,1,0:T(8,128)(2,1)S(1)}, u32[]{:S(2)}, u32[]{:S(2)}) async-start(bf16[64,16,128]{2,1,0:T(8,128)(2,1)} %bitcast.7), calls=%async_computation.1 | async-start | bytes 524288 | tf_op jit(solution)/shard_map/all_to_all | solution.py:437
  44.6 5.9 %shard_map.114 = (bf16[2048,256]{1,0:T(8,128)(2,1)}, bf16[512,128]{1,0:T(8,128)(2,1)S(1)}, bf16[512,128]{1,0:T(8,128)(2,1)S(1)}, bf16[512,128]{1,0:T(8,128)(2,1)...) custom-call(s32[1]{0:T(128)} %bitcast.refs_0_.which_ref, ...), custom_call_target="tpu_custom_call" | custom-call | flops 805306368 | bytes 10485760 | tf_op jit(solution)/shard_map/pallas_call | solution.py:402
  50.5 0.7 collective-permute-start
  51.2 1.0 collective-permute-done.refs_3_
  52.2 5.5 %all-to-all-done.1 = bf16[64,16,128]{2,1,0:T(8,128)(2,1)S(1)} async-done(((bf16[64,16,128]{2,1,0:T(8,128)(2,1)}), bf16[64,16,128]{2,1,0:T(8,128)(2,1)S(1)}, u32[]{:S(2)}, u32[]{:S(2)}) %all-to-all-start.1) | async-done | bytes 262176 | tf_op jit(solution)/shard_map/all_to_all | solution.py:437
  57.7 0.7 shard_map.115
  58.4 0.3 collective-permute-start.1
  58.8 1.2 %collective-permute-done.1.refs_1_ = bf16[768,128]{1,0:T(8,128)(2,1)S(1)} collective-permute-done((bf16[768,128]{1,0:T(8,128)(2,1)S(1)}, bf16[768,128]{1,0:T(8,128)(2,1)S(1)}, u32[]{:S(2)}, u32[]{:S(2)}) %collective-permute-start.1) | collective-permute-done | bytes 196640 | tf_op jit(solution)/shard_map/ppermute | solution.py:433
  60.0 0.8 shard_map.116
  60.8 3.9 %all-to-all-start.2 = ((bf16[32,40,128]{2,1,0:T(8,128)(2,1)}), bf16[32,40,128]{2,1,0:T(8,128)(2,1)S(1)}, u32[]{:S(2)}, u32[]{:S(2)}) async-start(bf16[32,40,128]{2,1,0:T(8,128)(2,1)} %bitcast.9), calls=%async_computation.2 | async-start | bytes 655360 | tf_op jit(solution)/shard_map/all_to_all | solution.py:442
  64.8 1.4 %collective-permute-start.2 = (bf16[32,512]{1,0:T(8,128)(2,1)S(1)}, bf16[32,512]{1,0:T(8,128)(2,1)S(1)}, u32[]{:S(2)}, u32[]{:S(2)}) collective-permute-start(bf16[32,512]{1,0:T(8,128)(2,1)S(1)} %get-tuple-element.78), channel_id=1, source_target_pairs={{0,1},{1,2},{2,3},{3,0},{4,5},{5,6},{6,7},{7,4},{8,9},{9,10},{10,1... | collective-permute-start | bytes 98312 | tf_op jit(solution)/shard_map/ppermute | solution.py:542
  66.1 2.6 %collective-permute-start.3 = (bf16[32,512]{1,0:T(8,128)(2,1)S(1)}, bf16[32,512]{1,0:T(8,128)(2,1)S(1)}, u32[]{:S(2)}, u32[]{:S(2)}) collective-permute-start(bf16[32,512]{1,0:T(8,128)(2,1)S(1)} %get-tuple-element.77), channel_id=1, source_target_pairs={{0,2},{1,3},{2,0},{3,1},{4,6},{5,7},{6,4},{7,5},{8,10},{9,11},{10,... | collective-permute-start | bytes 98312 | tf_op jit(solution)/shard_map/ppermute | solution.py:542
  68.8 1.1 %collective-permute-start.4 = (bf16[32,512]{1,0:T(8,128)(2,1)S(1)}, bf16[32,512]{1,0:T(8,128)(2,1)S(1)}, u32[]{:S(2)}, u32[]{:S(2)}) collective-permute-start(bf16[32,512]{1,0:T(8,128)(2,1)S(1)} %get-tuple-element.76), channel_id=1, source_target_pairs={{0,3},{1,0},{2,1},{3,2},{4,7},{5,4},{6,5},{7,6},{8,11},{9,8},{10,9... | collective-permute-start | bytes 98312 | tf_op jit(solution)/shard_map/ppermute | solution.py:542
  69.8 2.1 %reshape.57 = bf16[1,2048,2,128]{3,2,1,0:T(2,128)(2,1)} reshape(bf16[2048,256]{1,0:T(8,128)(2,1)} %get-tuple-element.63) | data formatting | bytes 2097152 | tf_op jit(solution)/shard_map/reshape | solution.py:544
  72.0 0.0 collective-permute-done.2
  72.0 0.0 collective-permute-done.3
  72.0 0.0 collective-permute-done.4
  72.0 5.5 %all-to-all-done.2 = bf16[32,40,128]{2,1,0:T(8,128)(2,1)S(1)} async-done(((bf16[32,40,128]{2,1,0:T(8,128)(2,1)}), bf16[32,40,128]{2,1,0:T(8,128)(2,1)S(1)}, u32[]{:S(2)}, u32[]{:S(2)}) %all-to-all-start.2) | async-done | bytes 327712 | tf_op jit(solution)/shard_map/all_to_all | solution.py:442
  77.4 0.1 shard_map.117
  77.5 0.6 add_convert_fusion
  78.2 15.8 %all_to_all.20 = bf16[32,40,128]{2,1,0:T(8,128)(2,1)S(1)} all-to-all(bf16[32,40,128]{2,1,0:T(8,128)(2,1)S(1)} %bitcast.16), channel_id=1, replica_groups={{0,8,16,24,32,40,48,56,64,72,80,88,96,104,112,120,128,136,144,152,160,1..., dimensions={0} | all-to-all | bytes 655360 | tf_op jit(solution)/shard_map/all_to_all | solution.py:442
  94.0 3.7 %collective-permute-start.5 = (bf16[1280,128]{1,0:T(8,128)(2,1)S(1)}, bf16[1280,128]{1,0:T(8,128)(2,1)S(1)}, u32[]{:S(2)}, u32[]{:S(2)}) collective-permute-start(bf16[1280,128]{1,0:T(8,128)(2,1)S(1)} %bitcast.14), channel_id=1, source_target_pairs={{0,4},{4,0},{8,12},{12,8},{16,20},{20,16},{24,28},{28,24},{32,36},... | collective-permute-start | bytes 983048 | tf_op jit(solution)/shard_map/ppermute | solution.py:433
  97.6 0.9 shard_map.118
  98.5 0.4 collective-permute-done.5.source_ref
  98.9 0.9 shard_map.119
  (1 shorter events, 0.0 us)
Async XLA Ops:
  3.3 28.1 %all-to-all-start = ((bf16[64,24,128]{2,1,0:T(8,128)(2,1)}), bf16[64,24,128]{2,1,0:T(8,128)(2,1)S(1)}, u32[]{:S(2)}, u32[]{:S(2)}) async-start(bf16[64,24,128]{2,1,0:T(8,128)(2,1)} %bitcast.4), calls=%async_computation | async-start | bytes 786432 | tf_op jit(solution)/shard_map/all_to_all | solution.py:437
  39.0 18.8 %all-to-all-start.1 = ((bf16[64,16,128]{2,1,0:T(8,128)(2,1)}), bf16[64,16,128]{2,1,0:T(8,128)(2,1)S(1)}, u32[]{:S(2)}, u32[]{:S(2)}) async-start(bf16[64,16,128]{2,1,0:T(8,128)(2,1)} %bitcast.7), calls=%async_computation.1 | async-start | bytes 524288 | tf_op jit(solution)/shard_map/all_to_all | solution.py:437
  50.5 1.7 %collective-permute-start = (bf16[512,128]{1,0:T(8,128)(2,1)S(1)}, bf16[512,128]{1,0:T(8,128)(2,1)S(1)}, u32[]{:S(2)}, u32[]{:S(2)}) collective-permute-start(bf16[512,128]{1,0:T(8,128)(2,1)S(1)} %get-tuple-element.52), channel_id=1, source_target_pairs={{0,4},{4,0},{8,12},{12,8},{16,20},{20,16},{24,28},{28,24},{32,36},... | collective-permute-start | bytes 393224 | tf_op jit(solution)/shard_map/ppermute | solution.py:433
  58.4 1.5 %collective-permute-start.1 = (bf16[768,128]{1,0:T(8,128)(2,1)S(1)}, bf16[768,128]{1,0:T(8,128)(2,1)S(1)}, u32[]{:S(2)}, u32[]{:S(2)}) collective-permute-start(bf16[768,128]{1,0:T(8,128)(2,1)S(1)} %get-tuple-element.62), channel_id=1, source_target_pairs={{0,4},{4,0},{8,12},{12,8},{16,20},{20,16},{24,28},{28,24},{32,36},... | collective-permute-start | bytes 589832 | tf_op jit(solution)/shard_map/ppermute | solution.py:433
  60.8 16.7 %all-to-all-start.2 = ((bf16[32,40,128]{2,1,0:T(8,128)(2,1)}), bf16[32,40,128]{2,1,0:T(8,128)(2,1)S(1)}, u32[]{:S(2)}, u32[]{:S(2)}) async-start(bf16[32,40,128]{2,1,0:T(8,128)(2,1)} %bitcast.9), calls=%async_computation.2 | async-start | bytes 655360 | tf_op jit(solution)/shard_map/all_to_all | solution.py:442
  64.8 7.2 %collective-permute-start.2 = (bf16[32,512]{1,0:T(8,128)(2,1)S(1)}, bf16[32,512]{1,0:T(8,128)(2,1)S(1)}, u32[]{:S(2)}, u32[]{:S(2)}) collective-permute-start(bf16[32,512]{1,0:T(8,128)(2,1)S(1)} %get-tuple-element.78), channel_id=1, source_target_pairs={{0,1},{1,2},{2,3},{3,0},{4,5},{5,6},{6,7},{7,4},{8,9},{9,10},{10,1... | collective-permute-start | bytes 98312 | tf_op jit(solution)/shard_map/ppermute | solution.py:542
  66.1 5.8 %collective-permute-start.3 = (bf16[32,512]{1,0:T(8,128)(2,1)S(1)}, bf16[32,512]{1,0:T(8,128)(2,1)S(1)}, u32[]{:S(2)}, u32[]{:S(2)}) collective-permute-start(bf16[32,512]{1,0:T(8,128)(2,1)S(1)} %get-tuple-element.77), channel_id=1, source_target_pairs={{0,2},{1,3},{2,0},{3,1},{4,6},{5,7},{6,4},{7,5},{8,10},{9,11},{10,... | collective-permute-start | bytes 98312 | tf_op jit(solution)/shard_map/ppermute | solution.py:542
  68.8 3.2 %collective-permute-start.4 = (bf16[32,512]{1,0:T(8,128)(2,1)S(1)}, bf16[32,512]{1,0:T(8,128)(2,1)S(1)}, u32[]{:S(2)}, u32[]{:S(2)}) collective-permute-start(bf16[32,512]{1,0:T(8,128)(2,1)S(1)} %get-tuple-element.76), channel_id=1, source_target_pairs={{0,3},{1,0},{2,1},{3,2},{4,7},{5,4},{6,5},{7,6},{8,11},{9,8},{10,9... | collective-permute-start | bytes 98312 | tf_op jit(solution)/shard_map/ppermute | solution.py:542
  94.0 4.9 %collective-permute-start.5 = (bf16[1280,128]{1,0:T(8,128)(2,1)S(1)}, bf16[1280,128]{1,0:T(8,128)(2,1)S(1)}, u32[]{:S(2)}, u32[]{:S(2)}) collective-permute-start(bf16[1280,128]{1,0:T(8,128)(2,1)S(1)} %bitcast.14), channel_id=1, source_target_pairs={{0,4},{4,0},{8,12},{12,8},{16,20},{20,16},{24,28},{28,24},{32,36},... | collective-permute-start | bytes 983048 | tf_op jit(solution)/shard_map/ppermute | solution.py:433

commit v6 on v5

--- a/solution.py
+++ b/solution.py
@@ -1,3 +1,5 @@
+import functools
+
 import jax
 import jax.numpy as jnp
 from jax import lax
@@ -262,23 +264,15 @@
     scr[0] = out[:half]
     scr[1] = out[half:]
     core = core_ref[0]
-    other_out.buffer[...] = scr[1 - core].astype(BF16)
-    chunks = half // 24
-    pair = kv_mine_in.get()[...].astype(F32) + kv_other_in.get()[...].astype(F32)
-    joined = jnp.concatenate(
-        [pair.reshape(chunks, 16, width), scr[core].reshape(chunks, 24, width)], axis=1
-    )
-    mine_out.buffer[...] = joined.reshape(chunks * 40, width).astype(BF16)
+    for kv_in, which, result in ((kv_other_in, 1 - core, other_out), (kv_mine_in, core, mine_out)):
+        chunks = half // 24
+        kv = kv_in.get()[...].astype(F32).reshape(chunks, 16, width)
+        joined = jnp.concatenate([kv, scr[which].reshape(chunks, 24, width)], axis=1)
+        result.buffer[...] = joined.reshape(chunks * 40, width).astype(BF16)
 
 
 def pair_kernel(mine_in, other_in, out):
-    width = other_in.buffer.shape[1]
-    other = other_in.get()[...].astype(F32)
-    chunks = other.shape[0] // 24
-    other = other.reshape(chunks, 24, width)
-    other = jnp.concatenate([jnp.zeros((chunks, 16, width), F32), other], axis=1)
-    total = mine_in.get()[...].astype(F32) + other.reshape(chunks * 40, width)
-    out.buffer[...] = total.astype(BF16)
+    out.buffer[...] = (mine_in.get()[...].astype(F32) + other_in.get()[...].astype(F32)).astype(BF16)
 
 
 def sum_kernel(factor, rows_in, out):
@@ -290,8 +284,17 @@
     out.buffer[...] = jnp.broadcast_to(total[None], (chunks, 40, shape[1])).reshape(shape).astype(BF16)
 
 
-def unfold_kernel(which_ref, source_ref, *refs):
-    win_ref, wout_ref, win_scr, wout_scr, sems = refs[-5:]
+def unfold_kernel(shares, which_ref, source_ref, *refs):
+    if shares:
+        share_refs, refs = refs[:shares], refs[shares:]
+        gx_ref, win_ref, wout_ref, win_scr, wout_scr, sems, share_scr, gx_scr, gx_sems = refs
+        loads = [
+            pltpu.make_async_copy(share, share_scr.at[i], gx_sems.at[i]) for i, share in enumerate(share_refs)
+        ]
+        for load in loads:
+            load.start()
+    else:
+        win_ref, wout_ref, win_scr, wout_scr, sems = refs[2:]
     got = source_ref[...].astype(F32)
     width = got.shape[1]
     chunks = got.shape[0] // 40
@@ -309,26 +312,42 @@
         wout_scr[:, i * width : (i + 1) * width] = last[i * rows : (i + 1) * rows]
     copies.append(pltpu.make_async_copy(wout_scr, wout_ref.at[:, at], sems.at[4]))
     copies[-1].start()
+    if shares:
+        for load in loads:
+            load.wait()
+        gx_scr[...] = jnp.sum(share_scr[...].astype(F32), axis=0).astype(BF16)
+        copies.append(pltpu.make_async_copy(gx_scr, gx_ref, gx_sems.at[shares]))
+        copies[-1].start()
     for copy in copies:
         copy.wait()
 
 
-def unfold(which, source, depth, filled=()):
+def unfold(which, source, depth, shares=(), filled=()):
     width = source.shape[1]
+    results = [pltpu.HBM((4, depth, width), F32), pltpu.HBM((width, depth), F32)]
+    scratch = [
+        pltpu.VMEM((4, depth // 2, width), F32),
+        pltpu.VMEM((width, depth // 2), F32),
+        pltpu.SemaphoreType.DMA((5,)),
+    ]
+    if shares:
+        shape, count = shares[0].shape, len(shares)
+        results = [pltpu.HBM(shape, BF16)] + results
+        scratch += [
+            pltpu.VMEM((count,) + shape, BF16),
+            pltpu.VMEM(shape, BF16),
+            pltpu.SemaphoreType.DMA((count + 1,)),
+        ]
     return pl.pallas_call(
-        unfold_kernel,
-        out_shape=[pltpu.HBM((4, depth, width), F32), pltpu.HBM((width, depth), F32)],
-        in_specs=[SMEM, VMEM] + [ANY] * len(filled),
-        out_specs=[ANY, ANY],
-        scratch_shapes=[
-            pltpu.VMEM((4, depth // 2, width), F32),
-            pltpu.VMEM((width, depth // 2), F32),
-            pltpu.SemaphoreType.DMA((5,)),
-        ],
+        functools.partial(unfold_kernel, len(shares)),
+        out_shape=results,
+        in_specs=[SMEM, VMEM] + [ANY] * (len(shares) + len(filled)),
+        out_specs=[ANY] * len(results),
+        scratch_shapes=scratch,
         input_output_aliases={2 + i: i for i in range(len(filled))},
         compiler_params=PARAMS,
         cost_estimate=pl.CostEstimate(flops=0, bytes_accessed=1 << 20, transcendentals=0),
-    )(which, source, *filled)
+    )(which, source, *shares, *filled)
 
 
 class Load:
@@ -511,12 +530,11 @@
         flops=4 * events * depth * width + 2 * events * slots * width,
         moved=10 << 20,
     )
-    kv_other = swap(kv_other)
     back, kv_mine, kv_other = lax.optimization_barrier((back, kv_mine, kv_other))
     half = depth * 3 // 2
     mine, other, gx = call(
         post_kernel,
-        [((chips * 40, width), BF16), ((half, width), BF16), ((rows, depth), BF16)],
+        [((chips * 40, width), BF16)] * 2 + [((rows, depth), BF16)],
         (back, kv_mine, kv_other, place, aux, x_near, w_near, gy_near),
         (core,),
         scratch=[pltpu.VMEM((2, half, width), F32)],
@@ -536,17 +554,13 @@
     )
     plane = lax.axis_index("mp")
     share = rows // planes
-    parts = []
+    parts = [lax.dynamic_slice_in_dim(gx, plane * share, share, 0)]
     for step in range(1, planes):
         part = lax.dynamic_slice_in_dim(gx, (plane + step) % planes * share, share, 0)
         parts.append(lax.ppermute(part, "mp", [(i, (i + step) % planes) for i in range(planes)]))
     factor = (rows * owners) ** (-0.5)
     grad_kv = gkv.reshape(1, events, 2, width)
     summed, grad_kv, *parts = lax.optimization_barrier((exchange_core(summed), grad_kv, *parts))
-    total = lax.dynamic_slice_in_dim(gx, plane * share, share, 0).astype(F32)
-    for part in parts:
-        total = total + part.astype(F32)
-    grad_x = total.astype(BF16)
     (piece,) = call(
         lambda i, o: sum_kernel(factor, i, o),
         [((chips * 40, width), BF16)],
@@ -555,11 +569,10 @@
         near_out=(0,),
         moved=1 << 20,
     )
-    piece, grad_x = lax.optimization_barrier((piece, grad_x))
     mine = exchange_core(piece)
     other = swap(mine)
-    filled = unfold(core, mine, depth)
-    grad_w_in, grad_w_out = unfold(1 - core, other, depth, filled)
+    grad_x, *filled = unfold(core, mine, depth, shares=parts)
+    grad_w_in, grad_w_out = unfold(1 - core, other, depth, filled=filled)
     return (grad_x, grad_kv, grad_w_in, grad_w_out)
 
 

time: 100 us -> 99.9 us (level)
  waiting for transfers between devices: 23.8 us -> 25.6 us
  local copies, waits for them, and re-layouts: 2.15 us -> 1.12 us
    all_to_all x2, waiting for transfers between devices: 15.8 us -> 17.5 us  [exchange(): a = lax.all_to_all(a, 'dp', 0, 0, tiled=True)]
    reshape x1, local copies, waits for them, and re-layouts: 2.13 us -> 1.09 us  [on_device(): grad_kv = gkv.reshape(1, events, 2, width)]
    ppermute x3 -> x2, waiting for transfers between devices: 2.54 us -> 1.56 us  [swap(): return lax.ppermute(a, 'dp', pairs)]
    ppermute x3 -> x2, starting transfers between devices: 4.74 us -> 4.02 us  [swap(): return lax.ppermute(a, 'dp', pairs)]
  transfers between devices with their start and end apart: 9 -> 8, of which waited for: 6 -> 6; matrix products, arithmetic and copies ran while one was open for 2% -> 1% of each run, Pallas kernels for 12% -> 12%
where the time goes in v6:
time: 99.9 us; the launch traced here: 99.5 us
  starting transfers between devices  31.6 us (32%)
  waiting for transfers between devices  25.6 us (26%)
  Pallas kernels  24.5 us (25%)
  blocking collectives  15.8 us (16%)
  local copies, waits for them, and re-layouts  1.12 us (1%)
    pallas_call x7, Pallas kernels, call(): pl.pallas_call(body, out_shape=[jax.ShapeDtypeStruct(s, d) if i in near_o...  22.5 us
    all_to_all x2, starting transfers between devices, exchange(): a = lax.all_to_all(a, 'dp', 0, 0, tiled=True)  18.6 us
    all_to_all x2, waiting for transfers between devices, exchange(): a = lax.all_to_all(a, 'dp', 0, 0, tiled=True)  17.5 us
    all_to_all x1, blocking collectives, exchange_core(): a = lax.all_to_all(a, 'dp', 0, 0, axis_index_groups=same_core, tiled=True)  15.8 us
    all_to_all x1, waiting for transfers between devices, exchange_core(): a = lax.all_to_all(a, 'dp', 0, 0, axis_index_groups=same_core, tiled=True)  5.63 us
    ppermute x3, starting transfers between devices, on_device(): lax.ppermute(part, 'mp', [(i, (i + step) % planes) for i in range(planes)])  5.06 us
    ppermute x2, starting transfers between devices, swap(): return lax.ppermute(a, 'dp', pairs)  4.02 us
    all_to_all x1, starting transfers between devices, exchange_core(): a = lax.all_to_all(a, 'dp', 0, 0, axis_index_groups=same_core, tiled=True)  3.91 us
  transfers between devices with their start and end apart: 8, of which 6 were waited for; matrix products, arithmetic and copies ran while one was open for 1% of the time, Pallas kernels for 12%

profile of v6, /device:TPU:1, one launch (start us, length us, event | category | flops | bytes accessed | tf_op | source)
XLA Modules:
  0.0 99.5 jit_solution(4117420978603345344)
XLA Ops:
  0.6 2.6 %shard_map.111 = bf16[1536,128]{1,0:T(8,128)(2,1)} custom-call(s32[1,128]{1,0:T(1,128)} %bitcast.21, s32[1,128]{1,0:T(1,128)} %bitcast.25, s32[1,64]{1,0:T(1,128)} %bitcast.23, bf16[128,512]{1,0:T(8,128)(2,1)} %refs_8_.1, bf16[4,512,128]{2,1,0:T(8,128)(2,1)} %refs_9_.1, bf16[128,512]{1,0:T(8,128)(2,1)} %refs_5_.3, bf16[128,512]{1,0:T(8,128)(2,1)} %refs_10_.1), custom_call_target="tpu_custom_call" | custom-call | flops 50331648 | bytes 1048576 | tf_op jit(solution)/shard_map/pallas_call | solution.py:421
  3.3 13.0 %all-to-all-start = ((bf16[64,24,128]{2,1,0:T(8,128)(2,1)}), bf16[64,24,128]{2,1,0:T(8,128)(2,1)S(1)}, u32[]{:S(2)}, u32[]{:S(2)}) async-start(bf16[64,24,128]{2,1,0:T(8,128)(2,1)} %bitcast.4), calls=%async_computation | async-start | bytes 786432 | tf_op jit(solution)/shard_map/all_to_all | solution.py:456
  16.3 4.8 %shard_map.112 = (bf16[2048,128]{1,0:T(8,128)(2,1)S(1)}, bf16[128,2048]{1,0:T(8,128)(2,1)S(1)}, bf16[2048,128]{1,0:T(8,128)(2,1)}, bf16[128,2048]{1,0:T(8,128)(2...) custom-call(bf16[4,512,128]{2,1,0:T(8,128)(2,1)} %refs_9_.1, ...), custom_call_target="tpu_custom_call" | custom-call | flops 536870912 | bytes 5242880 | tf_op jit(solution)/shard_map/pallas_call | solution.py:421
  21.0 10.3 %all-to-all-done = bf16[64,24,128]{2,1,0:T(8,128)(2,1)S(1)} async-done(((bf16[64,24,128]{2,1,0:T(8,128)(2,1)}), bf16[64,24,128]{2,1,0:T(8,128)(2,1)S(1)}, u32[]{:S(2)}, u32[]{:S(2)}) %all-to-all-start) | async-done | bytes 393248 | tf_op jit(solution)/shard_map/all_to_all | solution.py:456
  31.3 7.6 %shard_map.113 = (bf16[1024,128]{1,0:T(8,128)(2,1)}, bf16[2048,1024]{1,0:T(8,128)(2,1)}, bf16[2048,128]{1,0:T(8,128)(2,1)}, bf16[512,128]{1,0:T(8,128)(2,1)}) custom-call(bf16[1536,128]{1,0:T(8,128)(2,1)S(1)} %bitcast.18, bf16[2048,128]{1,0:T(8,128)(2,1)S(1)} %get-tuple-element.40.refs_1_, bf16[128,2048]{1,0:T(8,128)(2,1)S(1)} %get-tuple-element.41.refs_2_, ...), custom_call_target="tpu_custom_call" | custom-call | flops 1342177280 | bytes 8388608 | tf_op jit(solution)/shard_map/pallas_call | solution.py:421
  39.0 5.6 %all-to-all-start.1 = ((bf16[64,16,128]{2,1,0:T(8,128)(2,1)}), bf16[64,16,128]{2,1,0:T(8,128)(2,1)S(1)}, u32[]{:S(2)}, u32[]{:S(2)}) async-start(bf16[64,16,128]{2,1,0:T(8,128)(2,1)} %bitcast.7), calls=%async_computation.1 | async-start | bytes 524288 | tf_op jit(solution)/shard_map/all_to_all | solution.py:456
  44.6 5.9 %shard_map.114 = (bf16[2048,256]{1,0:T(8,128)(2,1)}, bf16[512,128]{1,0:T(8,128)(2,1)S(1)}, bf16[512,128]{1,0:T(8,128)(2,1)S(1)}, bf16[512,128]{1,0:T(8,128)(2,1)...) custom-call(s32[1]{0:T(128)} %bitcast.refs_0_.which_ref, ...), custom_call_target="tpu_custom_call" | custom-call | flops 805306368 | bytes 10485760 | tf_op jit(solution)/shard_map/pallas_call | solution.py:421
  50.5 0.0 copy-start
  50.5 7.2 %all-to-all-done.1 = bf16[64,16,128]{2,1,0:T(8,128)(2,1)S(1)} async-done(((bf16[64,16,128]{2,1,0:T(8,128)(2,1)}), bf16[64,16,128]{2,1,0:T(8,128)(2,1)S(1)}, u32[]{:S(2)}, u32[]{:S(2)}) %all-to-all-start.1) | async-done | bytes 262176 | tf_op jit(solution)/shard_map/all_to_all | solution.py:456
  57.7 0.7 shard_map.115
  58.4 0.3 collective-permute-start
  58.8 1.4 %collective-permute-done.refs_1_ = bf16[1280,128]{1,0:T(8,128)(2,1)S(1)} collective-permute-done((bf16[1280,128]{1,0:T(8,128)(2,1)S(1)}, bf16[1280,128]{1,0:T(8,128)(2,1)S(1)}, u32[]{:S(2)}, u32[]{:S(2)}) %collective-permute-start) | collective-permute-done | bytes 327712 | tf_op jit(solution)/shard_map/ppermute | solution.py:452
  60.1 0.8 shard_map.116
  61.0 3.9 %all-to-all-start.2 = ((bf16[32,40,128]{2,1,0:T(8,128)(2,1)}), bf16[32,40,128]{2,1,0:T(8,128)(2,1)S(1)}, u32[]{:S(2)}, u32[]{:S(2)}) async-start(bf16[32,40,128]{2,1,0:T(8,128)(2,1)} %bitcast.9), calls=%async_computation.2 | async-start | bytes 655360 | tf_op jit(solution)/shard_map/all_to_all | solution.py:461
  65.0 1.4 %collective-permute-start.1 = (bf16[32,512]{1,0:T(8,128)(2,1)S(1)}, bf16[32,512]{1,0:T(8,128)(2,1)S(1)}, u32[]{:S(2)}, u32[]{:S(2)}) collective-permute-start(bf16[32,512]{1,0:T(8,128)(2,1)S(1)} %get-tuple-element.78), channel_id=1, source_target_pairs={{0,1},{1,2},{2,3},{3,0},{4,5},{5,6},{6,7},{7,4},{8,9},{9,10},{10,1... | collective-permute-start | bytes 98312 | tf_op jit(solution)/shard_map/ppermute | solution.py:560
  66.3 2.6 %collective-permute-start.2 = (bf16[32,512]{1,0:T(8,128)(2,1)S(1)}, bf16[32,512]{1,0:T(8,128)(2,1)S(1)}, u32[]{:S(2)}, u32[]{:S(2)}) collective-permute-start(bf16[32,512]{1,0:T(8,128)(2,1)S(1)} %get-tuple-element.77), channel_id=1, source_target_pairs={{0,2},{1,3},{2,0},{3,1},{4,6},{5,7},{6,4},{7,5},{8,10},{9,11},{10,... | collective-permute-start | bytes 98312 | tf_op jit(solution)/shard_map/ppermute | solution.py:560
  69.0 1.1 %collective-permute-start.3 = (bf16[32,512]{1,0:T(8,128)(2,1)S(1)}, bf16[32,512]{1,0:T(8,128)(2,1)S(1)}, u32[]{:S(2)}, u32[]{:S(2)}) collective-permute-start(bf16[32,512]{1,0:T(8,128)(2,1)S(1)} %get-tuple-element.76), channel_id=1, source_target_pairs={{0,3},{1,0},{2,1},{3,2},{4,7},{5,4},{6,5},{7,6},{8,11},{9,8},{10,9... | collective-permute-start | bytes 98312 | tf_op jit(solution)/shard_map/ppermute | solution.py:560
  70.0 0.0 copy-done
  70.0 1.1 %reshape.57 = bf16[1,2048,2,128]{3,2,1,0:T(2,128)(2,1)} reshape(bf16[2048,256]{1,0:T(8,128)(2,1)S(1)} %copy-done) | data formatting | bytes 2097152 | tf_op jit(solution)/shard_map/reshape | solution.py:562
  71.1 0.0 collective-permute-done.1.refs_1_
  71.1 0.0 collective-permute-done.2.refs_2_
  71.1 0.9 collective-permute-done.3.refs_3_
  72.0 5.6 %all-to-all-done.2 = bf16[32,40,128]{2,1,0:T(8,128)(2,1)S(1)} async-done(((bf16[32,40,128]{2,1,0:T(8,128)(2,1)}), bf16[32,40,128]{2,1,0:T(8,128)(2,1)S(1)}, u32[]{:S(2)}, u32[]{:S(2)}) %all-to-all-start.2) | async-done | bytes 327712 | tf_op jit(solution)/shard_map/all_to_all | solution.py:461
  77.7 0.1 shard_map.117
  77.8 15.8 %all_to_all.20 = bf16[32,40,128]{2,1,0:T(8,128)(2,1)S(1)} all-to-all(bf16[32,40,128]{2,1,0:T(8,128)(2,1)S(1)} %bitcast.16), channel_id=1, replica_groups={{0,8,16,24,32,40,48,56,64,72,80,88,96,104,112,120,128,136,144,152,160,1..., dimensions={0} | all-to-all | bytes 655360 | tf_op jit(solution)/shard_map/all_to_all | solution.py:461
  93.5 3.7 %collective-permute-start.4 = (bf16[1280,128]{1,0:T(8,128)(2,1)S(1)}, bf16[1280,128]{1,0:T(8,128)(2,1)S(1)}, u32[]{:S(2)}, u32[]{:S(2)}) collective-permute-start(bf16[1280,128]{1,0:T(8,128)(2,1)S(1)} %bitcast.14), channel_id=1, source_target_pairs={{0,4},{4,0},{8,12},{12,8},{16,20},{20,16},{24,28},{28,24},{32,36},... | collective-permute-start | bytes 983048 | tf_op jit(solution)/shard_map/ppermute | solution.py:452
  97.2 1.1 %shard_map.118 = (bf16[32,512]{1,0:T(8,128)(2,1)}, f32[4,512,128]{2,1,0:T(8,128)}, f32[128,512]{1,0:T(8,128)}) custom-call(s32[1]{0:T(128)} %bitcast.refs_0_.which_ref, bf16[1280,128]{1,0:T(8,128)(2,1)S(1)} %bitcast.15, bf16[32,512]{1,0:T(8,128)(2,1)S(1)} %get-tuple-element.66.refs_0_, bf16[32,512]{1,0:T(8,128)(2,1)S(1)} %collective-permute-done.1.refs_1_, ...), custom_call_target="tpu_custom_call" | custom-call | bytes 1048576 | tf_op jit(solution)/shard_map/pallas_call | solution.py:341
  98.3 0.2 collective-permute-done.4.source_ref
  98.5 0.9 shard_map.119
  (1 shorter events, 0.0 us)
Async XLA Ops:
  3.3 28.1 %all-to-all-start = ((bf16[64,24,128]{2,1,0:T(8,128)(2,1)}), bf16[64,24,128]{2,1,0:T(8,128)(2,1)S(1)}, u32[]{:S(2)}, u32[]{:S(2)}) async-start(bf16[64,24,128]{2,1,0:T(8,128)(2,1)} %bitcast.4), calls=%async_computation | async-start | bytes 786432 | tf_op jit(solution)/shard_map/all_to_all | solution.py:456
  39.0 18.8 %all-to-all-start.1 = ((bf16[64,16,128]{2,1,0:T(8,128)(2,1)}), bf16[64,16,128]{2,1,0:T(8,128)(2,1)S(1)}, u32[]{:S(2)}, u32[]{:S(2)}) async-start(bf16[64,16,128]{2,1,0:T(8,128)(2,1)} %bitcast.7), calls=%async_computation.1 | async-start | bytes 524288 | tf_op jit(solution)/shard_map/all_to_all | solution.py:456
  50.5 19.5 %copy-start = (bf16[2048,256]{1,0:T(8,128)(2,1)S(1)}, bf16[2048,256]{1,0:T(8,128)(2,1)}, u32[]{:S(2)}) copy-start(bf16[2048,256]{1,0:T(8,128)(2,1)} %get-tuple-element.63) | copy-start | bytes 3145732
  58.4 1.7 %collective-permute-start = (bf16[1280,128]{1,0:T(8,128)(2,1)S(1)}, bf16[1280,128]{1,0:T(8,128)(2,1)S(1)}, u32[]{:S(2)}, u32[]{:S(2)}) collective-permute-start(bf16[1280,128]{1,0:T(8,128)(2,1)S(1)} %get-tuple-element.62), channel_id=1, source_target_pairs={{0,4},{4,0},{8,12},{12,8},{16,20},{20,16},{24,28},{28,24},{32,36},... | collective-permute-start | bytes 983048 | tf_op jit(solution)/shard_map/ppermute | solution.py:452
  61.0 16.7 %all-to-all-start.2 = ((bf16[32,40,128]{2,1,0:T(8,128)(2,1)}), bf16[32,40,128]{2,1,0:T(8,128)(2,1)S(1)}, u32[]{:S(2)}, u32[]{:S(2)}) async-start(bf16[32,40,128]{2,1,0:T(8,128)(2,1)} %bitcast.9), calls=%async_computation.2 | async-start | bytes 655360 | tf_op jit(solution)/shard_map/all_to_all | solution.py:461
  65.0 6.2 %collective-permute-start.1 = (bf16[32,512]{1,0:T(8,128)(2,1)S(1)}, bf16[32,512]{1,0:T(8,128)(2,1)S(1)}, u32[]{:S(2)}, u32[]{:S(2)}) collective-permute-start(bf16[32,512]{1,0:T(8,128)(2,1)S(1)} %get-tuple-element.78), channel_id=1, source_target_pairs={{0,1},{1,2},{2,3},{3,0},{4,5},{5,6},{6,7},{7,4},{8,9},{9,10},{10,1... | collective-permute-start | bytes 98312 | tf_op jit(solution)/shard_map/ppermute | solution.py:560
  66.3 4.8 %collective-permute-start.2 = (bf16[32,512]{1,0:T(8,128)(2,1)S(1)}, bf16[32,512]{1,0:T(8,128)(2,1)S(1)}, u32[]{:S(2)}, u32[]{:S(2)}) collective-permute-start(bf16[32,512]{1,0:T(8,128)(2,1)S(1)} %get-tuple-element.77), channel_id=1, source_target_pairs={{0,2},{1,3},{2,0},{3,1},{4,6},{5,7},{6,4},{7,5},{8,10},{9,11},{10,... | collective-permute-start | bytes 98312 | tf_op jit(solution)/shard_map/ppermute | solution.py:560
  69.0 3.1 %collective-permute-start.3 = (bf16[32,512]{1,0:T(8,128)(2,1)S(1)}, bf16[32,512]{1,0:T(8,128)(2,1)S(1)}, u32[]{:S(2)}, u32[]{:S(2)}) collective-permute-start(bf16[32,512]{1,0:T(8,128)(2,1)S(1)} %get-tuple-element.76), channel_id=1, source_target_pairs={{0,3},{1,0},{2,1},{3,2},{4,7},{5,4},{6,5},{7,6},{8,11},{9,8},{10,9... | collective-permute-start | bytes 98312 | tf_op jit(solution)/shard_map/ppermute | solution.py:560
  93.5 4.9 %collective-permute-start.4 = (bf16[1280,128]{1,0:T(8,128)(2,1)S(1)}, bf16[1280,128]{1,0:T(8,128)(2,1)S(1)}, u32[]{:S(2)}, u32[]{:S(2)}) collective-permute-start(bf16[1280,128]{1,0:T(8,128)(2,1)S(1)} %bitcast.14), channel_id=1, source_target_pairs={{0,4},{4,0},{8,12},{12,8},{16,20},{20,16},{24,28},{28,24},{32,36},... | collective-permute-start | bytes 983048 | tf_op jit(solution)/shard_map/ppermute | solution.py:452

commit v7 on v6

--- a/solution.py
+++ b/solution.py
@@ -13,6 +13,7 @@
 BLOCK = 256
 HISTORY_PARTS = 2
 LATE = 5
+ROWS = 2 * CAP + 2
 F32 = jnp.float32
 BF16 = jnp.bfloat16
 ANY = pl.BlockSpec(memory_space=pl.ANY)
@@ -53,7 +54,7 @@
     return joined.reshape(count * 8 * len(parts), parts[0].shape[1])
 
 
-def slot_table(hist, owner):
+def slot_parts(hist, owner):
     rows, owners = hist.shape[1], owner.shape[1]
     named = jnp.where(iota((owners, rows), 0) == hist, 1.0, 0.0).astype(BF16)
     owner = jnp.broadcast_to(owner.astype(F32), (8, owners)).astype(BF16)
@@ -62,33 +63,49 @@
     earlier = jnp.where(iota((rows, rows), 0) < iota((rows, rows), 1), 1.0, 0.0)
     before = nn(hit.astype(BF16), earlier.astype(BF16))
     rank = jnp.sum(before * hit, axis=0, keepdims=True)
-    slot = target * float(CAP) + rank
-    return jnp.where(iota((owners * CAP, rows), 0).astype(F32) == slot, 1.0, 0.0).astype(BF16)
-
-
-def pre_kernel(hist_in, len_in, owner_in, x_in, w_in, wo_in, gy_in, send_out, w_scr, w_sem):
+    return target, rank, hit
+
+
+def one_hot(slot, slots):
+    return jnp.where(iota((slots, slot.shape[1]), 0).astype(F32) == slot, 1.0, 0.0).astype(BF16)
+
+
+def every(first, count, step):
+    return pl.ds(first, count, stride=step)
+
+
+def column(row):
+    return jnp.transpose(jnp.broadcast_to(row, (row.shape[1], row.shape[1])))
+
+
+def pre_kernel(hist_in, len_in, owner_in, x_in, w_in, wo_in, gy_in, send_out, w_scr, w_sem, scr):
     w_copy = pltpu.make_async_copy(w_in.get().at[:2], w_scr, w_sem)
     w_copy.start()
-    place = slot_table(hist_in.get()[...], owner_in.get()[...])
+    target, rank, hit = slot_parts(hist_in.get()[...], owner_in.get()[...])
+    owners, rows = hit.shape
+    place = one_hot(rank * float(owners) + target, owners * CAP)
     length = len_in.get()[...].astype(F32)
-    rows = length.shape[1]
     high = jnp.floor(length * (1.0 / 256.0))
     low = length - 256.0 * high
-    digits = jnp.transpose(jnp.where(iota((rows, rows), 0) == 0, high, low))
+    lane = iota((rows, rows), 1).astype(F32) == column(rank)
+    hit = hit.astype(BF16)
+    for i, digit in enumerate((high, low)):
+        digit = jnp.where(lane, column(digit), 0.0).astype(BF16)
+        scr[every(2 * CAP + i, owners, ROWS), :] = nn(hit, digit)
     cot = nt(gy_in.get()[...], wo_in.get()[...]).astype(BF16).astype(F32)
     x = x_in.get()[...]
     w_copy.wait()
     queries, _ = silu_and_slope(nn(x, w_scr[0]))
     gates, _ = silu_and_slope(nn(x, w_scr[1]))
     gates = gates.astype(BF16).astype(F32)
-    payload = jnp.concatenate(
-        [queries.astype(BF16), (cot * gates).astype(BF16), digits.astype(BF16)], axis=1
-    )
+    payload = jnp.concatenate([queries.astype(BF16), (cot * gates).astype(BF16)], axis=1)
     packed = nn(place, payload)
     width = queries.shape[1]
-    send_out.buffer[...] = spread(
-        [packed[:, :width], packed[:, width : 2 * width], packed[:, 2 * width :]]
-    ).astype(BF16)
+    for j in range(CAP):
+        some = packed[j * owners : (j + 1) * owners]
+        scr[every(j, owners, ROWS), :] = some[:, :width]
+        scr[every(CAP + j, owners, ROWS), :] = some[:, width:]
+    send_out.buffer[...] = scr[...].astype(BF16)
 
 
 def project_kernel(
@@ -109,7 +126,8 @@
         vt_out.buffer[:, at] = jnp.transpose(values.astype(BF16))
     for out in (k_out, v_out, kt_out, vt_out, slope_out):
         out.send()
-    place_out.buffer[...] = slot_table(hist_in.get()[...], owner_in.get()[...])
+    target, rank, hit = slot_parts(hist_in.get()[...], owner_in.get()[...])
+    place_out.buffer[...] = one_hot(target * float(CAP) + rank, hit.shape[0] * CAP)
     x = x_in.get()[...]
     _, slope_q = silu_and_slope(nn(x, w_ref[0]))
     gates, slope_g = silu_and_slope(nn(x, w_ref[1]))
@@ -122,18 +140,19 @@
 def attend_kernel(
     recv_in, k_in, vt_in, v_in, kt_in,
     back_out, weights_out, d_keys_out, d_att_out,
-    s_scr,
+    s_scr, in_scr, out_scr,
 ):
     recv_ref, k_ref, vt_ref = recv_in.get(), k_in.get(), vt_in.get()
-    slots, width = recv_ref.shape[0] // 3, recv_ref.shape[1]
+    owners, width = recv_ref.shape[0] // ROWS, recv_ref.shape[1]
+    slots = owners * CAP
     heads = width // DH
     events = k_ref.shape[0]
-    got = recv_ref[...].astype(F32).reshape(slots // CAP, 3 * CAP, width)
-    q = got[:, :CAP].reshape(slots, width).astype(BF16)
-    dn = got[:, CAP : 2 * CAP].reshape(slots, width).astype(BF16)
-    digits = got[:, 2 * CAP :].reshape(slots, width).astype(BF16)
-    digits = jnp.transpose(digits).astype(F32)
-    length = digits[0:1] * 256.0 + digits[1:2]
+    in_scr[...] = recv_ref[...].astype(F32)
+    q = jnp.concatenate([in_scr[every(j, owners, ROWS), :] for j in range(CAP)], axis=0).astype(BF16)
+    dn = jnp.concatenate([in_scr[every(CAP + j, owners, ROWS), :] for j in range(CAP)], axis=0).astype(BF16)
+    high, low = (in_scr[every(2 * CAP + i, owners, ROWS), :] for i in range(2))
+    length = jnp.transpose(high * 256.0 + low)
+    length = jnp.concatenate([length[j : j + 1] for j in range(CAP)], axis=1)
     head_row = iota((width, slots), 0) // DH
     head_col = iota((slots, width), 1) // DH
     qt_half = (jnp.transpose(q).astype(F32) * (0.5 * DH ** (-0.5))).astype(BF16)
@@ -174,7 +193,12 @@
         d_keys_out.send_part((at,))
     d_query = [nn(kt_ref[mine_of[h], :], s_scr[:, cols_of[h]]) for h in range(heads)]
     d_query = (jnp.concatenate(d_query, axis=0) * (0.5 * DH ** (-0.5))).astype(BF16)
-    back_out.buffer[...] = spread([jnp.transpose(d_query).astype(F32), normed]).astype(BF16)
+    d_query = jnp.transpose(d_query).astype(F32)
+    for j in range(CAP):
+        some = slice(j * owners, (j + 1) * owners)
+        out_scr[every(j, owners, 2 * CAP), :] = d_query[some]
+        out_scr[every(CAP + j, owners, 2 * CAP), :] = normed[some]
+    back_out.buffer[...] = out_scr[...].astype(BF16)
 
 
 def history_kernel(
@@ -452,9 +476,10 @@
         return lax.ppermute(a, "dp", pairs)
 
     def exchange(a):
-        a = a.reshape(owners, a.shape[0] // owners, width)
-        a = lax.all_to_all(a, "dp", 0, 0, tiled=True)
-        return a.reshape(a.shape[0] * a.shape[1], width)
+        shape = a.shape
+        size = shape[0] // owners
+        a = a.reshape((owners, size, width) if size % 8 == 0 else (owners, size // 2, 2, width))
+        return lax.all_to_all(a, "dp", 0, 0, tiled=True).reshape(shape)
 
     def exchange_core(a):
         a = a.reshape(chips, a.shape[0] // chips, width)
@@ -465,9 +490,13 @@
     owner_row = owner_map.reshape(1, owners)
     (send,) = call(
         pre_kernel,
-        [((3 * slots, width), BF16)],
+        [((owners * ROWS, width), BF16)],
         (hist_rows, imp_len.reshape(1, rows), owner_row, imp_x, w_in, w_out, grad_y),
-        scratch=[pltpu.VMEM((2,) + w_in.shape[1:], BF16), pltpu.SemaphoreType.DMA(())],
+        scratch=[
+            pltpu.VMEM((2,) + w_in.shape[1:], BF16),
+            pltpu.SemaphoreType.DMA(()),
+            pltpu.VMEM((owners * ROWS, width), F32),
+        ],
         raw_in=(4,),
         near_out=(0,),
         flops=2 * rows * depth * width * 3,
@@ -500,7 +529,11 @@
             ((slots, width), BF16),
         ],
         (recv, keys, values_t, values, keys_t),
-        scratch=[pltpu.VMEM((events, heads * slots), BF16)],
+        scratch=[
+            pltpu.VMEM((events, heads * slots), BF16),
+            pltpu.VMEM((owners * ROWS, width), F32),
+            pltpu.VMEM((2 * slots, width), F32),
+        ],
         near_in=(0, 1, 2),
         near_out=(0,),
         flops=10 * events * slots * width,

time: 99.9 us -> 98.1 us (0.982)
  waiting for transfers between devices: 25.6 us -> 24.2 us
    all_to_all x2, waiting for transfers between devices: 17.5 us -> 16.2 us  [exchange(): return lax.all_to_all(a, 'dp', 0, 0, tiled=True).reshape(shape)]
where the time goes in v7:
time: 98.1 us; the launch traced here: 97.7 us
  starting transfers between devices  30.8 us (31%)
  Pallas kernels  24.7 us (25%)
  waiting for transfers between devices  24.2 us (25%)
  blocking collectives  15.8 us (16%)
  local copies, waits for them, and re-layouts  1.12 us (1%)
    pallas_call x7, Pallas kernels, call(): pl.pallas_call(body, out_shape=[jax.ShapeDtypeStruct(s, d) if i in near_o...  22.8 us
    all_to_all x2, starting transfers between devices, exchange(): return lax.all_to_all(a, 'dp', 0, 0, tiled=True).reshape(shape)  17.9 us
    all_to_all x2, waiting for transfers between devices, exchange(): return lax.all_to_all(a, 'dp', 0, 0, tiled=True).reshape(shape)  16.2 us
    all_to_all x1, blocking collectives, exchange_core(): a = lax.all_to_all(a, 'dp', 0, 0, axis_index_groups=same_core, tiled=True)  15.8 us
    all_to_all x1, waiting for transfers between devices, exchange_core(): a = lax.all_to_all(a, 'dp', 0, 0, axis_index_groups=same_core, tiled=True)  5.63 us
    ppermute x3, starting transfers between devices, on_device(): lax.ppermute(part, 'mp', [(i, (i + step) % planes) for i in range(planes)])  5.06 us
    ppermute x2, starting transfers between devices, swap(): return lax.ppermute(a, 'dp', pairs)  4.02 us
    all_to_all x1, starting transfers between devices, exchange_core(): a = lax.all_to_all(a, 'dp', 0, 0, axis_index_groups=same_core, tiled=True)  3.91 us
  transfers between devices with their start and end apart: 8, of which 6 were waited for; matrix products, arithmetic and copies ran while one was open for 1% of the time, Pallas kernels for 12%

profile of v7, /device:TPU:1, one launch (start us, length us, event | category | flops | bytes accessed | tf_op | source)
XLA Modules:
  0.0 97.7 jit_solution(14358366442330904048)
XLA Ops:
  0.6 2.7 %shard_map.111 = bf16[1152,128]{1,0:T(8,128)(2,1)} custom-call(s32[1,128]{1,0:T(1,128)} %bitcast.21, s32[1,128]{1,0:T(1,128)} %bitcast.25, s32[1,64]{1,0:T(1,128)} %bitcast.23, bf16[128,512]{1,0:T(8,128)(2,1)} %refs_8_.1, bf16[4,512,128]{2,1,0:T(8,128)(2,1)} %refs_9_.1, bf16[128,512]{1,0:T(8,128)(2,1)} %refs_5_.3, bf16[128,512]{1,0:T(8,128)(2,1)} %refs_10_.1), custom_call_target="tpu_custom_call" | custom-call | flops 50331648 | bytes 1048576 | tf_op jit(solution)/shard_map/pallas_call | solution.py:445
  3.3 13.0 %all-to-all-start = ((bf16[64,9,2,128]{3,2,1,0:T(2,128)(2,1)}), bf16[64,9,2,128]{3,2,1,0:T(2,128)(2,1)S(1)}, u32[]{:S(2)}, u32[]{:S(2)}) async-start(bf16[64,9,2,128]{3,2,1,0:T(2,128)(2,1)} %bitcast.4), calls=%async_computation | async-start | bytes 589824 | tf_op jit(solution)/shard_map/all_to_all | solution.py:482
  16.3 4.8 %shard_map.112 = (bf16[2048,128]{1,0:T(8,128)(2,1)S(1)}, bf16[128,2048]{1,0:T(8,128)(2,1)S(1)}, bf16[2048,128]{1,0:T(8,128)(2,1)}, bf16[128,2048]{1,0:T(8,128)(2...) custom-call(bf16[4,512,128]{2,1,0:T(8,128)(2,1)} %refs_9_.1, ...), custom_call_target="tpu_custom_call" | custom-call | flops 536870912 | bytes 5242880 | tf_op jit(solution)/shard_map/pallas_call | solution.py:445
  21.1 9.0 %all-to-all-done = bf16[64,9,2,128]{3,2,1,0:T(2,128)(2,1)S(1)} async-done(((bf16[64,9,2,128]{3,2,1,0:T(2,128)(2,1)}), bf16[64,9,2,128]{3,2,1,0:T(2,128)(2,1)S(1)}, u32[]{:S(2)}, u32[]{:S(2)}) %all-to-all-start) | async-done | bytes 294944 | tf_op jit(solution)/shard_map/all_to_all | solution.py:482
  30.0 7.8 %shard_map.113 = (bf16[1024,128]{1,0:T(8,128)(2,1)}, bf16[2048,1024]{1,0:T(8,128)(2,1)}, bf16[2048,128]{1,0:T(8,128)(2,1)}, bf16[512,128]{1,0:T(8,128)(2,1)}) custom-call(bf16[1152,128]{1,0:T(8,128)(2,1)S(1)} %bitcast.18, bf16[2048,128]{1,0:T(8,128)(2,1)S(1)} %get-tuple-element.40.refs_1_, bf16[128,2048]{1,0:T(8,128)(2,1)S(1)} %get-tuple-element.41.refs_2_, ...), custom_call_target="tpu_custom_call" | custom-call | flops 1342177280 | bytes 8388608 | tf_op jit(solution)/shard_map/pallas_call | solution.py:445
  37.9 4.9 %all-to-all-start.1 = ((bf16[64,16,128]{2,1,0:T(8,128)(2,1)}), bf16[64,16,128]{2,1,0:T(8,128)(2,1)S(1)}, u32[]{:S(2)}, u32[]{:S(2)}) async-start(bf16[64,16,128]{2,1,0:T(8,128)(2,1)} %bitcast.7), calls=%async_computation.1 | async-start | bytes 524288 | tf_op jit(solution)/shard_map/all_to_all | solution.py:482
  42.8 5.9 %shard_map.114 = (bf16[2048,256]{1,0:T(8,128)(2,1)}, bf16[512,128]{1,0:T(8,128)(2,1)S(1)}, bf16[512,128]{1,0:T(8,128)(2,1)S(1)}, bf16[512,128]{1,0:T(8,128)(2,1)...) custom-call(s32[1]{0:T(128)} %bitcast.refs_0_.which_ref, ...), custom_call_target="tpu_custom_call" | custom-call | flops 805306368 | bytes 10485760 | tf_op jit(solution)/shard_map/pallas_call | solution.py:445
  48.7 0.0 copy-start
  48.7 7.2 %all-to-all-done.1 = bf16[64,16,128]{2,1,0:T(8,128)(2,1)S(1)} async-done(((bf16[64,16,128]{2,1,0:T(8,128)(2,1)}), bf16[64,16,128]{2,1,0:T(8,128)(2,1)S(1)}, u32[]{:S(2)}, u32[]{:S(2)}) %all-to-all-start.1) | async-done | bytes 262176 | tf_op jit(solution)/shard_map/all_to_all | solution.py:482
  55.9 0.7 shard_map.115
  56.6 0.3 collective-permute-start
  57.0 1.4 %collective-permute-done.refs_1_ = bf16[1280,128]{1,0:T(8,128)(2,1)S(1)} collective-permute-done((bf16[1280,128]{1,0:T(8,128)(2,1)S(1)}, bf16[1280,128]{1,0:T(8,128)(2,1)S(1)}, u32[]{:S(2)}, u32[]{:S(2)}) %collective-permute-start) | collective-permute-done | bytes 327712 | tf_op jit(solution)/shard_map/ppermute | solution.py:476
  58.3 0.8 shard_map.116
  59.2 3.9 %all-to-all-start.2 = ((bf16[32,40,128]{2,1,0:T(8,128)(2,1)}), bf16[32,40,128]{2,1,0:T(8,128)(2,1)S(1)}, u32[]{:S(2)}, u32[]{:S(2)}) async-start(bf16[32,40,128]{2,1,0:T(8,128)(2,1)} %bitcast.9), calls=%async_computation.2 | async-start | bytes 655360 | tf_op jit(solution)/shard_map/all_to_all | solution.py:486
  63.2 1.4 %collective-permute-start.1 = (bf16[32,512]{1,0:T(8,128)(2,1)S(1)}, bf16[32,512]{1,0:T(8,128)(2,1)S(1)}, u32[]{:S(2)}, u32[]{:S(2)}) collective-permute-start(bf16[32,512]{1,0:T(8,128)(2,1)S(1)} %get-tuple-element.78), channel_id=1, source_target_pairs={{0,1},{1,2},{2,3},{3,0},{4,5},{5,6},{6,7},{7,4},{8,9},{9,10},{10,1... | collective-permute-start | bytes 98312 | tf_op jit(solution)/shard_map/ppermute | solution.py:593
  64.5 2.6 %collective-permute-start.2 = (bf16[32,512]{1,0:T(8,128)(2,1)S(1)}, bf16[32,512]{1,0:T(8,128)(2,1)S(1)}, u32[]{:S(2)}, u32[]{:S(2)}) collective-permute-start(bf16[32,512]{1,0:T(8,128)(2,1)S(1)} %get-tuple-element.77), channel_id=1, source_target_pairs={{0,2},{1,3},{2,0},{3,1},{4,6},{5,7},{6,4},{7,5},{8,10},{9,11},{10,... | collective-permute-start | bytes 98312 | tf_op jit(solution)/shard_map/ppermute | solution.py:593
  67.1 1.1 %collective-permute-start.3 = (bf16[32,512]{1,0:T(8,128)(2,1)S(1)}, bf16[32,512]{1,0:T(8,128)(2,1)S(1)}, u32[]{:S(2)}, u32[]{:S(2)}) collective-permute-start(bf16[32,512]{1,0:T(8,128)(2,1)S(1)} %get-tuple-element.76), channel_id=1, source_target_pairs={{0,3},{1,0},{2,1},{3,2},{4,7},{5,4},{6,5},{7,6},{8,11},{9,8},{10,9... | collective-permute-start | bytes 98312 | tf_op jit(solution)/shard_map/ppermute | solution.py:593
  68.2 0.0 copy-done
  68.2 1.1 %reshape.57 = bf16[1,2048,2,128]{3,2,1,0:T(2,128)(2,1)} reshape(bf16[2048,256]{1,0:T(8,128)(2,1)S(1)} %copy-done) | data formatting | bytes 2097152 | tf_op jit(solution)/shard_map/reshape | solution.py:595
  69.3 0.0 collective-permute-done.1.refs_1_
  69.3 0.0 collective-permute-done.2.refs_2_
  69.3 0.9 collective-permute-done.3.refs_3_
  70.2 5.6 %all-to-all-done.2 = bf16[32,40,128]{2,1,0:T(8,128)(2,1)S(1)} async-done(((bf16[32,40,128]{2,1,0:T(8,128)(2,1)}), bf16[32,40,128]{2,1,0:T(8,128)(2,1)S(1)}, u32[]{:S(2)}, u32[]{:S(2)}) %all-to-all-start.2) | async-done | bytes 327712 | tf_op jit(solution)/shard_map/all_to_all | solution.py:486
  75.8 0.1 shard_map.117
  75.9 15.8 %all_to_all.20 = bf16[32,40,128]{2,1,0:T(8,128)(2,1)S(1)} all-to-all(bf16[32,40,128]{2,1,0:T(8,128)(2,1)S(1)} %bitcast.16), channel_id=1, replica_groups={{0,8,16,24,32,40,48,56,64,72,80,88,96,104,112,120,128,136,144,152,160,1..., dimensions={0} | all-to-all | bytes 655360 | tf_op jit(solution)/shard_map/all_to_all | solution.py:486
  91.7 3.7 %collective-permute-start.4 = (bf16[1280,128]{1,0:T(8,128)(2,1)S(1)}, bf16[1280,128]{1,0:T(8,128)(2,1)S(1)}, u32[]{:S(2)}, u32[]{:S(2)}) collective-permute-start(bf16[1280,128]{1,0:T(8,128)(2,1)S(1)} %bitcast.14), channel_id=1, source_target_pairs={{0,4},{4,0},{8,12},{12,8},{16,20},{20,16},{24,28},{28,24},{32,36},... | collective-permute-start | bytes 983048 | tf_op jit(solution)/shard_map/ppermute | solution.py:476
  95.4 1.1 %shard_map.118 = (bf16[32,512]{1,0:T(8,128)(2,1)}, f32[4,512,128]{2,1,0:T(8,128)}, f32[128,512]{1,0:T(8,128)}) custom-call(s32[1]{0:T(128)} %bitcast.refs_0_.which_ref, bf16[1280,128]{1,0:T(8,128)(2,1)S(1)} %bitcast.15, bf16[32,512]{1,0:T(8,128)(2,1)S(1)} %get-tuple-element.66.refs_0_, bf16[32,512]{1,0:T(8,128)(2,1)S(1)} %collective-permute-done.1.refs_1_, ...), custom_call_target="tpu_custom_call" | custom-call | bytes 1048576 | tf_op jit(solution)/shard_map/pallas_call | solution.py:365
  96.5 0.2 collective-permute-done.4.source_ref
  96.7 0.9 shard_map.119
  (1 shorter events, 0.0 us)
Async XLA Ops:
  3.3 26.7 %all-to-all-start = ((bf16[64,9,2,128]{3,2,1,0:T(2,128)(2,1)}), bf16[64,9,2,128]{3,2,1,0:T(2,128)(2,1)S(1)}, u32[]{:S(2)}, u32[]{:S(2)}) async-start(bf16[64,9,2,128]{3,2,1,0:T(2,128)(2,1)} %bitcast.4), calls=%async_computation | async-start | bytes 589824 | tf_op jit(solution)/shard_map/all_to_all | solution.py:482
  37.9 18.0 %all-to-all-start.1 = ((bf16[64,16,128]{2,1,0:T(8,128)(2,1)}), bf16[64,16,128]{2,1,0:T(8,128)(2,1)S(1)}, u32[]{:S(2)}, u32[]{:S(2)}) async-start(bf16[64,16,128]{2,1,0:T(8,128)(2,1)} %bitcast.7), calls=%async_computation.1 | async-start | bytes 524288 | tf_op jit(solution)/shard_map/all_to_all | solution.py:482
  48.7 19.5 %copy-start = (bf16[2048,256]{1,0:T(8,128)(2,1)S(1)}, bf16[2048,256]{1,0:T(8,128)(2,1)}, u32[]{:S(2)}) copy-start(bf16[2048,256]{1,0:T(8,128)(2,1)} %get-tuple-element.63) | copy-start | bytes 3145732
  56.6 1.7 %collective-permute-start = (bf16[1280,128]{1,0:T(8,128)(2,1)S(1)}, bf16[1280,128]{1,0:T(8,128)(2,1)S(1)}, u32[]{:S(2)}, u32[]{:S(2)}) collective-permute-start(bf16[1280,128]{1,0:T(8,128)(2,1)S(1)} %get-tuple-element.62), channel_id=1, source_target_pairs={{0,4},{4,0},{8,12},{12,8},{16,20},{20,16},{24,28},{28,24},{32,36},... | collective-permute-start | bytes 983048 | tf_op jit(solution)/shard_map/ppermute | solution.py:476
  59.2 16.7 %all-to-all-start.2 = ((bf16[32,40,128]{2,1,0:T(8,128)(2,1)}), bf16[32,40,128]{2,1,0:T(8,128)(2,1)S(1)}, u32[]{:S(2)}, u32[]{:S(2)}) async-start(bf16[32,40,128]{2,1,0:T(8,128)(2,1)} %bitcast.9), calls=%async_computation.2 | async-start | bytes 655360 | tf_op jit(solution)/shard_map/all_to_all | solution.py:486
  63.2 6.2 %collective-permute-start.1 = (bf16[32,512]{1,0:T(8,128)(2,1)S(1)}, bf16[32,512]{1,0:T(8,128)(2,1)S(1)}, u32[]{:S(2)}, u32[]{:S(2)}) collective-permute-start(bf16[32,512]{1,0:T(8,128)(2,1)S(1)} %get-tuple-element.78), channel_id=1, source_target_pairs={{0,1},{1,2},{2,3},{3,0},{4,5},{5,6},{6,7},{7,4},{8,9},{9,10},{10,1... | collective-permute-start | bytes 98312 | tf_op jit(solution)/shard_map/ppermute | solution.py:593
  64.5 4.8 %collective-permute-start.2 = (bf16[32,512]{1,0:T(8,128)(2,1)S(1)}, bf16[32,512]{1,0:T(8,128)(2,1)S(1)}, u32[]{:S(2)}, u32[]{:S(2)}) collective-permute-start(bf16[32,512]{1,0:T(8,128)(2,1)S(1)} %get-tuple-element.77), channel_id=1, source_target_pairs={{0,2},{1,3},{2,0},{3,1},{4,6},{5,7},{6,4},{7,5},{8,10},{9,11},{10,... | collective-permute-start | bytes 98312 | tf_op jit(solution)/shard_map/ppermute | solution.py:593
  67.1 3.1 %collective-permute-start.3 = (bf16[32,512]{1,0:T(8,128)(2,1)S(1)}, bf16[32,512]{1,0:T(8,128)(2,1)S(1)}, u32[]{:S(2)}, u32[]{:S(2)}) collective-permute-start(bf16[32,512]{1,0:T(8,128)(2,1)S(1)} %get-tuple-element.76), channel_id=1, source_target_pairs={{0,3},{1,0},{2,1},{3,2},{4,7},{5,4},{6,5},{7,6},{8,11},{9,8},{10,9... | collective-permute-start | bytes 98312 | tf_op jit(solution)/shard_map/ppermute | solution.py:593
  91.7 4.9 %collective-permute-start.4 = (bf16[1280,128]{1,0:T(8,128)(2,1)S(1)}, bf16[1280,128]{1,0:T(8,128)(2,1)S(1)}, u32[]{:S(2)}, u32[]{:S(2)}) collective-permute-start(bf16[1280,128]{1,0:T(8,128)(2,1)S(1)} %bitcast.14), channel_id=1, source_target_pairs={{0,4},{4,0},{8,12},{12,8},{16,20},{20,16},{24,28},{28,24},{32,36},... | collective-permute-start | bytes 983048 | tf_op jit(solution)/shard_map/ppermute | solution.py:476

commit v8 on v7

--- a/solution.py
+++ b/solution.py
@@ -13,6 +13,7 @@
 BLOCK = 256
 HISTORY_PARTS = 2
 LATE = 5
+MOVED = 1024
 ROWS = 2 * CAP + 2
 F32 = jnp.float32
 BF16 = jnp.bfloat16
@@ -139,7 +140,7 @@
 
 def attend_kernel(
     recv_in, k_in, vt_in, v_in, kt_in,
-    back_out, weights_out, d_keys_out, d_att_out,
+    back_out, weights_out, d_keys_out, d_att_out, d_scores_out, q_out,
     s_scr, in_scr, out_scr,
 ):
     recv_ref, k_ref, vt_ref = recv_in.get(), k_in.get(), vt_in.get()
@@ -150,6 +151,8 @@
     in_scr[...] = recv_ref[...].astype(F32)
     q = jnp.concatenate([in_scr[every(j, owners, ROWS), :] for j in range(CAP)], axis=0).astype(BF16)
     dn = jnp.concatenate([in_scr[every(CAP + j, owners, ROWS), :] for j in range(CAP)], axis=0).astype(BF16)
+    q_out.buffer[...] = q
+    q_out.send()
     high, low = (in_scr[every(2 * CAP + i, owners, ROWS), :] for i in range(2))
     length = jnp.transpose(high * 256.0 + low)
     length = jnp.concatenate([length[j : j + 1] for j in range(CAP)], axis=1)
@@ -188,9 +191,15 @@
         for h in range(heads):
             ds = nn(v_ref[at, :], dt_of[h]) * s_scr[at, cols_of[h]].astype(F32)
             s_scr[at, cols_of[h]] = ds.astype(BF16)
+            if start < MOVED:
+                d_scores_out.buffer[at, cols_of[h]] = ds.astype(BF16)
+        if start < MOVED:
+            d_scores_out.send_part((at,))
+            continue
         d_keys = nn(s_scr[at, :], q_of) * (0.5 * DH ** (-0.5))
-        d_keys_out.buffer[at, :] = d_keys.astype(BF16)
-        d_keys_out.send_part((at,))
+        left = pl.ds(start - MOVED, BLOCK)
+        d_keys_out.buffer[left, :] = d_keys.astype(BF16)
+        d_keys_out.send_part((left,))
     d_query = [nn(kt_ref[mine_of[h], :], s_scr[:, cols_of[h]]) for h in range(heads)]
     d_query = (jnp.concatenate(d_query, axis=0) * (0.5 * DH ** (-0.5))).astype(BF16)
     d_query = jnp.transpose(d_query).astype(F32)
@@ -202,7 +211,7 @@
 
 
 def history_kernel(
-    core_ref, d_att_in, d_keys_in, slope_in, weights_in, ev_in, *rest
+    core_ref, d_att_in, q_in, d_scores_in, d_keys_in, slope_in, weights_in, ev_in, *rest
 ):
     late, rest = rest[:LATE], rest[LATE:]
     gkv_out, mine_out, other_out, rest = rest[0], rest[1], rest[2], rest[3:]
@@ -230,9 +239,17 @@
     head_col = iota((slots, width), 1) // DH
     zero = jnp.zeros((), BF16)
     d_of = jnp.concatenate([jnp.where(head_col == h, d_att, zero) for h in range(heads)], axis=0)
+    q = q_in.get()[...]
+    q_of = jnp.concatenate([jnp.where(head_col == h, q, zero) for h in range(heads)], axis=0)
+    moved = (nn(d_scores_in.get()[...], q_of) * (0.5 * DH ** (-0.5))).astype(BF16)
     d_keys_ref, slope_ref, gkv_ref = d_keys_in.get(), slope_in.get(), gkv_out.buffer
-    for at, copy in zip(parts, copies):
-        d_keys = d_keys_ref[at, :]
+    for b, (at, copy) in enumerate(zip(parts, copies)):
+        if b == 0:
+            d_keys = moved
+            if step > MOVED:
+                d_keys = jnp.concatenate([moved, d_keys_ref[: step - MOVED, :]], axis=0)
+        else:
+            d_keys = d_keys_ref[b * step - MOVED : (b + 1) * step - MOVED, :]
         gkv_ref[at, :width] = d_keys
         term_scr[at, :width] = (d_keys.astype(F32) * slope_ref[at, :].astype(F32)).astype(BF16)
         copy.wait()
@@ -520,12 +537,14 @@
         moved=5 << 20,
     )
     heads = width // DH
-    back, weights, d_keys, d_att = call(
+    back, weights, d_keys, d_att, d_scores, queries = call(
         attend_kernel,
         [
             ((2 * slots, width), BF16),
             ((events, heads * slots), BF16),
-            ((events, width), BF16),
+            ((events - MOVED, width), BF16),
+            ((slots, width), BF16),
+            ((MOVED, heads * slots), BF16),
             ((slots, width), BF16),
         ],
         (recv, keys, values_t, values, keys_t),
@@ -547,7 +566,7 @@
         + [((half, width), BF16)] * 2
         + [(place.shape, BF16), (aux.shape, F32), (imp_x.shape, BF16)]
         + [((2,) + w_in.shape[1:], BF16), (grad_y.shape, BF16)],
-        (d_att, d_keys, key_slope, weights, hist, place, aux, imp_x, w_in, grad_y),
+        (d_att, queries, d_scores, d_keys, key_slope, weights, hist, place, aux, imp_x, w_in, grad_y),
         (core,),
         scratch=[
             pltpu.VMEM((2, half, width), BF16),
@@ -558,7 +577,7 @@
             pltpu.SemaphoreType.DMA(()),
             pltpu.SemaphoreType.DMA((LATE,)),
         ],
-        raw_in=(3, 4, 5, 6, 7, 8, 9),
+        raw_in=(5, 6, 7, 8, 9, 10, 11),
         near_out=(1, 2, 3, 4, 5, 6, 7),
         flops=4 * events * depth * width + 2 * events * slots * width,
         moved=10 << 20,

time: 98.1 us -> 97.5 us (level)
  waiting for transfers between devices: 24.2 us -> 22.8 us
    all_to_all x2, waiting for transfers between devices: 16.2 us -> 14.7 us  [exchange(): return lax.all_to_all(a, 'dp', 0, 0, tiled=True).reshape(shape)]
  transfers between devices with their start and end apart: 8 -> 8, of which waited for: 6 -> 6; matrix products, arithmetic and copies ran while one was open for 1% -> 1% of each run, Pallas kernels for 12% -> 14%
where the time goes in v8:
time: 97.5 us; the launch traced here: 97.2 us
  starting transfers between devices  30.8 us (32%)
  Pallas kernels  25.6 us (26%)
  waiting for transfers between devices  22.8 us (23%)
  blocking collectives  15.8 us (16%)
  local copies, waits for them, and re-layouts  1.12 us (1%)
    pallas_call x7, Pallas kernels, call(): pl.pallas_call(body, out_shape=[jax.ShapeDtypeStruct(s, d) if i in near_o...  23.7 us
    all_to_all x2, starting transfers between devices, exchange(): return lax.all_to_all(a, 'dp', 0, 0, tiled=True).reshape(shape)  17.9 us
    all_to_all x1, blocking collectives, exchange_core(): a = lax.all_to_all(a, 'dp', 0, 0, axis_index_groups=same_core, tiled=True)  15.8 us
    all_to_all x2, waiting for transfers between devices, exchange(): return lax.all_to_all(a, 'dp', 0, 0, tiled=True).reshape(shape)  14.7 us
    all_to_all x1, waiting for transfers between devices, exchange_core(): a = lax.all_to_all(a, 'dp', 0, 0, axis_index_groups=same_core, tiled=True)  5.63 us
    ppermute x3, starting transfers between devices, on_device(): lax.ppermute(part, 'mp', [(i, (i + step) % planes) for i in range(planes)])  5.06 us
    ppermute x2, starting transfers between devices, swap(): return lax.ppermute(a, 'dp', pairs)  4.02 us
    all_to_all x1, starting transfers between devices, exchange_core(): a = lax.all_to_all(a, 'dp', 0, 0, axis_index_groups=same_core, tiled=True)  3.91 us
  transfers between devices with their start and end apart: 8, of which 6 were waited for; matrix products, arithmetic and copies ran while one was open for 1% of the time, Pallas kernels for 14%

profile of v8, /device:TPU:1, one launch (start us, length us, event | category | flops | bytes accessed | tf_op | source)
XLA Modules:
  0.0 97.2 jit_solution(17271716776867246583)
XLA Ops:
  0.6 2.7 %shard_map.111 = bf16[1152,128]{1,0:T(8,128)(2,1)} custom-call(s32[1,128]{1,0:T(1,128)} %bitcast.21, s32[1,128]{1,0:T(1,128)} %bitcast.25, s32[1,64]{1,0:T(1,128)} %bitcast.23, bf16[128,512]{1,0:T(8,128)(2,1)} %refs_10_.1, bf16[4,512,128]{2,1,0:T(8,128)(2,1)} %refs_11_.1, bf16[128,512]{1,0:T(8,128)(2,1)} %refs_5_.3, bf16[128,512]{1,0:T(8,128)(2,1)} %refs_12_.1), custom_call_target="tpu_custom_call" | custom-call | flops 50331648 | bytes 1048576 | tf_op jit(solution)/shard_map/pallas_call | solution.py:462
  3.3 13.0 %all-to-all-start = ((bf16[64,9,2,128]{3,2,1,0:T(2,128)(2,1)}), bf16[64,9,2,128]{3,2,1,0:T(2,128)(2,1)S(1)}, u32[]{:S(2)}, u32[]{:S(2)}) async-start(bf16[64,9,2,128]{3,2,1,0:T(2,128)(2,1)} %bitcast.4), calls=%async_computation | async-start | bytes 589824 | tf_op jit(solution)/shard_map/all_to_all | solution.py:499
  16.3 4.7 %shard_map.112 = (bf16[2048,128]{1,0:T(8,128)(2,1)S(1)}, bf16[128,2048]{1,0:T(8,128)(2,1)S(1)}, bf16[2048,128]{1,0:T(8,128)(2,1)}, bf16[128,2048]{1,0:T(8,128)(2...) custom-call(bf16[4,512,128]{2,1,0:T(8,128)(2,1)} %refs_11_.1, ...), custom_call_target="tpu_custom_call" | custom-call | flops 536870912 | bytes 5242880 | tf_op jit(solution)/shard_map/pallas_call | solution.py:462
  21.1 9.0 %all-to-all-done = bf16[64,9,2,128]{3,2,1,0:T(2,128)(2,1)S(1)} async-done(((bf16[64,9,2,128]{3,2,1,0:T(2,128)(2,1)}), bf16[64,9,2,128]{3,2,1,0:T(2,128)(2,1)S(1)}, u32[]{:S(2)}, u32[]{:S(2)}) %all-to-all-start) | async-done | bytes 294944 | tf_op jit(solution)/shard_map/all_to_all | solution.py:499
  30.0 7.3 %shard_map.113 = (bf16[1024,128]{1,0:T(8,128)(2,1)}, bf16[2048,1024]{1,0:T(8,128)(2,1)}, bf16[1024,128]{1,0:T(8,128)(2,1)}, bf16[512,128]{1,0:T(8,128)(2,1)}, bf...) custom-call(bf16[1152,128]{1,0:T(8,128)(2,1)S(1)} %bitcast.18, bf16[2048,128]{1,0:T(8,128)(2,1)S(1)} %get-tuple-element.42.refs_1_, ...), custom_call_target="tpu_custom_call" | custom-call | flops 1342177280 | bytes 8388608 | tf_op jit(solution)/shard_map/pallas_call | solution.py:462
  37.4 4.9 %all-to-all-start.1 = ((bf16[64,16,128]{2,1,0:T(8,128)(2,1)}), bf16[64,16,128]{2,1,0:T(8,128)(2,1)S(1)}, u32[]{:S(2)}, u32[]{:S(2)}) async-start(bf16[64,16,128]{2,1,0:T(8,128)(2,1)} %bitcast.7), calls=%async_computation.1 | async-start | bytes 524288 | tf_op jit(solution)/shard_map/all_to_all | solution.py:499
  42.2 7.4 %shard_map.114 = (bf16[2048,256]{1,0:T(8,128)(2,1)}, bf16[512,128]{1,0:T(8,128)(2,1)S(1)}, bf16[512,128]{1,0:T(8,128)(2,1)S(1)}, bf16[512,128]{1,0:T(8,128)(2,1)...) custom-call(s32[1]{0:T(128)} %bitcast.refs_0_.which_ref, ...), custom_call_target="tpu_custom_call" | custom-call | flops 805306368 | bytes 10485760 | tf_op jit(solution)/shard_map/pallas_call | solution.py:462
  49.6 0.0 copy-start
  49.6 5.8 %all-to-all-done.1 = bf16[64,16,128]{2,1,0:T(8,128)(2,1)S(1)} async-done(((bf16[64,16,128]{2,1,0:T(8,128)(2,1)}), bf16[64,16,128]{2,1,0:T(8,128)(2,1)S(1)}, u32[]{:S(2)}, u32[]{:S(2)}) %all-to-all-start.1) | async-done | bytes 262176 | tf_op jit(solution)/shard_map/all_to_all | solution.py:499
  55.4 0.7 shard_map.115
  56.1 0.3 collective-permute-start
  56.4 1.4 %collective-permute-done.refs_1_ = bf16[1280,128]{1,0:T(8,128)(2,1)S(1)} collective-permute-done((bf16[1280,128]{1,0:T(8,128)(2,1)S(1)}, bf16[1280,128]{1,0:T(8,128)(2,1)S(1)}, u32[]{:S(2)}, u32[]{:S(2)}) %collective-permute-start) | collective-permute-done | bytes 327712 | tf_op jit(solution)/shard_map/ppermute | solution.py:493
  57.8 0.8 shard_map.116
  58.6 3.9 %all-to-all-start.2 = ((bf16[32,40,128]{2,1,0:T(8,128)(2,1)}), bf16[32,40,128]{2,1,0:T(8,128)(2,1)S(1)}, u32[]{:S(2)}, u32[]{:S(2)}) async-start(bf16[32,40,128]{2,1,0:T(8,128)(2,1)} %bitcast.9), calls=%async_computation.2 | async-start | bytes 655360 | tf_op jit(solution)/shard_map/all_to_all | solution.py:503
  62.6 1.4 %collective-permute-start.1 = (bf16[32,512]{1,0:T(8,128)(2,1)S(1)}, bf16[32,512]{1,0:T(8,128)(2,1)S(1)}, u32[]{:S(2)}, u32[]{:S(2)}) collective-permute-start(bf16[32,512]{1,0:T(8,128)(2,1)S(1)} %get-tuple-element.82), channel_id=1, source_target_pairs={{0,1},{1,2},{2,3},{3,0},{4,5},{5,6},{6,7},{7,4},{8,9},{9,10},{10,1... | collective-permute-start | bytes 98312 | tf_op jit(solution)/shard_map/ppermute | solution.py:612
  64.0 2.6 %collective-permute-start.2 = (bf16[32,512]{1,0:T(8,128)(2,1)S(1)}, bf16[32,512]{1,0:T(8,128)(2,1)S(1)}, u32[]{:S(2)}, u32[]{:S(2)}) collective-permute-start(bf16[32,512]{1,0:T(8,128)(2,1)S(1)} %get-tuple-element.81), channel_id=1, source_target_pairs={{0,2},{1,3},{2,0},{3,1},{4,6},{5,7},{6,4},{7,5},{8,10},{9,11},{10,... | collective-permute-start | bytes 98312 | tf_op jit(solution)/shard_map/ppermute | solution.py:612
  66.6 1.1 %collective-permute-start.3 = (bf16[32,512]{1,0:T(8,128)(2,1)S(1)}, bf16[32,512]{1,0:T(8,128)(2,1)S(1)}, u32[]{:S(2)}, u32[]{:S(2)}) collective-permute-start(bf16[32,512]{1,0:T(8,128)(2,1)S(1)} %get-tuple-element.80), channel_id=1, source_target_pairs={{0,3},{1,0},{2,1},{3,2},{4,7},{5,4},{6,5},{7,6},{8,11},{9,8},{10,9... | collective-permute-start | bytes 98312 | tf_op jit(solution)/shard_map/ppermute | solution.py:612
  67.7 0.0 copy-done
  67.7 1.1 %reshape.57 = bf16[1,2048,2,128]{3,2,1,0:T(2,128)(2,1)} reshape(bf16[2048,256]{1,0:T(8,128)(2,1)S(1)} %copy-done) | data formatting | bytes 2097152 | tf_op jit(solution)/shard_map/reshape | solution.py:614
  68.8 0.0 collective-permute-done.1.refs_1_
  68.8 0.0 collective-permute-done.2.refs_2_
  68.8 0.9 collective-permute-done.3.refs_3_
  69.7 5.6 %all-to-all-done.2 = bf16[32,40,128]{2,1,0:T(8,128)(2,1)S(1)} async-done(((bf16[32,40,128]{2,1,0:T(8,128)(2,1)}), bf16[32,40,128]{2,1,0:T(8,128)(2,1)S(1)}, u32[]{:S(2)}, u32[]{:S(2)}) %all-to-all-start.2) | async-done | bytes 327712 | tf_op jit(solution)/shard_map/all_to_all | solution.py:503
  75.3 0.1 shard_map.117
  75.4 15.8 %all_to_all.20 = bf16[32,40,128]{2,1,0:T(8,128)(2,1)S(1)} all-to-all(bf16[32,40,128]{2,1,0:T(8,128)(2,1)S(1)} %bitcast.16), channel_id=1, replica_groups={{0,8,16,24,32,40,48,56,64,72,80,88,96,104,112,120,128,136,144,152,160,1..., dimensions={0} | all-to-all | bytes 655360 | tf_op jit(solution)/shard_map/all_to_all | solution.py:503
  91.2 3.7 %collective-permute-start.4 = (bf16[1280,128]{1,0:T(8,128)(2,1)S(1)}, bf16[1280,128]{1,0:T(8,128)(2,1)S(1)}, u32[]{:S(2)}, u32[]{:S(2)}) collective-permute-start(bf16[1280,128]{1,0:T(8,128)(2,1)S(1)} %bitcast.14), channel_id=1, source_target_pairs={{0,4},{4,0},{8,12},{12,8},{16,20},{20,16},{24,28},{28,24},{32,36},... | collective-permute-start | bytes 983048 | tf_op jit(solution)/shard_map/ppermute | solution.py:493
  94.9 1.1 %shard_map.118 = (bf16[32,512]{1,0:T(8,128)(2,1)}, f32[4,512,128]{2,1,0:T(8,128)}, f32[128,512]{1,0:T(8,128)}) custom-call(s32[1]{0:T(128)} %bitcast.refs_0_.which_ref, bf16[1280,128]{1,0:T(8,128)(2,1)S(1)} %bitcast.15, bf16[32,512]{1,0:T(8,128)(2,1)S(1)} %get-tuple-element.70.refs_0_, bf16[32,512]{1,0:T(8,128)(2,1)S(1)} %collective-permute-done.1.refs_1_, ...), custom_call_target="tpu_custom_call" | custom-call | bytes 1048576 | tf_op jit(solution)/shard_map/pallas_call | solution.py:382
  95.9 0.2 collective-permute-done.4.source_ref
  96.1 0.9 shard_map.119
  (1 shorter events, 0.0 us)
Async XLA Ops:
  3.3 26.7 %all-to-all-start = ((bf16[64,9,2,128]{3,2,1,0:T(2,128)(2,1)}), bf16[64,9,2,128]{3,2,1,0:T(2,128)(2,1)S(1)}, u32[]{:S(2)}, u32[]{:S(2)}) async-start(bf16[64,9,2,128]{3,2,1,0:T(2,128)(2,1)} %bitcast.4), calls=%async_computation | async-start | bytes 589824 | tf_op jit(solution)/shard_map/all_to_all | solution.py:499
  37.4 18.0 %all-to-all-start.1 = ((bf16[64,16,128]{2,1,0:T(8,128)(2,1)}), bf16[64,16,128]{2,1,0:T(8,128)(2,1)S(1)}, u32[]{:S(2)}, u32[]{:S(2)}) async-start(bf16[64,16,128]{2,1,0:T(8,128)(2,1)} %bitcast.7), calls=%async_computation.1 | async-start | bytes 524288 | tf_op jit(solution)/shard_map/all_to_all | solution.py:499
  49.6 18.1 %copy-start = (bf16[2048,256]{1,0:T(8,128)(2,1)S(1)}, bf16[2048,256]{1,0:T(8,128)(2,1)}, u32[]{:S(2)}) copy-start(bf16[2048,256]{1,0:T(8,128)(2,1)} %get-tuple-element.67) | copy-start | bytes 3145732
  56.1 1.7 %collective-permute-start = (bf16[1280,128]{1,0:T(8,128)(2,1)S(1)}, bf16[1280,128]{1,0:T(8,128)(2,1)S(1)}, u32[]{:S(2)}, u32[]{:S(2)}) collective-permute-start(bf16[1280,128]{1,0:T(8,128)(2,1)S(1)} %get-tuple-element.66), channel_id=1, source_target_pairs={{0,4},{4,0},{8,12},{12,8},{16,20},{20,16},{24,28},{28,24},{32,36},... | collective-permute-start | bytes 983048 | tf_op jit(solution)/shard_map/ppermute | solution.py:493
  58.6 16.7 %all-to-all-start.2 = ((bf16[32,40,128]{2,1,0:T(8,128)(2,1)}), bf16[32,40,128]{2,1,0:T(8,128)(2,1)S(1)}, u32[]{:S(2)}, u32[]{:S(2)}) async-start(bf16[32,40,128]{2,1,0:T(8,128)(2,1)} %bitcast.9), calls=%async_computation.2 | async-start | bytes 655360 | tf_op jit(solution)/shard_map/all_to_all | solution.py:503
  62.6 6.2 %collective-permute-start.1 = (bf16[32,512]{1,0:T(8,128)(2,1)S(1)}, bf16[32,512]{1,0:T(8,128)(2,1)S(1)}, u32[]{:S(2)}, u32[]{:S(2)}) collective-permute-start(bf16[32,512]{1,0:T(8,128)(2,1)S(1)} %get-tuple-element.82), channel_id=1, source_target_pairs={{0,1},{1,2},{2,3},{3,0},{4,5},{5,6},{6,7},{7,4},{8,9},{9,10},{10,1... | collective-permute-start | bytes 98312 | tf_op jit(solution)/shard_map/ppermute | solution.py:612
  64.0 4.8 %collective-permute-start.2 = (bf16[32,512]{1,0:T(8,128)(2,1)S(1)}, bf16[32,512]{1,0:T(8,128)(2,1)S(1)}, u32[]{:S(2)}, u32[]{:S(2)}) collective-permute-start(bf16[32,512]{1,0:T(8,128)(2,1)S(1)} %get-tuple-element.81), channel_id=1, source_target_pairs={{0,2},{1,3},{2,0},{3,1},{4,6},{5,7},{6,4},{7,5},{8,10},{9,11},{10,... | collective-permute-start | bytes 98312 | tf_op jit(solution)/shard_map/ppermute | solution.py:612
  66.6 3.1 %collective-permute-start.3 = (bf16[32,512]{1,0:T(8,128)(2,1)S(1)}, bf16[32,512]{1,0:T(8,128)(2,1)S(1)}, u32[]{:S(2)}, u32[]{:S(2)}) collective-permute-start(bf16[32,512]{1,0:T(8,128)(2,1)S(1)} %get-tuple-element.80), channel_id=1, source_target_pairs={{0,3},{1,0},{2,1},{3,2},{4,7},{5,4},{6,5},{7,6},{8,11},{9,8},{10,9... | collective-permute-start | bytes 98312 | tf_op jit(solution)/shard_map/ppermute | solution.py:612
  91.2 4.9 %collective-permute-start.4 = (bf16[1280,128]{1,0:T(8,128)(2,1)S(1)}, bf16[1280,128]{1,0:T(8,128)(2,1)S(1)}, u32[]{:S(2)}, u32[]{:S(2)}) collective-permute-start(bf16[1280,128]{1,0:T(8,128)(2,1)S(1)} %bitcast.14), channel_id=1, source_target_pairs={{0,4},{4,0},{8,12},{12,8},{16,20},{20,16},{24,28},{28,24},{32,36},... | collective-permute-start | bytes 983048 | tf_op jit(solution)/shard_map/ppermute | solution.py:493
